TPU v7x, 32 devices: a whole 2x2x4 slice. The times are simulated.
32 devices in a mesh: dp: 2 (over y), row: 4 (over x, core), col: 4 (over z).
Axes of the slice: x: 2, y: 2, z: 4, core: 2. Of those that a mesh axis runs over, the one named last changes fastest.
Arguments:
- hidden_in: bfloat16 [4096, 1024], P(('dp', 'row'), 'col'), may hold values from -6 to 6
- segments: int32 [4096], P('dp'), may hold values from 0 to 15, never falling along the last dimension, each value on 1 to 800 neighbouring positions
- cotangent: bfloat16 [4096, 1024], P(('dp', 'row'), 'col'), may hold values from -6 to 6
- input_gain: float32 [2, 1024], P(None, 'col'), may hold values from 0.1 to 1.9
- query_weight: bfloat16 [2, 1024, 512], P(None, 'col', 'row'), may hold values from -0.1875 to 0.1875
- keyval_weight: bfloat16 [2, 1024, 256], P(None, 'col'), may hold values from -0.1875 to 0.1875
- mixer_gate_weight: bfloat16 [2, 1024, 1536], P(None, 'col', 'row'), may hold values from -0.1875 to 0.1875
- mixer_input_weight: bfloat16 [2, 1024, 1536], P(None, 'col', 'row'), may hold values from -0.1875 to 0.1875
- state_weight: bfloat16 [2, 1024, 256], P(None, 'col'), may hold values from -0.1875 to 0.1875
- step_weight: bfloat16 [2, 1024, 24], P(None, 'col'), may hold values from -0.1875 to 0.1875
- conv_values: float32 [2, 4, 1536], P(None, None, 'row'), may hold values from -3 to 3
- conv_shared: float32 [2, 4, 256], replicated, may hold values from -3 to 3
- step_bias: float32 [2, 24], P(None, 'row'), may hold values from -5 to -1
- decay_log: float32 [2, 24], P(None, 'row'), may hold values from -1.5 to 1.5
- skip_gain: float32 [2, 24], P(None, 'row'), may hold values from 0.5 to 2
- attention_out: bfloat16 [2, 512, 1024], P(None, 'row', 'col'), may hold values from -0.75 to 0.75
- mixer_out: bfloat16 [2, 1536, 1024], P(None, 'row', 'col'), may hold values from -0.15625 to 0.15625
- post_gain: float32 [2, 1024], P(None, 'col'), may hold values from 0.1 to 1.9
- gate_weight: bfloat16 [2, 1024, 2048], P(None, 'col', 'row'), may hold values from -0.1875 to 0.1875
- up_weight: bfloat16 [2, 1024, 2048], P(None, 'col', 'row'), may hold values from -0.1875 to 0.1875
- down_weight: bfloat16 [2, 2048, 1024], P(None, 'row', 'col'), may hold values from -0.125 to 0.125
Outputs:
- hidden_out: bfloat16 [4096, 1024], P(('dp', 'row'), 'col')
- hidden_grad: float32 [4096, 1024], P(('dp', 'row'), 'col')
- input_gain_grad: float32 [2, 1024], P(None, 'col')
- query_weight_grad: float32 [2, 1024, 512], P(None, 'col', 'row')
- keyval_weight_grad: float32 [2, 1024, 256], P(None, 'col')
- mixer_gate_weight_grad: float32 [2, 1024, 1536], P(None, 'col', 'row')
- mixer_input_weight_grad: float32 [2, 1024, 1536], P(None, 'col', 'row')
- state_weight_grad: float32 [2, 1024, 256], P(None, 'col')
- step_weight_grad: float32 [2, 1024, 24], P(None, 'col')
- conv_values_grad: float32 [2, 4, 1536], P(None, None, 'row')
- conv_shared_grad: float32 [2, 4, 256], replicated
- step_bias_grad: float32 [2, 24], P(None, 'row')
- decay_log_grad: float32 [2, 24], P(None, 'row')
- skip_gain_grad: float32 [2, 24], P(None, 'row')
- attention_out_grad: float32 [2, 512, 1024], P(None, 'row', 'col')
- mixer_out_grad: float32 [2, 1536, 1024], P(None, 'row', 'col')
- post_gain_grad: float32 [2, 1024], P(None, 'col')
- gate_weight_grad: float32 [2, 1024, 2048], P(None, 'col', 'row')
- up_weight_grad: float32 [2, 1024, 2048], P(None, 'col', 'row')
- down_weight_grad: float32 [2, 2048, 1024], P(None, 'row', 'col')
Inputs may be any that keep to these rules, and one draw needn't show every extreme that they name: `segments`: document numbers never fall along the tokens; each document holds 800 tokens or fewer, and one holds exactly 800.
All inputs are finite; a program needn't handle non-finite values.
Results may differ from a plain program's by a relative error of at most 0.02.
Values may be sent and summed in bfloat16 or wider, within the bound.
No kernel may reach another device: no remote copies, remote signals or barrier semaphores. Data moves between devices by JAX's collectives and lax.ppermute only.
A program may use at most 192 MiB of HBM per device.

v0:
```python
from functools import partial

import jax
import jax.numpy as jnp
from jax import lax
from jax.sharding import PartitionSpec as P

HEADS = 8
KV_HEADS = 2
HEAD = 64
M_HEAD = 64
LAYERS = 2
SPAN = 128


epsilon = 1e-05
highest = lax.Precision.HIGHEST


def narrowed(value):
    rounded_value = lax.optimization_barrier(value.astype(jnp.bfloat16)).astype(jnp.float32)
    return value + lax.stop_gradient(rounded_value - value)


def causal_conv(signal, kernel, segment_ids):
    length = signal.shape[0]
    summed = signal * kernel[0][None, :]
    for offset in range(1, kernel.shape[0]):
        earlier = jnp.concatenate(
            [jnp.zeros((offset, signal.shape[1]), signal.dtype), signal[: length - offset]], axis=0
        )
        prior_ids = jnp.concatenate(
            [jnp.full((offset,), -1, jnp.int32), segment_ids[: length - offset]]
        )
        same_doc = (prior_ids == segment_ids).astype(signal.dtype)
        summed = summed + earlier * kernel[offset][None, :] * same_doc[:, None]
    return summed


def attend(queries, key_heads, value_heads, segment_ids):
    length, query_count, head_size = queries.shape
    kv_count = key_heads.shape[1]
    block_rows = min(512, length)
    positions = jnp.arange(length, dtype=jnp.int32)
    scaling = head_size ** (-0.5)

    def query_block(block_index):
        first_row = block_index * block_rows
        chosen = queries
        chosen = chosen.reshape(block_rows, kv_count, query_count // kv_count, head_size)
        query_pos = first_row + jnp.arange(block_rows, dtype=jnp.int32)
        scores = jnp.einsum("qkge,ske->kgqs", chosen, key_heads, precision=highest) * scaling
        allowed = (query_pos[:, None] >= positions[None, :]) & (
            segment_ids[:, None] == segment_ids[None, :]
        )
        scores = jnp.where(allowed[None, None], scores, -1e30)
        highest_score = jnp.max(scores, axis=-1, keepdims=True)
        weights = jnp.exp(scores - highest_score)
        weights_low = narrowed(weights / jnp.sum(weights, axis=-1, keepdims=True))
        attended = jnp.einsum("kgqs,ske->qkge", weights_low, value_heads, precision=highest)
        return attended.reshape(block_rows, query_count * head_size)

    blocks = lax.map(jax.checkpoint(query_block), jnp.arange(length // block_rows, dtype=jnp.int32))
    return blocks.reshape(length, query_count * head_size)


def scan_spans(inner, bmatrix, cmatrix, time_steps, rates, segment_ids, width):
    length, head_count, head_size = inner.shape
    span_count = length // width
    state_size = bmatrix.shape[1]
    seg_blocks = segment_ids.reshape(span_count, width)
    previous = jnp.concatenate([jnp.full((1,), -1, jnp.int32), seg_blocks[:-1, -1]])
    positions = jnp.arange(width, dtype=jnp.int32)
    causal = positions[:, None] >= positions[None, :]

    def span_step(carry_state, pieces):
        block_inner, block_b, block_c, block_dt, block_seg, prior_segment = pieces
        cumulative = jnp.cumsum(-block_dt * rates[None, :], axis=0)
        inside = causal & (block_seg[:, None] == block_seg[None, :])
        spread = jnp.where(inside[:, :, None], cumulative[:, None, :] - cumulative[None, :, :], 0.0)
        decay_matrix = jnp.exp(spread) * inside[:, :, None].astype(cumulative.dtype)
        affinity = jnp.dot(block_c, block_b.T, precision=highest)
        scaled = block_inner * block_dt[:, :, None]
        result = jnp.einsum(
            "ijh,jhp->ihp", affinity[:, :, None] * decay_matrix, scaled, precision=highest
        )
        continuing = (block_seg == prior_segment).astype(cumulative.dtype)
        carried = jnp.einsum("in,hpn->ihp", block_c, carry_state, precision=highest)
        result = result + carried * (jnp.exp(cumulative) * continuing[:, None])[:, :, None]
        last_segment = block_seg[-1]
        tail_weight = (
            jnp.exp(cumulative[-1][None, :] - cumulative)
            * (block_seg == last_segment).astype(cumulative.dtype)[:, None]
        )
        retained = jnp.exp(cumulative[-1]) * (last_segment == prior_segment).astype(
            cumulative.dtype
        )
        update = jnp.einsum(
            "jhp,jn->hpn", scaled * tail_weight[:, :, None], block_b, precision=highest
        )
        return (carry_state * retained[:, None, None] + update, result)

    zero_state = jnp.zeros((head_count, head_size, state_size), inner.dtype)
    pieces = (
        inner.reshape(span_count, width, head_count, head_size),
        bmatrix.reshape(span_count, width, state_size),
        cmatrix.reshape(span_count, width, state_size),
        time_steps.reshape(span_count, width, head_count),
        seg_blocks,
        previous,
    )
    ignored, outputs = lax.scan(jax.checkpoint(span_step), zero_state, pieces)
    return outputs.reshape(length, head_count, head_size)


def mixer_local(
    projected, conv_values, conv_shared, step_bias, decay_log, skip_gain, segment_ids, layout
):
    query_cols, gate_cols, input_cols, kv_cols, state_cols, kv_index, step_first, heads_row = layout
    length = projected.shape[0]
    first_kv = query_cols + gate_cols + input_cols
    queries = projected[:, :query_cols]
    mgate = projected[:, query_cols : query_cols + gate_cols]
    minput = projected[:, query_cols + gate_cols : first_kv]
    keyval = projected[:, first_kv : first_kv + kv_cols]
    states = projected[:, first_kv + kv_cols : first_kv + kv_cols + state_cols]
    time_all = projected[:, first_kv + kv_cols + state_cols :]
    key_head = lax.dynamic_slice_in_dim(keyval, kv_index * HEAD, HEAD, 1)
    value_head = lax.dynamic_slice_in_dim(keyval, KV_HEADS * HEAD + kv_index * HEAD, HEAD, 1)
    time_raw = lax.dynamic_slice_in_dim(time_all, step_first, heads_row, 1)
    query_heads = narrowed(queries).reshape(length, -1, HEAD)
    key_heads = narrowed(key_head).reshape(length, 1, HEAD)
    value_heads = narrowed(value_head).reshape(length, 1, HEAD)
    attended = narrowed(attend(query_heads, key_heads, value_heads, segment_ids))
    inner = jax.nn.silu(causal_conv(minput, conv_values, segment_ids))
    shared = jax.nn.silu(causal_conv(states, conv_shared, segment_ids))
    half_width = shared.shape[1] // 2
    time_steps = jax.nn.softplus(time_raw + step_bias[None, :])
    inner_heads = inner.reshape(length, heads_row, M_HEAD)
    scanned = scan_spans(
        inner_heads,
        shared[:, :half_width],
        shared[:, half_width:],
        time_steps,
        jnp.exp(decay_log),
        segment_ids,
        SPAN,
    )
    scanned = scanned + skip_gain[None, :, None] * inner_heads
    mamba = narrowed(scanned.reshape(length, heads_row * M_HEAD) * jax.nn.silu(mgate))
    return jnp.concatenate([attended, mamba], axis=1)


def swiglu(projected):
    half_width = projected.shape[1] // 2
    return narrowed(jax.nn.silu(projected[:, :half_width]) * projected[:, half_width:])


def norm_forward(hidden, gain, width):
    summed = lax.psum(jnp.sum(hidden * hidden, axis=1), "col")
    inverse = lax.rsqrt(summed / width + epsilon)
    return (hidden * inverse[:, None] * gain[None, :], inverse)


def norm_backward(hidden, inverse, gain, grad_normed, width):
    weighted = grad_normed * gain[None, :]
    summed = lax.psum(jnp.sum(weighted * hidden, axis=1), "col")
    grad_hidden = (
        inverse[:, None] * weighted
        - hidden * (inverse * inverse * inverse * summed / width)[:, None]
    )
    grad_gain = jnp.sum(grad_normed * hidden * inverse[:, None], axis=0)
    return (grad_hidden, grad_gain)


def project_in(normed_low, weight):
    gathered = lax.all_gather(normed_low, "row", axis=0, tiled=True)

    def product_term(first_row, row_count):
        return jnp.dot(gathered, weight, preferred_element_type=jnp.float32)

    return (
        gathered,
        lax.psum_scatter(
            product_term(jnp.int32(0), normed_low.shape[0] * lax.axis_size("col")),
            "col",
            scatter_dimension=0,
            tiled=True,
        ),
    )


def project_out(middle_low, weight):
    gathered = lax.all_gather(middle_low, "col", axis=0, tiled=True)

    def product_term(first_row, row_count):
        return jnp.dot(gathered, weight, preferred_element_type=jnp.float32)

    return (
        gathered,
        lax.psum_scatter(
            product_term(jnp.int32(0), middle_low.shape[0] * lax.axis_size("row")),
            "row",
            scatter_dimension=0,
            tiled=True,
        ),
    )


def branch_back(grad_low, weight):
    gathered = lax.all_gather(grad_low, "row", axis=0, tiled=True)

    def product_term(first_row, row_count):
        return lax.dot_general(
            gathered, weight, (((1,), (1,)), ((), ())), preferred_element_type=jnp.float32
        )

    return (
        gathered,
        lax.psum_scatter(
            product_term(jnp.int32(0), grad_low.shape[0] * lax.axis_size("col")),
            "col",
            scatter_dimension=0,
            tiled=True,
        ),
    )


def project_back(grad_low, weight, split_cols, row_index):
    gathered = lax.all_gather(grad_low, "col", axis=0, tiled=True)
    split_weight = weight[:, :split_cols]

    def product_term(first_row, row_count):
        rows_piece = gathered[:, :split_cols]
        return lax.dot_general(
            rows_piece, split_weight, (((1,), (1,)), ((), ())), preferred_element_type=jnp.float32
        )

    result = lax.psum_scatter(
        product_term(jnp.int32(0), grad_low.shape[0] * lax.axis_size("row")),
        "row",
        scatter_dimension=0,
        tiled=True,
    )
    if split_cols < weight.shape[1]:
        row_total = grad_low.shape[0]
        own_rows = lax.dynamic_slice_in_dim(gathered, row_index * row_total, row_total, 0)[
            :, split_cols:
        ]
        result = result + lax.dot_general(
            own_rows,
            weight[:, split_cols:],
            (((1,), (1,)), ((), ())),
            preferred_element_type=jnp.float32,
        )
    return (gathered, result)


def contract_rows(left, right):
    return lax.dot_general(
        left, right, (((0,), (0,)), ((), ())), preferred_element_type=jnp.float32
    )


def layer_run(hidden, params, segment_ids, layout, width):
    (
        input_gain,
        query_weight,
        keyval_weight,
        mixer_gate_weight,
        mixer_input_weight,
        state_weight,
        step_weight,
        conv_values,
        conv_shared,
        step_bias,
        decay_log,
        skip_gain,
        attention_out,
        mixer_out,
        post_gain,
        gate_weight,
        up_weight,
        down_weight,
    ) = params
    normed, inverse = norm_forward(hidden, input_gain, width)
    mixer_weight = jnp.concatenate(
        [
            query_weight,
            mixer_gate_weight,
            mixer_input_weight,
            keyval_weight,
            state_weight,
            step_weight,
        ],
        axis=1,
    )
    gathered, projected = project_in(normed.astype(jnp.bfloat16), mixer_weight)
    mixed, mixer_pull = jax.vjp(
        partial(mixer_local, segment_ids=segment_ids, layout=layout),
        projected,
        conv_values,
        conv_shared,
        step_bias,
        decay_log,
        skip_gain,
    )
    out_weight = jnp.concatenate([attention_out, mixer_out], axis=0)
    mixed_gathered, branch = project_out(mixed.astype(jnp.bfloat16), out_weight)
    middle = hidden + branch
    post_normed, post_inverse = norm_forward(middle, post_gain, width)
    ffn_weight = jnp.concatenate([gate_weight, up_weight], axis=1)
    post_gathered, post_projected = project_in(post_normed.astype(jnp.bfloat16), ffn_weight)
    activated, act_pull = jax.vjp(swiglu, post_projected)
    act_gathered, ffn_branch = project_out(activated.astype(jnp.bfloat16), down_weight)
    output = middle + ffn_branch
    saved = (
        hidden,
        inverse,
        gathered,
        mixer_pull,
        mixed_gathered,
        middle,
        post_inverse,
        post_gathered,
        act_pull,
        act_gathered,
        mixer_weight,
        out_weight,
        ffn_weight,
    )
    return (output, saved)


def layer_back(grad_out, saved, params, row_index, width, split_cols):
    (
        hidden,
        inverse,
        gathered,
        mixer_pull,
        mixed_gathered,
        middle,
        post_inverse,
        post_gathered,
        act_pull,
        act_gathered,
        mixer_weight,
        out_weight,
        ffn_weight,
    ) = saved
    input_gain = params[0]
    post_gain = params[14]
    down_weight = params[17]
    dy_gathered, grad_act = branch_back(grad_out.astype(jnp.bfloat16), down_weight)
    down_grad = contract_rows(act_gathered, dy_gathered)
    (grad_post,) = act_pull(grad_act)
    dpost_gathered, grad_post_normed = project_back(
        grad_post.astype(jnp.bfloat16), ffn_weight, ffn_weight.shape[1], row_index
    )
    ffn_grad = contract_rows(post_gathered, dpost_gathered)
    grad_from_post, post_gain_grad = norm_backward(
        middle, post_inverse, post_gain, grad_post_normed, width
    )
    grad_middle = grad_out + grad_from_post
    dmid_gathered, grad_mixed = branch_back(grad_middle.astype(jnp.bfloat16), out_weight)
    out_grad = contract_rows(mixed_gathered, dmid_gathered)
    (
        grad_proj,
        conv_values_grad,
        conv_shared_grad,
        step_bias_grad,
        decay_log_grad,
        skip_gain_grad,
    ) = mixer_pull(grad_mixed)
    shared_total, conv_shared_grad = lax.psum((grad_proj[:, split_cols:], conv_shared_grad), "row")
    grad_proj_low = jnp.concatenate(
        [grad_proj[:, :split_cols].astype(jnp.bfloat16), shared_total.astype(jnp.bfloat16)], axis=1
    )
    dproj_gathered, grad_normed = project_back(grad_proj_low, mixer_weight, split_cols, row_index)
    mixer_grad = contract_rows(gathered, dproj_gathered)
    grad_from_input, input_gain_grad = norm_backward(
        hidden, inverse, input_gain, grad_normed, width
    )
    grad_hidden = grad_middle + grad_from_input
    layer_grads = (
        mixer_grad,
        out_grad,
        ffn_grad,
        down_grad,
        conv_values_grad,
        conv_shared_grad,
        step_bias_grad,
        decay_log_grad,
        skip_gain_grad,
        input_gain_grad,
        post_gain_grad,
    )
    return (grad_hidden, layer_grads)


def reduce_grads(layer_grads):
    (
        mixer_grad,
        out_grad,
        ffn_grad,
        down_grad,
        conv_values_grad,
        conv_shared_grad,
        step_bias_grad,
        decay_log_grad,
        skip_gain_grad,
        input_gain_grad,
        post_gain_grad,
    ) = layer_grads
    mixer_grad, out_grad, ffn_grad, down_grad = lax.psum(
        (mixer_grad, out_grad, ffn_grad, down_grad), "dp"
    )
    conv_values_grad, conv_shared_grad, step_bias_grad, decay_log_grad, skip_gain_grad = lax.psum(
        (conv_values_grad, conv_shared_grad, step_bias_grad, decay_log_grad, skip_gain_grad),
        ("dp", "col"),
    )
    input_gain_grad, post_gain_grad = lax.psum((input_gain_grad, post_gain_grad), ("dp", "row"))
    return (
        mixer_grad,
        out_grad,
        ffn_grad,
        down_grad,
        conv_values_grad,
        conv_shared_grad,
        step_bias_grad,
        decay_log_grad,
        skip_gain_grad,
        input_gain_grad,
        post_gain_grad,
    )


def shards(
    hidden_in,
    segments,
    cotangent,
    input_gain,
    query_weight,
    keyval_weight,
    mixer_gate_weight,
    mixer_input_weight,
    state_weight,
    step_weight,
    conv_values,
    conv_shared,
    step_bias,
    decay_log,
    skip_gain,
    attention_out,
    mixer_out,
    post_gain,
    gate_weight,
    up_weight,
    down_weight,
):
    tokens = hidden_in.shape[0]
    width = hidden_in.shape[1] * lax.axis_size("col")
    row_index = lax.axis_index("row")
    col_index = lax.axis_index("col")
    segment_ids = lax.dynamic_slice_in_dim(segments, col_index * tokens, tokens, 0)
    query_cols = query_weight.shape[2]
    gate_cols = mixer_gate_weight.shape[2]
    input_cols = mixer_input_weight.shape[2]
    split_cols = query_cols + gate_cols + input_cols
    heads_row = step_bias.shape[1]
    kv_index = row_index * (query_cols // HEAD) // (HEADS // KV_HEADS)
    layout = (
        query_cols,
        gate_cols,
        input_cols,
        keyval_weight.shape[2],
        state_weight.shape[2],
        kv_index,
        row_index * heads_row,
        heads_row,
    )
    weights = (
        input_gain,
        query_weight,
        keyval_weight,
        mixer_gate_weight,
        mixer_input_weight,
        state_weight,
        step_weight,
        conv_values,
        conv_shared,
        step_bias,
        decay_log,
        skip_gain,
        attention_out,
        mixer_out,
        post_gain,
        gate_weight,
        up_weight,
        down_weight,
    )
    hidden = hidden_in.astype(jnp.float32)
    stored = []
    for layer_index in range(LAYERS):
        params = tuple((stacked[layer_index] for stacked in weights))
        hidden_next, saved = layer_run(hidden, params, segment_ids, layout, width)
        stored.append(saved)
        hidden = hidden_next
    grad_hidden = cotangent.astype(jnp.float32)
    collected = []
    for layer_index in reversed(range(LAYERS)):
        params = tuple((stacked[layer_index] for stacked in weights))
        saved = stored[layer_index]
        grad_hidden, layer_grads = layer_back(
            grad_hidden, saved, params, row_index, width, split_cols
        )
        collected.insert(0, layer_grads)
    stacked_grads = tuple(
        (jnp.stack([entry[member] for entry in collected]) for member in range(11))
    )
    stacked_grads = reduce_grads(stacked_grads)
    (
        mixer_grad,
        out_grad,
        ffn_grad,
        down_grad,
        conv_values_grad,
        conv_shared_grad,
        step_bias_grad,
        decay_log_grad,
        skip_gain_grad,
        input_gain_grad,
        post_gain_grad,
    ) = stacked_grads
    kv_end = split_cols + keyval_weight.shape[2]
    state_end = kv_end + state_weight.shape[2]
    ffn_half = gate_weight.shape[2]
    attn_rows = attention_out.shape[1]
    return (
        hidden.astype(jnp.bfloat16),
        grad_hidden,
        input_gain_grad,
        mixer_grad[:, :, :query_cols],
        mixer_grad[:, :, split_cols:kv_end],
        mixer_grad[:, :, query_cols : query_cols + gate_cols],
        mixer_grad[:, :, query_cols + gate_cols : split_cols],
        mixer_grad[:, :, kv_end:state_end],
        mixer_grad[:, :, state_end:],
        conv_values_grad,
        conv_shared_grad,
        step_bias_grad,
        decay_log_grad,
        skip_gain_grad,
        out_grad[:, :attn_rows, :],
        out_grad[:, attn_rows:, :],
        post_gain_grad,
        ffn_grad[:, :, :ffn_half],
        ffn_grad[:, :, ffn_half:],
        down_grad,
    )


def solution(mesh):
    placed = (
        P(("dp", "row"), "col"),
        P("dp"),
        P(("dp", "row"), "col"),
        P(None, "col"),
        P(None, "col", "row"),
        P(None, "col", None),
        P(None, "col", "row"),
        P(None, "col", "row"),
        P(None, "col", None),
        P(None, "col", None),
        P(None, None, "row"),
        P(),
        P(None, "row"),
        P(None, "row"),
        P(None, "row"),
        P(None, "row", "col"),
        P(None, "row", "col"),
        P(None, "col"),
        P(None, "col", "row"),
        P(None, "col", "row"),
        P(None, "row", "col"),
    )
    return jax.shard_map(
        shards,
        mesh=mesh,
        in_specs=placed,
        out_specs=(
            P(("dp", "row"), "col"),
            P(("dp", "row"), "col"),
            P(None, "col"),
            P(None, "col", "row"),
            P(None, "col", None),
            P(None, "col", "row"),
            P(None, "col", "row"),
            P(None, "col", None),
            P(None, "col", None),
            P(None, None, "row"),
            P(),
            P(None, "row"),
            P(None, "row"),
            P(None, "row"),
            P(None, "row", "col"),
            P(None, "row", "col"),
            P(None, "col"),
            P(None, "col", "row"),
            P(None, "col", "row"),
            P(None, "row", "col"),
        ),
        check_vma=False,
    )
```

profile of v0, /device:TPU:0, one launch (start us, length us, event | category | flops | bytes accessed | tf_op | source)
XLA Modules:
  0.0 2948.4 jit_solution(17855262520182137801)
XLA Ops:
  53.8 191.9 %reduce-scatter.17.cloned.1.call-done = f32[512,1432]{0,1:T(8,128)} async-done(((f32[2048,1432]{0,1:T(8,128)}), f32[512,1432]{0,1:T(8,128)}) %reduce-scatter.17.cloned.1.call-update) | async-done | bytes 2932752 | tf_op jit(solution)/shard_map/reduce_scatter | solution.py:184
  269.7 77.8 %while.102 = (s32[]{:T(128)}, f32[6,64,128]{2,1,0:T(8,128)S(1)}, f32[4,128,6,64]{1,0,3,2:T(4,128)}, f32[4,6,64,128]{3,2,1,0:T(8,128)}, f32[4,128,6]{2,1,0:T(8,12...) while((s32[]{:T(128)}, f32[6,64,128]{2,1,0:T(8,128)S(1)}, ...), condition=%wide.region_7.9_spmd.clone, body=%wide.region_5.8_spmd.clone.sunk | while | flops 252710400 | bytes 2995063 | solution.py:112
  351.8 45.7 %all-gather.19.cloned.1.call-done = bf16[2048,512]{0,1:T(8,128)(2,1)} async-done(((bf16[512,512]{0,1:T(8,128)(2,1)}), bf16[2048,512]{0,1:T(8,128)(2,1)}) %all-gather.19.cloned.1.call-update) | async-done | bytes 2097168 | tf_op jit(solution)/shard_map/all_gather | solution.py:194
  402.4 29.2 reduce-scatter.19.cloned.1.call-done
  465.3 144.6 %reduce-scatter.21.cloned.1.call-done = f32[512,1024]{1,0:T(8,128)} async-done(((f32[2048,1024]{1,0:T(8,128)}), f32[512,1024]{1,0:T(8,128)}) %reduce-scatter.21.cloned.1.call-update) | async-done | bytes 2097168 | tf_op jit(solution)/shard_map/reduce_scatter | solution.py:184
  613.4 46.8 %all-gather.23.cloned.1.call-done = bf16[2048,512]{1,0:T(8,128)(2,1)} async-done(((bf16[512,512]{1,0:T(8,128)(2,1)}), bf16[2048,512]{1,0:T(8,128)(2,1)}) %all-gather.23.cloned.1.call-update) | async-done | bytes 2097168 | tf_op jit(solution)/shard_map/all_gather | solution.py:194
  663.9 30.3 %reduce-scatter.23.cloned.1.call-done = f32[512,256]{1,0:T(8,128)} async-done(((f32[2048,256]{1,0:T(8,128)}), f32[512,256]{1,0:T(8,128)}) %reduce-scatter.23.cloned.1.call-update) | async-done | bytes 524304 | tf_op jit(solution)/shard_map/reduce_scatter | solution.py:201
  730.7 196.9 %reduce-scatter.25.cloned.1.call-done = f32[512,1432]{0,1:T(8,128)} async-done(((f32[2048,1432]{0,1:T(8,128)}), f32[512,1432]{0,1:T(8,128)}) %reduce-scatter.25.cloned.1.call-update) | async-done | bytes 2932752 | tf_op jit(solution)/shard_map/reduce_scatter | solution.py:184
  953.7 78.8 %while.103 = (s32[]{:T(128)}, f32[6,64,128]{2,1,0:T(8,128)S(1)}, f32[4,128,6,64]{1,0,3,2:T(4,128)}, f32[4,6,64,128]{3,2,1,0:T(8,128)}, f32[4,128,6]{2,1,0:T(8,12...) while((s32[]{:T(128)}, f32[6,64,128]{2,1,0:T(8,128)S(1)}, ...), condition=%wide.region_20.22_spmd.clone, body=%wide.region_18.21_spmd.clone.sunk | while | flops 252710400 | bytes 2995063 | solution.py:112
  1035.4 47.1 %all-gather.27.cloned.1.call-done = bf16[2048,512]{0,1:T(8,128)(2,1)} async-done(((bf16[512,512]{0,1:T(8,128)(2,1)}), bf16[2048,512]{0,1:T(8,128)(2,1)}) %all-gather.27.cloned.1.call-update) | async-done | bytes 2097168 | tf_op jit(solution)/shard_map/all_gather | solution.py:194
  1086.2 30.3 %reduce-scatter.27.cloned.1.call-done = f32[512,256]{1,0:T(8,128)} async-done(((f32[2048,256]{1,0:T(8,128)}), f32[512,256]{1,0:T(8,128)}) %reduce-scatter.27.cloned.1.call-update) | async-done | bytes 524304 | tf_op jit(solution)/shard_map/reduce_scatter | solution.py:201
  1166.9 142.7 %reduce-scatter.29.cloned.1.call-done = f32[512,1024]{1,0:T(8,128)} async-done(((f32[2048,1024]{1,0:T(8,128)}), f32[512,1024]{1,0:T(8,128)}) %reduce-scatter.29.cloned.1.call-update) | async-done | bytes 2097168 | tf_op jit(solution)/shard_map/reduce_scatter | solution.py:184
  1312.2 77.1 %reduce-scatter.33.cloned.1.call-done = f32[512,512]{1,0:T(8,128)} async-done(((f32[2048,512]{1,0:T(8,128)}), f32[512,512]{1,0:T(8,128)}) %reduce-scatter.33.cloned.1.call-update) | async-done | bytes 1048592 | tf_op jit(solution)/shard_map/reduce_scatter | solution.py:220
  1393.9 81.4 %all-gather.35.cloned.1.call-done = bf16[2048,1024]{1,0:T(8,128)(2,1)} async-done(((bf16[512,1024]{1,0:T(8,128)(2,1)}), bf16[2048,1024]{1,0:T(8,128)(2,1)}) %all-gather.35.cloned.1.call-update) | async-done | bytes 4194320 | tf_op jit(solution)/shard_map/all_gather | solution.py:230
  1480.3 30.1 %reduce-scatter.35.cloned.1.call-done = f32[512,256]{1,0:T(8,128)} async-done(((f32[2048,256]{1,0:T(8,128)}), f32[512,256]{1,0:T(8,128)}) %reduce-scatter.35.cloned.1.call-update) | async-done | bytes 524304 | tf_op jit(solution)/shard_map/reduce_scatter | solution.py:239
  1547.2 75.1 %reduce-scatter.37.cloned.1.call-done = f32[512,512]{0,1:T(8,128)} async-done(((f32[2048,512]{0,1:T(8,128)}), f32[512,512]{0,1:T(8,128)}) %reduce-scatter.37.cloned.1.call-update) | async-done | bytes 1048592 | tf_op jit(solution)/shard_map/reduce_scatter | solution.py:220
  1630.3 96.6 %while.104 = (s32[]{:T(128)}, f32[6]{0:T(128)S(1)}, f32[6,64,128]{2,1,0:T(8,128)S(1)}, f32[4,128,6,64]{1,0,3,2:T(4,128)}, f32[4,128,128]{2,1,0:T(8,128)S(1)}, /*...) while((s32[]{:T(128)}, f32[6]{0:T(128)S(1)}, ...), condition=%wide.region_43.45_spmd.clone, body=%wide.region_31.44_spmd.clone.sunk | while | flops 606731008 | bytes 7752462 | solution.py:112
  1769.0 26.8 all-reduce.75
  1799.4 105.9 %all-gather.39.cloned.1.call-done = bf16[2048,1432]{0,1:T(8,128)(2,1)} async-done(((bf16[512,1432]{0,1:T(8,128)(2,1)}), bf16[2048,1432]{0,1:T(8,128)(2,1)}) %all-gather.39.cloned.1.call-update) | async-done | bytes 5865488 | tf_op jit(solution)/shard_map/all_gather | solution.py:230
  1910.1 41.6 %all-gather.31.cloned.1.call-done = bf16[2048,512]{1,0:T(8,128)(2,1)} async-done(((bf16[512,512]{1,0:T(8,128)(2,1)}), bf16[2048,512]{1,0:T(8,128)(2,1)}) %all-gather.31.cloned.1.call-update) | async-done | bytes 2097168 | tf_op jit(solution)/shard_map/all_gather | solution.py:194
  1957.1 27.3 reduce-scatter.39.cloned.1.call-done
  1999.1 19.3 reduce-scatter.31.cloned.1.call-done
  2020.7 16.8 all-gather.41.cloned.1.call-done
  2041.7 76.9 %reduce-scatter.41.cloned.1.call-done = f32[512,512]{1,0:T(8,128)} async-done(((f32[2048,512]{1,0:T(8,128)}), f32[512,512]{1,0:T(8,128)}) %reduce-scatter.41.cloned.1.call-update) | async-done | bytes 1048592 | tf_op jit(solution)/shard_map/reduce_scatter | solution.py:220
  2121.5 81.4 %all-gather.43.cloned.1.call-done = bf16[2048,1024]{1,0:T(8,128)(2,1)} async-done(((bf16[512,1024]{1,0:T(8,128)(2,1)}), bf16[2048,1024]{1,0:T(8,128)(2,1)}) %all-gather.43.cloned.1.call-update) | async-done | bytes 4194320 | tf_op jit(solution)/shard_map/all_gather | solution.py:230
  2207.8 30.0 %reduce-scatter.43.cloned.1.call-done = f32[512,256]{1,0:T(8,128)} async-done(((f32[2048,256]{1,0:T(8,128)}), f32[512,256]{1,0:T(8,128)}) %reduce-scatter.43.cloned.1.call-update) | async-done | bytes 524304 | tf_op jit(solution)/shard_map/reduce_scatter | solution.py:239
  2274.1 74.6 %reduce-scatter.45.cloned.1.call-done = f32[512,512]{0,1:T(8,128)} async-done(((f32[2048,512]{0,1:T(8,128)}), f32[512,512]{0,1:T(8,128)}) %reduce-scatter.45.cloned.1.call-update) | async-done | bytes 1048592 | tf_op jit(solution)/shard_map/reduce_scatter | solution.py:220
  2355.6 183.9 %while.105 = (s32[]{:T(128)}, f32[6]{0:T(128)}, f32[6,64,128]{2,1,0:T(8,128)}, f32[4,128,6,64]{1,0,3,2:T(4,128)}, f32[4,128,128]{2,1,0:T(8,128)}, /*index=5*/f32...) while((s32[]{:T(128)}, f32[6]{0:T(128)}, ...), condition=%wide.region_70.72_spmd.clone, body=%wide.region_58.71_spmd.clone.sunk | while | flops 606731008 | bytes 8121266 | solution.py:112
  2578.8 26.6 all-reduce.76
  2606.6 108.2 %all-gather.47.cloned.1.call-done = bf16[2048,1432]{0,1:T(8,128)(2,1)} async-done(((bf16[512,1432]{0,1:T(8,128)(2,1)}), bf16[2048,1432]{0,1:T(8,128)(2,1)}) %all-gather.47.cloned.1.call-update) | async-done | bytes 5865488 | tf_op jit(solution)/shard_map/all_gather | solution.py:230
  2744.6 35.9 %all-reduce.66 = (f32[2,4,384]{2,1,0:T(4,128)}, f32[2,4,256]{2,1,0:T(4,128)}, f32[2,6]{1,0:T(2,128)}, f32[2,6]{1,0:T(2,128)}, f32[2,6]{1,0:T(2,128)}) all-reduce(f32[2,4,384]{2,1,0:T(4,128)S(1)} %pad_maximum_fusion.20, f32[2,4,256]{2,1,0:T(4,128)S(1)} %pad_maximum_fusion.21, ...), channel_id=1, replica_groups=mesh['dp'=2,'row'=4,'col'=4] {'dp','col'}, use_global_device_ids=true, to_apply=%region_92.94 | all-reduce | flops 5156 | bytes 41248 | tf_op jit(solution)/shard_map/psum | solution.py:418
  2804.6 120.7 %all-reduce.74.cloned.1.call-done = (f32[2,256,1432]{1,2,0:T(8,128)}, f32[2,512,256]{2,1,0:T(8,128)}, f32[2,256,1024]{2,1,0:T(8,128)}, f32[2,512,256]{2,1,0:T(8,128)}) async-done(((f32[2,256,1432]{1,2,0:T(8,128)}, f32[2,512,256]{2,1,0:T(8,128)}, f32[2,256,1024]{2,1,0:T(8,128)}, f32[2,512,256]{2,1,0:T(8,128)}), (f32[2,256,1432]{1,2,0:T(8,128)}, f32[2,512,256]{2,1,0:T(8,128)}, f32[2,256,1024]{2,1,0:T(8,128)}, ...) | async-done | bytes 7127056 | tf_op jit(solution)/shard_map/psum | solution.py:415
  (1450 shorter events, 946.8 us)
Async XLA Ops:
  7.2 32.9 %all-gather.17.cloned.1.call-start = ((), (), s32[]{:S(2)}) async-start(), calls=%async_computation.16 | async-start | bytes 1310720 | tf_op jit(solution)/shard_map/all_gather | solution.py:177
  25.1 220.7 %reduce-scatter.17.cloned.1.call-start = ((), (), s32[]{:S(2)}) async-start(), calls=%async_computation.17 | async-start | bytes 14663680 | tf_op jit(solution)/shard_map/reduce_scatter | solution.py:184
  47.5 350.0 %all-gather.19.cloned.1.call-start = ((), (), s32[]{:S(2)}) async-start(), calls=%async_computation.18 | async-start | bytes 2621440 | tf_op jit(solution)/shard_map/all_gather | solution.py:194
  350.4 81.2 %reduce-scatter.19.cloned.1.call-start = ((), (), s32[]{:S(2)}) async-start(), calls=%async_computation.19 | async-start | bytes 2621440 | tf_op jit(solution)/shard_map/reduce_scatter | solution.py:201
  401.2 58.2 %all-gather.21.cloned.1.call-start = ((), (), s32[]{:S(2)}) async-start(), calls=%async_computation.20 | async-start | bytes 1310720 | tf_op jit(solution)/shard_map/all_gather | solution.py:177
  445.3 164.6 %reduce-scatter.21.cloned.1.call-start = ((), (), s32[]{:S(2)}) async-start(), calls=%async_computation.21 | async-start | bytes 10485760 | tf_op jit(solution)/shard_map/reduce_scatter | solution.py:184
  465.3 194.9 %all-gather.23.cloned.1.call-start = ((), (), s32[]{:S(2)}) async-start(), calls=%async_computation.22 | async-start | bytes 2621440 | tf_op jit(solution)/shard_map/all_gather | solution.py:194
  613.3 80.8 %reduce-scatter.23.cloned.1.call-start = ((), (), s32[]{:S(2)}) async-start(), calls=%async_computation.23 | async-start | bytes 2621440 | tf_op jit(solution)/shard_map/reduce_scatter | solution.py:201
  663.8 58.2 %all-gather.25.cloned.1.call-start = ((), (), s32[]{:S(2)}) async-start(), calls=%async_computation.24 | async-start | bytes 1310720 | tf_op jit(solution)/shard_map/all_gather | solution.py:177
  707.9 219.7 %reduce-scatter.25.cloned.1.call-start = ((), (), s32[]{:S(2)}) async-start(), calls=%async_computation.25 | async-start | bytes 14663680 | tf_op jit(solution)/shard_map/reduce_scatter | solution.py:184
  729.4 353.1 %all-gather.27.cloned.1.call-start = ((), (), s32[]{:S(2)}) async-start(), calls=%async_computation.26 | async-start | bytes 2621440 | tf_op jit(solution)/shard_map/all_gather | solution.py:194
  1035.4 81.1 %reduce-scatter.27.cloned.1.call-start = ((), (), s32[]{:S(2)}) async-start(), calls=%async_computation.27 | async-start | bytes 2621440 | tf_op jit(solution)/shard_map/reduce_scatter | solution.py:201
  1086.2 58.3 %all-gather.29.cloned.1.call-start = ((), (), s32[]{:S(2)}) async-start(), calls=%async_computation.28 | async-start | bytes 1310720 | tf_op jit(solution)/shard_map/all_gather | solution.py:177
  1131.0 178.6 %reduce-scatter.29.cloned.1.call-start = ((), (), s32[]{:S(2)}) async-start(), calls=%async_computation.29 | async-start | bytes 10485760 | tf_op jit(solution)/shard_map/reduce_scatter | solution.py:184
  1150.5 238.9 %reduce-scatter.33.cloned.1.call-start = ((), (), s32[]{:S(2)}) async-start(), calls=%async_computation.33 | async-start | bytes 5242880 | tf_op jit(solution)/shard_map/reduce_scatter | solution.py:220
  1166.9 308.5 %all-gather.35.cloned.1.call-start = ((), (), s32[]{:S(2)}) async-start(), calls=%async_computation.34 | async-start | bytes 5242880 | tf_op jit(solution)/shard_map/all_gather | solution.py:230
  1393.9 116.5 %reduce-scatter.35.cloned.1.call-start = ((), (), s32[]{:S(2)}) async-start(), calls=%async_computation.35 | async-start | bytes 2621440 | tf_op jit(solution)/shard_map/reduce_scatter | solution.py:239
  1480.3 61.1 %all-gather.37.cloned.1.call-start = ((), (), s32[]{:S(2)}) async-start(), calls=%async_computation.36 | async-start | bytes 1310720 | tf_op jit(solution)/shard_map/all_gather | solution.py:211
  1527.2 95.1 %reduce-scatter.37.cloned.1.call-start = ((), (), s32[]{:S(2)}) async-start(), calls=%async_computation.37 | async-start | bytes 5242880 | tf_op jit(solution)/shard_map/reduce_scatter | solution.py:220
  1545.4 359.9 %all-gather.39.cloned.1.call-start = ((), (), s32[]{:S(2)}) async-start(), calls=%async_computation.38 | async-start | bytes 7331840 | tf_op jit(solution)/shard_map/all_gather | solution.py:230
  1797.1 154.5 %all-gather.31.cloned.1.call-start = ((), (), s32[]{:S(2)}) async-start(), calls=%async_computation.30 | async-start | bytes 2621440 | tf_op jit(solution)/shard_map/all_gather | solution.py:194
  1797.9 186.5 %reduce-scatter.39.cloned.1.call-start = ((), (), s32[]{:S(2)}) async-start(), calls=%async_computation.39 | async-start | bytes 2621440 | tf_op jit(solution)/shard_map/reduce_scatter | solution.py:239
  1910.0 108.4 %reduce-scatter.31.cloned.1.call-start = ((), (), s32[]{:S(2)}) async-start(), calls=%async_computation.31 | async-start | bytes 2621440 | tf_op jit(solution)/shard_map/reduce_scatter | solution.py:201
  1955.4 82.2 %all-gather.41.cloned.1.call-start = ((), (), s32[]{:S(2)}) async-start(), calls=%async_computation.40 | async-start | bytes 1310720 | tf_op jit(solution)/shard_map/all_gather | solution.py:211
  2020.7 97.8 %reduce-scatter.41.cloned.1.call-start = ((), (), s32[]{:S(2)}) async-start(), calls=%async_computation.41 | async-start | bytes 5242880 | tf_op jit(solution)/shard_map/reduce_scatter | solution.py:220
  2041.6 161.3 %all-gather.43.cloned.1.call-start = ((), (), s32[]{:S(2)}) async-start(), calls=%async_computation.42 | async-start | bytes 5242880 | tf_op jit(solution)/shard_map/all_gather | solution.py:230
  2121.4 116.4 %reduce-scatter.43.cloned.1.call-start = ((), (), s32[]{:S(2)}) async-start(), calls=%async_computation.43 | async-start | bytes 2621440 | tf_op jit(solution)/shard_map/reduce_scatter | solution.py:239
  2207.7 59.9 %all-gather.45.cloned.1.call-start = ((), (), s32[]{:S(2)}) async-start(), calls=%async_computation.44 | async-start | bytes 1310720 | tf_op jit(solution)/shard_map/all_gather | solution.py:211
  2253.5 95.2 %reduce-scatter.45.cloned.1.call-start = ((), (), s32[]{:S(2)}) async-start(), calls=%async_computation.45 | async-start | bytes 5242880 | tf_op jit(solution)/shard_map/reduce_scatter | solution.py:220
  2271.7 443.1 %all-gather.47.cloned.1.call-start = ((), (), s32[]{:S(2)}) async-start(), calls=%async_computation.46 | async-start | bytes 7331840 | tf_op jit(solution)/shard_map/all_gather | solution.py:230
  2606.6 173.9 %reduce-scatter.47.cloned.1.call-start = ((), (), s32[]{:S(2)}) async-start(), calls=%async_computation.47 | async-start | bytes 2621440 | tf_op jit(solution)/shard_map/reduce_scatter | solution.py:239
  2719.7 205.6 %all-reduce.74.cloned.1.call-start = ((), (), s32[]{:S(2)}) async-start(), calls=%async_computation.48 | async-start | bytes 14254080 | tf_op jit(solution)/shard_map/psum | solution.py:415
  (271 other events, 15354.2 us)
Sparse Core Ops, SparseCore 0:
  25.2 14.9 all-gather.16
  47.6 198.0 reduce-scatter.16
  350.5 46.9 all-gather.18
  401.4 30.1 reduce-scatter.18
  445.4 13.9 all-gather.20
  465.4 144.4 reduce-scatter.20
  613.5 46.6 all-gather.22
  664.0 30.1 reduce-scatter.22
  708.1 13.9 all-gather.24
  729.5 198.1 reduce-scatter.24
  1035.5 46.9 all-gather.26
  1086.3 30.1 reduce-scatter.26
  1146.0 16.7 all-gather.32
  1165.1 144.4 reduce-scatter.28
  1311.8 77.4 reduce-scatter.32
  1394.0 81.2 all-gather.34
  1480.4 29.9 reduce-scatter.34
  1527.3 13.9 all-gather.36
  1545.5 76.7 reduce-scatter.36
  1797.3 107.9 all-gather.38
  1907.4 44.1 all-gather.30
  1954.2 30.1 reduce-scatter.38
  1986.9 31.4 reduce-scatter.30
  2020.8 16.7 all-gather.40
  2041.7 76.7 reduce-scatter.40
  2121.6 81.2 all-gather.42
  2207.8 29.9 reduce-scatter.42
  2253.6 13.9 all-gather.44
  2271.9 76.7 reduce-scatter.44
  2606.7 108.1 all-gather.46
  2719.8 29.6 reduce-scatter.46
  2752.5 172.7 all-reduce.73
  (1 shorter events, 13.9 us)
where the time goes:
time: 2960 us; the launch traced here: 2950 us
  waiting for transfers between devices  1960 us (66%)
  local copies, waits for them, and re-layouts  292 us (10%)
  matrix products  247 us (8%)
  other arithmetic  208 us (7%)
  blocking collectives  195 us (7%)
    reduce_scatter x4, waiting for transfers between devices, project_in(): lax.psum_scatter(product_term(jnp.int32(0), normed_low.shape[0] * lax.axi...  676 us
    all_gather x4, waiting for transfers between devices, project_back(): gathered = lax.all_gather(grad_low, 'col', axis=0, tiled=True)  377 us
    reduce_scatter x4, waiting for transfers between devices, branch_back(): lax.psum_scatter(product_term(jnp.int32(0), grad_low.shape[0] * lax.axis_...  304 us
    all_gather x4, waiting for transfers between devices, project_out(): gathered = lax.all_gather(middle_low, 'col', axis=0, tiled=True)  181 us
    psum x1, waiting for transfers between devices, reduce_grads(): lax.psum((mixer_grad, out_grad, ffn_grad, down_grad), 'dp')  121 us
    reduce_scatter x4, waiting for transfers between devices, project_out(): lax.psum_scatter(product_term(jnp.int32(0), middle_low.shape[0] * lax.axi...  109 us
    dynamic_update_slice x16, local copies, waits for them, and re-layouts, scan_spans(): ignored, outputs = lax.scan(jax.checkpoint(span_step), zero_state, pieces)  95.3 us
    reduce_scatter x4, waiting for transfers between devices, project_back(): lax.psum_scatter(product_term(jnp.int32(0), grad_low.shape[0] * lax.axis_...  87.4 us
  transfers between devices with their start and end apart: 33, of which 32 were waited for; matrix products, arithmetic and copies ran while one was open for 2% of the time, Pallas kernels for 0%

commit v1 on v0

v1 whole, which is shorter than its diff:
```python
from functools import partial

import jax
import jax.numpy as jnp
from jax import lax
from jax.experimental import pallas as pl
from jax.experimental.pallas import tpu as pltpu
from jax.sharding import PartitionSpec as P

HEADS = 8
KV_HEADS = 2
HEAD = 64
M_HEAD = 64
LAYERS = 2
LANES = 128
ROWS = 128

epsilon = 1e-05
highest = lax.Precision.HIGHEST
f32 = jnp.float32
bf16 = jnp.bfloat16

NN = (((1,), (0,)), ((), ()))
NT = (((1,), (1,)), ((), ()))
TN = (((0,), (0,)), ((), ()))


def dot(left, right, dims=NN, precision=None):
    return lax.dot_general(left, right, dims, precision=precision, preferred_element_type=f32)


def left_lanes():
    return lax.broadcasted_iota(jnp.int32, (ROWS, LANES), 1) < HEAD


def side_lanes():
    lane = lax.broadcasted_iota(jnp.int32, (ROWS, LANES), 1)
    return lane < HEAD, lane >= HEAD


def prepare(block, sizes, proj_ref, link_ref, taps_ref, heads_ref, spread_ref):
    first, last = block * ROWS, (block + 1) * ROWS
    conv_first, conv_last, steps_first = sizes[2], sizes[4], sizes[5]
    signal = proj_ref[first:last, conv_first:conv_last]
    if block == 0:
        prior = jnp.zeros((8, conv_last - conv_first), f32)
    else:
        prior = proj_ref[first - 8 : first, conv_first:conv_last]
    joined = jnp.concatenate([prior, signal], axis=0)
    pre = signal * taps_ref[0:1, :]
    for offset in range(1, 4):
        earlier = joined[8 - offset : 8 - offset + ROWS]
        pre = pre + earlier * taps_ref[offset : offset + 1, :] * link_ref[first:last, offset : offset + 1]
    raw = proj_ref[first:last, steps_first : steps_first + LANES] + heads_ref[0:1, :]
    steps = jnp.maximum(raw, 0.0) + jnp.log1p(jnp.exp(-jnp.abs(raw)))
    wide = dot(steps, spread_ref[...], NN, highest)
    return pre, raw, steps, wide


def running(steps, heads_ref, carry):
    lower = (
        lax.broadcasted_iota(jnp.int32, (ROWS, ROWS), 0)
        >= lax.broadcasted_iota(jnp.int32, (ROWS, ROWS), 1)
    ).astype(f32)
    return dot(lower, -steps * heads_ref[1:2, :], NN, highest) + carry


def key_value(block, sizes, proj_ref):
    pair = proj_ref[block * ROWS : (block + 1) * ROWS, sizes[4] : sizes[5]]
    turned = pltpu.roll(pair, HEAD, 1)
    left = left_lanes()
    return jnp.where(left, pair, turned).astype(bf16), jnp.where(left, turned, pair).astype(bf16)


def hidden_links(block, segc_ref, segr_ref):
    width = (block + 1) * ROWS
    token = lax.broadcasted_iota(jnp.int32, (ROWS, width), 0) + block * ROWS
    source = lax.broadcasted_iota(jnp.int32, (ROWS, width), 1)
    same = segc_ref[block * ROWS : width, :] == segr_ref[:, :width]
    return jnp.where((token >= source) & same, 0.0, -1e30)


def mixer_forward_kernel(
    sizes,
    proj_ref,
    segc_ref,
    segr_ref,
    link_ref,
    taps_ref,
    heads_ref,
    skip_ref,
    spread_ref,
    out_ref,
    inner_s,
    xdt_s,
    b_s,
    c_s,
    cum_s,
    turned_s,
    key_s,
    value_s,
):
    blocks = proj_ref.shape[0] // ROWS
    width = sizes[3] - sizes[2]
    carry = jnp.zeros((1, LANES), f32)
    for block in range(blocks):
        rows = slice(block * ROWS, (block + 1) * ROWS)
        pre, raw, steps, wide = prepare(
            block, sizes, proj_ref, link_ref, taps_ref, heads_ref, spread_ref
        )
        active = pre * jax.nn.sigmoid(pre)
        inner = active[:, :width]
        inner_s[rows, :] = inner
        xdt_s[rows, :] = (inner * wide).astype(bf16)
        b_s[rows, :] = active[:, width : width + LANES].astype(bf16)
        c_s[rows, :] = active[:, width + LANES :].astype(bf16)
        cum = running(steps, heads_ref, carry)
        carry = cum[ROWS - 1 :, :]
        cum_s[rows, :] = cum
        turned_s[:, rows] = cum.T
        key_s[rows, :], value_s[rows, :] = key_value(block, sizes, proj_ref)
    left = left_lanes()
    for block in range(blocks):
        rows = slice(block * ROWS, (block + 1) * ROWS)
        span = (block + 1) * ROWS
        bias = hidden_links(block, segc_ref, segr_ref)
        query = proj_ref[rows, : sizes[1]]
        parts = []
        for side in range(2):
            chosen = jnp.where(side_lanes()[side], query, 0.0).astype(bf16)
            scores = dot(chosen, key_s[:span, :], NT) * (HEAD**-0.5) + bias
            weights = jnp.exp(scores - jnp.max(scores, axis=1, keepdims=True))
            weights = weights * (1.0 / jnp.sum(weights, axis=1, keepdims=True))
            parts.append(dot(weights.astype(bf16), value_s[:span, :]))
        out_ref[rows, : sizes[1]] = jnp.where(left, parts[0], parts[1]).astype(bf16)
        affinity = dot(c_s[rows, :], b_s[:span, :], NT)
        for pair in range(width // LANES):
            cols = slice(pair * LANES, (pair + 1) * LANES)
            parts = []
            for side in range(2):
                head = 2 * pair + side
                decay = jnp.exp(
                    cum_s[rows, head : head + 1] - turned_s[head : head + 1, :span] + bias
                )
                parts.append(dot((affinity * decay).astype(bf16), xdt_s[:span, cols]))
            scanned = jnp.where(left, parts[0], parts[1])
            scanned = scanned + skip_ref[:, cols] * inner_s[rows, cols]
            gate = proj_ref[rows, sizes[1] + pair * LANES : sizes[1] + (pair + 1) * LANES]
            out_ref[rows, sizes[1] + pair * LANES : sizes[1] + (pair + 1) * LANES] = (
                scanned * gate * jax.nn.sigmoid(gate)
            ).astype(bf16)


def mixer_backward_kernel(
    sizes,
    proj_ref,
    dmix_ref,
    segc_ref,
    segr_ref,
    link_ref,
    taps_ref,
    heads_ref,
    skip_ref,
    spread_ref,
    dproj_ref,
    dtaps_ref,
    dheads_ref,
    inner_s,
    xdt_s,
    b_s,
    c_s,
    cum_s,
    turned_s,
    key_s,
    value_s,
    pre_s,
    dscan_s,
    dxdt_s,
    db_s,
    dc_s,
    dkey_s,
    dvalue_s,
    dcum_s,
    dpre_s,
):
    length = proj_ref.shape[0]
    blocks = length // ROWS
    width = sizes[3] - sizes[2]
    conv_first, conv_last, steps_first = sizes[2], sizes[4], sizes[5]
    conv_width = conv_last - conv_first
    carry = jnp.zeros((1, LANES), f32)
    for block in range(blocks):
        rows = slice(block * ROWS, (block + 1) * ROWS)
        pre, raw, steps, wide = prepare(
            block, sizes, proj_ref, link_ref, taps_ref, heads_ref, spread_ref
        )
        pre_s[rows, :] = pre
        active = pre * jax.nn.sigmoid(pre)
        inner = active[:, :width]
        inner_s[rows, :] = inner
        xdt_s[rows, :] = (inner * wide).astype(bf16)
        b_s[rows, :] = active[:, width : width + LANES].astype(bf16)
        c_s[rows, :] = active[:, width + LANES :].astype(bf16)
        cum = running(steps, heads_ref, carry)
        carry = cum[ROWS - 1 :, :]
        cum_s[rows, :] = cum
        turned_s[:, rows] = cum.T
        key_s[rows, :], value_s[rows, :] = key_value(block, sizes, proj_ref)
    dxdt_s[...] = jnp.zeros_like(dxdt_s)
    db_s[...] = jnp.zeros_like(db_s)
    dkey_s[...] = jnp.zeros_like(dkey_s)
    dvalue_s[...] = jnp.zeros_like(dvalue_s)
    left = left_lanes()
    dskip = jnp.zeros((1, width), f32)
    for block in range(blocks):
        rows = slice(block * ROWS, (block + 1) * ROWS)
        span = (block + 1) * ROWS
        bias = hidden_links(block, segc_ref, segr_ref)
        query = proj_ref[rows, : sizes[1]]
        dattended = dmix_ref[rows, : sizes[1]]
        parts = []
        for side in range(2):
            own = side_lanes()[side]
            chosen = jnp.where(own, query, 0.0).astype(bf16)
            dchosen = jnp.where(own, dattended, 0.0).astype(bf16)
            scores = dot(chosen, key_s[:span, :], NT) * (HEAD**-0.5) + bias
            weights = jnp.exp(scores - jnp.max(scores, axis=1, keepdims=True))
            weights = weights * (1.0 / jnp.sum(weights, axis=1, keepdims=True))
            dweights = dot(dchosen, value_s[:span, :], NT)
            dvalue_s[:span, :] += dot(weights.astype(bf16), dchosen, TN)
            mean = jnp.sum(weights * dweights, axis=1, keepdims=True)
            dscores = (weights * (dweights - mean) * (HEAD**-0.5)).astype(bf16)
            parts.append(dot(dscores, key_s[:span, :]))
            dkey_s[:span, :] += dot(dscores, chosen, TN)
        dproj_ref[rows, : sizes[1]] = jnp.where(left, parts[0], parts[1]).astype(bf16)
        affinity = dot(c_s[rows, :], b_s[:span, :], NT)
        daffinity = jnp.zeros((ROWS, span), f32)
        dcum = jnp.zeros((ROWS, LANES), f32)
        for pair in range(width // LANES):
            cols = slice(pair * LANES, (pair + 1) * LANES)
            gate_cols = slice(sizes[1] + pair * LANES, sizes[1] + (pair + 1) * LANES)
            gate = proj_ref[rows, gate_cols]
            lifted = jax.nn.sigmoid(gate)
            dmamba = dmix_ref[rows, gate_cols]
            dscan = dmamba * gate * lifted
            dscan_s[rows, cols] = dscan
            parts, mixes, sides = [], [], []
            for side in range(2):
                head = 2 * pair + side
                decay = jnp.exp(
                    cum_s[rows, head : head + 1] - turned_s[head : head + 1, :span] + bias
                )
                mix = (affinity * decay).astype(bf16)
                dside = jnp.where(side_lanes()[side], dscan, 0.0).astype(bf16)
                daffinity = daffinity + dot(dside, xdt_s[:span, cols], NT) * decay
                parts.append(dot(mix, xdt_s[:span, cols]))
                mixes.append(mix)
                sides.append(dside)
            dxdt_s[:span, cols] += dot(
                jnp.concatenate(mixes, axis=0), jnp.concatenate(sides, axis=0), TN
            )
            scanned = jnp.where(left, parts[0], parts[1])
            inner = inner_s[rows, cols]
            dcum = dcum + dot(
                scanned * dscan.astype(bf16).astype(f32), spread_ref[:, cols], NT, highest
            )
            scanned = scanned + skip_ref[:, cols] * inner
            dproj_ref[rows, gate_cols] = (
                dmamba * scanned * lifted * (1.0 + gate * (1.0 - lifted))
            ).astype(bf16)
        dcum_s[rows, :] = dcum
        dskip = dskip + jnp.sum(dscan_s[rows, :] * inner_s[rows, :], axis=0, keepdims=True)
        daffinity = daffinity.astype(bf16)
        dc_s[rows, :] = dot(daffinity, b_s[:span, :])
        db_s[:span, :] += dot(daffinity, c_s[rows, :], TN)
    upper = (
        lax.broadcasted_iota(jnp.int32, (ROWS, ROWS), 0)
        <= lax.broadcasted_iota(jnp.int32, (ROWS, ROWS), 1)
    ).astype(f32)
    carry = jnp.zeros((1, LANES), f32)
    dbias = jnp.zeros((1, LANES), f32)
    drate = jnp.zeros((1, LANES), f32)
    dpre_s[length:, :] = jnp.zeros((8, conv_width), f32)
    for block in reversed(range(blocks)):
        rows = slice(block * ROWS, (block + 1) * ROWS)
        raw = proj_ref[rows, steps_first : steps_first + LANES] + heads_ref[0:1, :]
        steps = jnp.maximum(raw, 0.0) + jnp.log1p(jnp.exp(-jnp.abs(raw)))
        wide = dot(steps, spread_ref[...], NN, highest)
        dxdt = dxdt_s[rows, :]
        dcum = dcum_s[rows, :] - dot(
            xdt_s[rows, :].astype(f32) * dxdt, spread_ref[...], NT, highest
        )
        dlog = dot(upper, dcum, NN, highest) + carry
        carry = dlog[0:1, :]
        dsteps = (
            dot(dxdt * inner_s[rows, :], spread_ref[...], NT, highest) - heads_ref[1:2, :] * dlog
        )
        drate = drate - jnp.sum(steps * dlog, axis=0, keepdims=True)
        draw = dsteps * jax.nn.sigmoid(raw)
        dbias = dbias + jnp.sum(draw, axis=0, keepdims=True)
        dproj_ref[rows, steps_first : steps_first + LANES] = draw.astype(bf16)
        dinner = dxdt * wide + skip_ref[...] * dscan_s[rows, :]
        dactive = jnp.concatenate([dinner, db_s[rows, :], dc_s[rows, :]], axis=1)
        pre = pre_s[rows, :]
        lifted = jax.nn.sigmoid(pre)
        dpre_s[rows, :] = dactive * lifted * (1.0 + pre * (1.0 - lifted))
        dkey = dkey_s[rows, :]
        dvalue = dvalue_s[rows, :]
        dkey = dkey + pltpu.roll(dkey, HEAD, 1)
        dvalue = dvalue + pltpu.roll(dvalue, HEAD, 1)
        dproj_ref[rows, conv_last:steps_first] = jnp.where(left, dkey, dvalue).astype(bf16)
    dtaps = [jnp.zeros((1, conv_width), f32) for _ in range(4)]
    for block in range(blocks):
        first, last = block * ROWS, (block + 1) * ROWS
        signal = proj_ref[first:last, conv_first:conv_last]
        joined = dpre_s[first : last + 8, :]
        own = joined[:ROWS]
        dsignal = own * taps_ref[0:1, :]
        dtaps[0] = dtaps[0] + jnp.sum(signal * own, axis=0, keepdims=True)
        for offset in range(1, 4):
            later = (joined * link_ref[first : last + 8, offset : offset + 1])[
                offset : offset + ROWS
            ]
            dsignal = dsignal + later * taps_ref[offset : offset + 1, :]
            dtaps[offset] = dtaps[offset] + jnp.sum(signal * later, axis=0, keepdims=True)
        dproj_ref[first:last, conv_first:conv_last] = dsignal.astype(bf16)
    dtaps_ref[...] = jnp.concatenate(dtaps + [jnp.zeros((4, conv_width), f32)], axis=0)
    dheads_ref[...] = jnp.concatenate(
        [
            dbias,
            drate * heads_ref[1:2, :],
            dot(dskip, spread_ref[...], NT, highest),
            jnp.zeros((5, LANES), f32),
        ],
        axis=0,
    )


def shared_scratch(length, width):
    return [
        pltpu.VMEM((length, width), f32),
        pltpu.VMEM((length, width), bf16),
        pltpu.VMEM((length, LANES), bf16),
        pltpu.VMEM((length, LANES), bf16),
        pltpu.VMEM((length, LANES), f32),
        pltpu.VMEM((LANES, length), f32),
        pltpu.VMEM((length, LANES), bf16),
        pltpu.VMEM((length, LANES), bf16),
    ]


def mixer_forward(sizes, proj, side):
    length, width = proj.shape[0], sizes[3] - sizes[2]
    return pl.pallas_call(
        partial(mixer_forward_kernel, sizes),
        out_shape=jax.ShapeDtypeStruct((length, sizes[2]), bf16),
        scratch_shapes=shared_scratch(length, width),
        compiler_params=pltpu.CompilerParams(vmem_limit_bytes=40 * 1024 * 1024),
        cost_estimate=pl.CostEstimate(flops=10**9, bytes_accessed=4 * 10**6, transcendentals=10**6),
        name="mixer_forward",
    )(proj, *side)


def mixer_backward(sizes, proj, dmix, side):
    length, width = proj.shape[0], sizes[3] - sizes[2]
    conv_width = sizes[4] - sizes[2]
    return pl.pallas_call(
        partial(mixer_backward_kernel, sizes),
        out_shape=(
            jax.ShapeDtypeStruct(proj.shape, bf16),
            jax.ShapeDtypeStruct((8, conv_width), f32),
            jax.ShapeDtypeStruct((8, LANES), f32),
        ),
        scratch_shapes=shared_scratch(length, width)
        + [
            pltpu.VMEM((length, conv_width), f32),
            pltpu.VMEM((length, width), f32),
            pltpu.VMEM((length, width), f32),
            pltpu.VMEM((length, LANES), f32),
            pltpu.VMEM((length, LANES), f32),
            pltpu.VMEM((length, LANES), f32),
            pltpu.VMEM((length, LANES), f32),
            pltpu.VMEM((length, LANES), f32),
            pltpu.VMEM((length + 8, conv_width), f32),
        ],
        compiler_params=pltpu.CompilerParams(vmem_limit_bytes=48 * 1024 * 1024),
        cost_estimate=pl.CostEstimate(flops=3 * 10**9, bytes_accessed=6 * 10**6, transcendentals=10**6),
        name="mixer_backward",
    )(proj, dmix, *side)


def swap(value, distance):
    size = lax.axis_size("row")
    return lax.ppermute(value, "row", [(i, i ^ distance) for i in range(size)])


def row_sum(part):
    if lax.axis_size("row") != 4:
        return lax.psum(part, "row")
    half = part.shape[0] // 2
    parity = lax.axis_index("row") % 2
    away = lax.dynamic_slice_in_dim(part, (1 - parity) * half, half, 0)
    kept = lax.dynamic_slice_in_dim(part, parity * half, half, 0)
    kept = (kept.astype(f32) + swap(away, 1).astype(f32)).astype(bf16)
    kept = (kept.astype(f32) + swap(kept, 2).astype(f32)).astype(bf16)
    other = swap(kept, 1)
    return jnp.where(
        parity == 0,
        jnp.concatenate([kept, other], axis=0),
        jnp.concatenate([other, kept], axis=0),
    )


def transpose_blocks(value):
    rows, cols = lax.axis_size("row"), lax.axis_size("col")
    pairs = [(r * cols + c, c * cols + r) for r in range(rows) for c in range(cols)]
    return lax.ppermute(value, ("row", "col"), pairs)


def whole_features(value):
    return lax.all_gather(transpose_blocks(value), "row", axis=1, tiled=True)


def own_block(value):
    count = value.shape[1] // lax.axis_size("row")
    block = lax.dynamic_slice_in_dim(value, lax.axis_index("row") * count, count, 1)
    return transpose_blocks(block)


def gather_weight(weight):
    return lax.all_gather(weight, "col", axis=0, tiled=True)


def scatter_grad(grad):
    grad = lax.psum_scatter(grad.astype(bf16), "col", scatter_dimension=0, tiled=True)
    return lax.psum(grad, "dp")


def norm(hidden, gain):
    inverse = lax.rsqrt(jnp.mean(hidden * hidden, axis=1, keepdims=True) + epsilon)
    return (hidden * inverse * gain[None, :]).astype(bf16), inverse


def norm_back(hidden, inverse, gain, grad):
    weighted = grad * gain[None, :]
    mean = jnp.mean(weighted * hidden, axis=1, keepdims=True)
    grad_hidden = inverse * weighted - hidden * (inverse * inverse * inverse * mean)
    return grad_hidden, jnp.sum(grad * hidden * inverse, axis=0)


def layer_forward(hidden, params, sizes):
    input_gain, post_gain, in_weight, out_weight, ffn_weight, side = params
    half = (ffn_weight.shape[1]) // 3
    normed, inverse = norm(hidden, input_gain)
    proj = dot(normed, in_weight)
    mixed = mixer_forward(sizes, proj, side)
    middle = hidden + row_sum(dot(mixed, out_weight, NT).astype(bf16)).astype(f32)
    post, post_inverse = norm(middle, post_gain)
    wide = dot(post, ffn_weight[:, : 2 * half])
    gate, upper = wide[:, :half], wide[:, half:]
    active = (jax.nn.silu(gate) * upper).astype(bf16)
    output = middle + row_sum(dot(active, ffn_weight[:, 2 * half :], NT).astype(bf16)).astype(f32)
    return output, (hidden, inverse, normed, proj, mixed, middle, post_inverse, post, wide, active)


def layer_backward(grad, saved, params, sizes):
    input_gain, post_gain, in_weight, out_weight, ffn_weight, side = params
    hidden, inverse, normed, proj, mixed, middle, post_inverse, post, wide, active = saved
    half = (ffn_weight.shape[1]) // 3
    gate, upper = wide[:, :half], wide[:, half:]
    low = grad.astype(bf16)
    dactive = dot(low, ffn_weight[:, 2 * half :])
    lifted = jax.nn.sigmoid(gate)
    dgate = dactive * upper * lifted * (1.0 + gate * (1.0 - lifted))
    dwide = jnp.concatenate([dgate, dactive * gate * lifted], axis=1).astype(bf16)
    dpost = row_sum(dot(dwide, ffn_weight[:, : 2 * half], NT).astype(bf16)).astype(f32)
    ffn_grad = scatter_grad(
        jnp.concatenate([dot(post, dwide, TN), dot(low, active, TN)], axis=1)
    )
    dmiddle, post_gain_grad = norm_back(middle, post_inverse, post_gain, dpost)
    dmiddle = dmiddle + grad
    low = dmiddle.astype(bf16)
    dmix = dot(low, out_weight)
    out_grad = scatter_grad(dot(low, mixed, TN))
    dproj, dtaps, dheads = mixer_backward(sizes, proj, dmix, side)
    dnormed = row_sum(dot(dproj, in_weight, NT).astype(bf16)).astype(f32)
    in_grad = scatter_grad(dot(normed, dproj, TN))
    dhidden, input_gain_grad = norm_back(hidden, inverse, input_gain, dnormed)
    return dmiddle + dhidden, (
        ffn_grad,
        out_grad,
        in_grad,
        dtaps,
        dheads,
        input_gain_grad,
        post_gain_grad,
    )


def shards(
    hidden_in,
    segments,
    cotangent,
    input_gain,
    query_weight,
    keyval_weight,
    mixer_gate_weight,
    mixer_input_weight,
    state_weight,
    step_weight,
    conv_values,
    conv_shared,
    step_bias,
    decay_log,
    skip_gain,
    attention_out,
    mixer_out,
    post_gain,
    gate_weight,
    up_weight,
    down_weight,
):
    tokens = hidden_in.shape[0]
    row_index = lax.axis_index("row")
    col_index = lax.axis_index("col")
    query_cols = query_weight.shape[2]
    gate_cols = mixer_gate_weight.shape[2]
    input_cols = mixer_input_weight.shape[2]
    state_cols = state_weight.shape[2]
    heads_row = step_bias.shape[1]
    sizes = [0]
    for count in (query_cols, gate_cols, input_cols, state_cols, 2 * HEAD):
        sizes.append(sizes[-1] + count)
    sizes = tuple(sizes)
    kv_index = row_index * (query_cols // HEAD) // (HEADS // KV_HEADS)
    key_first = kv_index * HEAD
    value_first = KV_HEADS * HEAD + kv_index * HEAD
    step_first = row_index * heads_row

    in_local = jnp.concatenate(
        [
            query_weight,
            mixer_gate_weight,
            mixer_input_weight,
            state_weight,
            lax.dynamic_slice_in_dim(keyval_weight, key_first, HEAD, 2),
            lax.dynamic_slice_in_dim(keyval_weight, value_first, HEAD, 2),
            lax.dynamic_slice_in_dim(step_weight, step_first, heads_row, 2),
            jnp.zeros(step_weight.shape[:2] + (LANES - heads_row,), bf16),
        ],
        axis=2,
    )
    out_local = jnp.swapaxes(jnp.concatenate([attention_out, mixer_out], axis=1), 1, 2)
    ffn_local = jnp.concatenate([gate_weight, up_weight, jnp.swapaxes(down_weight, 1, 2)], axis=2)

    segment_ids = lax.dynamic_slice_in_dim(segments, col_index * tokens, tokens, 0)
    links = [jnp.ones((tokens,), f32)]
    for offset in range(1, 4):
        earlier = jnp.concatenate([jnp.full((offset,), -1, jnp.int32), segment_ids[:-offset]])
        links.append((earlier == segment_ids).astype(f32))
    links = jnp.pad(jnp.stack(links, axis=1), ((0, 8), (0, 4)))
    spread = (
        lax.broadcasted_iota(jnp.int32, (LANES, heads_row * M_HEAD), 0)
        == lax.broadcasted_iota(jnp.int32, (LANES, heads_row * M_HEAD), 1) // M_HEAD
    ).astype(f32)

    params = []
    for layer in range(LAYERS):
        heads = jnp.stack([step_bias[layer], jnp.exp(decay_log[layer])])
        side = (
            segment_ids[:, None],
            segment_ids[None, :],
            links,
            jnp.pad(
                jnp.concatenate([conv_values[layer], conv_shared[layer]], axis=1), ((0, 4), (0, 0))
            ),
            jnp.pad(heads, ((0, 6), (0, LANES - heads_row))),
            jnp.repeat(skip_gain[layer], M_HEAD)[None, :],
            spread,
        )
        params.append(
            (
                lax.all_gather(input_gain[layer], "col", axis=0, tiled=True),
                lax.all_gather(post_gain[layer], "col", axis=0, tiled=True),
                gather_weight(in_local[layer]),
                gather_weight(out_local[layer]),
                gather_weight(ffn_local[layer]),
                side,
            )
        )

    hidden = whole_features(hidden_in).astype(f32)
    grad = whole_features(cotangent).astype(f32)
    stored = []
    for layer in range(LAYERS):
        hidden, saved = layer_forward(hidden, params[layer], sizes)
        stored.append(saved)
    hidden_out = own_block(hidden.astype(bf16))
    collected = [None] * LAYERS
    for layer in reversed(range(LAYERS)):
        grad, collected[layer] = layer_backward(grad, stored[layer], params[layer], sizes)
    hidden_grad = own_block(grad)

    ffn_grad, out_grad, in_grad, dtaps, dheads, input_gain_grad, post_gain_grad = (
        jnp.stack([entry[member] for entry in collected]) for member in range(7)
    )
    first = sizes[3]
    states_part = in_grad[:, :, sizes[3] : sizes[4]].astype(f32)
    key_part = in_grad[:, :, sizes[4] : sizes[4] + HEAD].astype(f32)
    value_part = in_grad[:, :, sizes[4] + HEAD : sizes[5]].astype(f32)
    steps_part = in_grad[:, :, sizes[5] : sizes[5] + heads_row].astype(f32)
    keyval_part = jnp.zeros(keyval_weight.shape, f32)
    keyval_part = lax.dynamic_update_slice_in_dim(keyval_part, key_part, key_first, 2)
    keyval_part = lax.dynamic_update_slice_in_dim(keyval_part, value_part, value_first, 2)
    step_part = lax.dynamic_update_slice_in_dim(
        jnp.zeros(step_weight.shape, f32), steps_part, step_first, 2
    )
    shared_grad = lax.psum(
        jnp.concatenate([keyval_part, states_part, step_part], axis=2).astype(bf16), "row"
    ).astype(f32)
    kv_cols = keyval_weight.shape[2]
    dtaps, dheads, input_gain_grad, post_gain_grad = lax.psum(
        (dtaps, dheads, input_gain_grad, post_gain_grad), ("dp", "col")
    )
    conv_shared_grad = lax.psum(dtaps[:, :4, input_cols:], "row")
    features = hidden_in.shape[1]

    def own_gain(value):
        return lax.dynamic_slice_in_dim(value, col_index * features, features, 1)

    half = gate_weight.shape[2]
    attn_rows = attention_out.shape[1]
    out_grad = jnp.swapaxes(out_grad.astype(f32), 1, 2)
    return (
        hidden_out,
        hidden_grad,
        own_gain(input_gain_grad),
        in_grad[:, :, :query_cols].astype(f32),
        shared_grad[:, :, :kv_cols],
        in_grad[:, :, sizes[1] : sizes[2]].astype(f32),
        in_grad[:, :, sizes[2] : sizes[3]].astype(f32),
        shared_grad[:, :, kv_cols : kv_cols + state_cols],
        shared_grad[:, :, kv_cols + state_cols :],
        dtaps[:, :4, :input_cols],
        conv_shared_grad,
        dheads[:, 0, :heads_row],
        dheads[:, 1, :heads_row],
        dheads[:, 2, :heads_row],
        out_grad[:, :attn_rows, :],
        out_grad[:, attn_rows:, :],
        own_gain(post_gain_grad),
        ffn_grad[:, :, :half].astype(f32),
        ffn_grad[:, :, half : 2 * half].astype(f32),
        jnp.swapaxes(ffn_grad[:, :, 2 * half :].astype(f32), 1, 2),
    )


def solution(mesh):
    placed = (
        P(("dp", "row"), "col"),
        P("dp"),
        P(("dp", "row"), "col"),
        P(None, "col"),
        P(None, "col", "row"),
        P(None, "col", None),
        P(None, "col", "row"),
        P(None, "col", "row"),
        P(None, "col", None),
        P(None, "col", None),
        P(None, None, "row"),
        P(),
        P(None, "row"),
        P(None, "row"),
        P(None, "row"),
        P(None, "row", "col"),
        P(None, "row", "col"),
        P(None, "col"),
        P(None, "col", "row"),
        P(None, "col", "row"),
        P(None, "row", "col"),
    )
    return jax.shard_map(
        shards,
        mesh=mesh,
        in_specs=placed,
        out_specs=(
            P(("dp", "row"), "col"),
            P(("dp", "row"), "col"),
            P(None, "col"),
            P(None, "col", "row"),
            P(None, "col", None),
            P(None, "col", "row"),
            P(None, "col", "row"),
            P(None, "col", None),
            P(None, "col", None),
            P(None, None, "row"),
            P(),
            P(None, "row"),
            P(None, "row"),
            P(None, "row"),
            P(None, "row", "col"),
            P(None, "row", "col"),
            P(None, "col"),
            P(None, "col", "row"),
            P(None, "col", "row"),
            P(None, "row", "col"),
        ),
        check_vma=False,
    )
```

time: 2960 us -> 957 us (0.32)
  waiting for transfers between devices: 1960 us -> 633 us
  local copies, waits for them, and re-layouts: 292 us -> 45.4 us
  matrix products: 247 us -> 64.4 us
  other arithmetic: 208 us -> 52.1 us
  blocking collectives: 195 us -> 81.6 us
  Pallas kernels: 0 us -> 39.8 us
    reduce_scatter x16 -> x6, waiting for transfers between devices: 1180 us -> 159 us  [scatter_grad(): lax.psum_scatter(grad.astype(bf16), 'col', scatter_dimension=0, tiled=True)]
    all_gather x16 -> x8, waiting for transfers between devices: 665 us -> 176 us  [the longest x6 162 us: gather_weight(): return lax.all_gather(weight, 'col', axis=0, tiled=True)]
    psum x12 -> x1, blocking collectives: 195 us -> 6.57 us  [shards(): conv_shared_grad = lax.psum(dtaps[:, :4, input_cols:], 'row')]
    dot_general x152 -> x24, matrix products: 247 us -> 64.4 us  [dot(): lax.dot_general(left, right, dims, precision=precision, preferred_element...]
    ppermute x0 -> x28, waiting for transfers between devices: none -> 124 us  [the longest x24 124 us: swap(): return lax.ppermute(value, 'row', [(i, i ^ distance) for i in range(size)])]
    dynamic_update_slice x18 -> x3, local copies, waits for them, and re-layouts: 95.7 us -> 1.33 us  [the longest x1 0.5 us: shards(): lax.dynamic_update_slice_in_dim(keyval_part, key_part, key_first, 2)]
    all_gather x0 -> x4, blocking collectives: none -> 75 us  [the longest x2 42.7 us: shards(): lax.all_gather(post_gain[layer], 'col', axis=0, tiled=True)]
    psum x1 -> x3, waiting for transfers between devices: 121 us -> 174 us  [the longest x1 85.3 us: scatter_grad(): return lax.psum(grad, 'dp')]
  transfers between devices with their start and end apart: 33 -> 45, of which waited for: 32 -> 33; matrix products, arithmetic and copies ran while one was open for 2% -> 13% of each run, Pallas kernels for 0% -> 4%
where the time goes in v1:
time: 957 us; the launch traced here: 948 us
  waiting for transfers between devices  633 us (66%)
  blocking collectives  81.6 us (9%)
  matrix products  64.4 us (7%)
  other arithmetic  52.1 us (5%)
  local copies, waits for them, and re-layouts  45.4 us (5%)
  Pallas kernels  39.8 us (4%)
  starting transfers between devices  16 us (2%)
  between operations  15.8 us (2%)
    all_gather x6, waiting for transfers between devices, gather_weight(): return lax.all_gather(weight, 'col', axis=0, tiled=True)  162 us
    reduce_scatter x6, waiting for transfers between devices, scatter_grad(): lax.psum_scatter(grad.astype(bf16), 'col', scatter_dimension=0, tiled=True)  159 us
    ppermute x24, waiting for transfers between devices, swap(): return lax.ppermute(value, 'row', [(i, i ^ distance) for i in range(size)])  124 us
    psum x1, waiting for transfers between devices, scatter_grad(): return lax.psum(grad, 'dp')  85.3 us
    dot_general x24, matrix products, dot(): lax.dot_general(left, right, dims, precision=precision, preferred_element...  64.4 us
    psum x1, waiting for transfers between devices, shards(): lax.psum((dtaps, dheads, input_gain_grad, post_gain_grad), ('dp', 'col'))  60.6 us
    all_gather x2, blocking collectives, shards(): lax.all_gather(post_gain[layer], 'col', axis=0, tiled=True)  42.7 us
    all_gather x2, blocking collectives, shards(): lax.all_gather(input_gain[layer], 'col', axis=0, tiled=True)  32.3 us
  transfers between devices with their start and end apart: 45, of which 33 were waited for; matrix products, arithmetic and copies ran while one was open for 13% of the time, Pallas kernels for 4%

profile of v1, /device:TPU:0, one launch (start us, length us, event | category | flops | bytes accessed | tf_op | source)
XLA Modules:
  0.0 948.3 jit_solution(4233181026498088876)
XLA Ops:
  18.4 24.1 %all-gather = f32[1,1024]{1,0:T(1,128)S(1)} all-gather(f32[1,256]{1,0:T(1,128)S(1)} %get-tuple-element.145), channel_id=2, replica_groups=mesh['dp'=2,'row'=4,'col'=4] {'col'}, dimensions={1}, use_global_device_ids=true | all-gather | bytes 5120 | tf_op jit(solution)/shard_map/all_gather | solution.py:583
  45.5 59.2 %all-gather.23.cloned.1.call-done = bf16[1,1024,1408]{2,1,0:T(8,128)(2,1)} async-done(((bf16[1,256,1408]{2,1,0:T(8,128)(2,1)}), bf16[1,1024,1408]{2,1,0:T(8,128)(2,1)}) %all-gather.23.cloned.1.call-update) | async-done | bytes 2883600 | tf_op jit(solution)/shard_map/all_gather | solution.py:431
  108.8 5.2 mixer_forward.2
  114.8 21.0 %all-gather.25.cloned.1.call-done = bf16[1,1024,512]{1,2,0:T(8,128)(2,1)} async-done(((bf16[1,256,512]{1,2,0:T(8,128)(2,1)}), bf16[1,1024,512]{1,2,0:T(8,128)(2,1)}) %all-gather.25.cloned.1.call-update) | async-done | bytes 1048592 | tf_op jit(solution)/shard_map/all_gather | solution.py:431
  143.8 13.6 %collective-permute-done.2 = bf16[256,1024]{1,0:T(8,128)(2,1)S(1)} collective-permute-done((bf16[256,1024]{1,0:T(8,128)(2,1)S(1)}, bf16[256,1024]{1,0:T(8,128)(2,1)S(1)}, u32[]{:S(2)}, u32[]{:S(2)}) %collective-permute-start.2) | collective-permute-done | bytes 524320 | tf_op jit(solution)/shard_map/ppermute | solution.py:394
  158.5 10.7 %all-gather.3 = f32[1,1024]{1,0:T(1,128)S(1)} all-gather(f32[1,256]{1,0:T(1,128)S(1)} %get-tuple-element.143), channel_id=5, replica_groups=mesh['dp'=2,'row'=4,'col'=4] {'col'}, dimensions={1}, use_global_device_ids=true | all-gather | bytes 5120 | tf_op jit(solution)/shard_map/all_gather | solution.py:584
  171.8 27.8 %all-gather.27.cloned.1.call-done = bf16[1,1024,1536]{1,2,0:T(8,128)(2,1)} async-done(((bf16[1,256,1536]{1,2,0:T(8,128)(2,1)}), bf16[1,1024,1536]{1,2,0:T(8,128)(2,1)}) %all-gather.27.cloned.1.call-update) | async-done | bytes 3145744 | tf_op jit(solution)/shard_map/all_gather | solution.py:431
  213.2 12.5 %collective-permute-done.5 = bf16[256,1024]{1,0:T(8,128)(2,1)S(1)} collective-permute-done((bf16[256,1024]{1,0:T(8,128)(2,1)S(1)}, bf16[256,1024]{1,0:T(8,128)(2,1)S(1)}, u32[]{:S(2)}, u32[]{:S(2)}) %collective-permute-start.5) | collective-permute-done | bytes 524320 | tf_op jit(solution)/shard_map/ppermute | solution.py:394
  226.8 8.2 all-gather.5
  239.7 19.3 %all-gather.29.cloned.1.call-done = bf16[1,1024,1408]{2,1,0:T(8,128)(2,1)} async-done(((bf16[1,256,1408]{2,1,0:T(8,128)(2,1)}), bf16[1,1024,1408]{2,1,0:T(8,128)(2,1)}) %all-gather.29.cloned.1.call-update) | async-done | bytes 2883600 | tf_op jit(solution)/shard_map/all_gather | solution.py:431
  263.4 5.3 mixer_forward.3
  270.9 19.0 %all-gather.31.cloned.1.call-done = bf16[1,1024,512]{1,2,0:T(8,128)(2,1)} async-done(((bf16[1,256,512]{1,2,0:T(8,128)(2,1)}), bf16[1,1024,512]{1,2,0:T(8,128)(2,1)}) %all-gather.31.cloned.1.call-update) | async-done | bytes 1048592 | tf_op jit(solution)/shard_map/all_gather | solution.py:431
  297.0 12.4 %collective-permute-done.8 = bf16[256,1024]{1,0:T(8,128)(2,1)} collective-permute-done((bf16[256,1024]{1,0:T(8,128)(2,1)}, bf16[256,1024]{1,0:T(8,128)(2,1)}, u32[]{:S(2)}, u32[]{:S(2)}) %collective-permute-start.8) | collective-permute-done | bytes 524320 | tf_op jit(solution)/shard_map/ppermute | solution.py:394
  314.1 32.0 %all-gather.8 = f32[1,1024]{1,0:T(1,128)S(1)} all-gather(f32[1,256]{1,0:T(1,128)S(1)} %get-tuple-element.142), channel_id=10, replica_groups=mesh['dp'=2,'row'=4,'col'=4] {'col'}, dimensions={1}, use_global_device_ids=true | all-gather | bytes 5120 | tf_op jit(solution)/shard_map/all_gather | solution.py:584
  349.4 15.7 %all-gather.33.cloned.1.call-done = bf16[1,1024,1536]{1,2,0:T(8,128)(2,1)} async-done(((bf16[1,256,1536]{1,2,0:T(8,128)(2,1)}), bf16[1,1024,1536]{1,2,0:T(8,128)(2,1)}) %all-gather.33.cloned.1.call-update) | async-done | bytes 3145744 | tf_op jit(solution)/shard_map/all_gather | solution.py:431
  365.1 4.9 fusion.37
  370.0 13.6 %all-gather.21.cloned.1.call-done = bf16[512,1024]{1,0:T(8,128)(2,1)} async-done(((bf16[512,256]{1,0:T(8,128)(2,1)}), bf16[512,1024]{1,0:T(8,128)(2,1)}) %all-gather.21.cloned.1.call-update) | async-done | bytes 1048592 | tf_op jit(solution)/shard_map/all_gather | solution.py:421
  391.8 13.8 %collective-permute-done.16 = bf16[256,1024]{1,0:T(8,128)(2,1)S(1)} collective-permute-done((bf16[256,1024]{1,0:T(8,128)(2,1)S(1)}, bf16[256,1024]{1,0:T(8,128)(2,1)S(1)}, u32[]{:S(2)}, u32[]{:S(2)}) %collective-permute-start.16) | collective-permute-done | bytes 524320 | tf_op jit(solution)/shard_map/ppermute | solution.py:394
  415.2 14.8 %mixer_backward.2 = (bf16[512,1408]{1,0:T(8,128)(2,1)S(1)}, f32[8,640]{1,0:T(8,128)S(1)}, f32[8,128]{1,0:T(8,128)S(1)}) custom-call(f32[512,1408]{1,0:T(8,128)S(1)} %copy-done.3, f32[512,512]{1,0:T(8,128)S(1)} %fusion.56.dmix_ref, s32[512,1]{1,0:T(8,128)S(1)} %copy.72.segc_ref, s32[1,512]{1,0:T(1,128)S(1)} %bitcast.99, f32[520,8]{1,0:T(8,128)S(1)} %pad.20.link_ref, ...), custom_call_target="tpu_custom_call" | custom-call | flops 3000000000 | bytes 6000000 | tf_op jit(solution)/shard_map/mixer_backward/pallas_call | solution.py:367
  438.2 11.1 %collective-permute-done.19 = bf16[256,1024]{1,0:T(8,128)(2,1)} collective-permute-done((bf16[256,1024]{1,0:T(8,128)(2,1)}, bf16[256,1024]{1,0:T(8,128)(2,1)}, u32[]{:S(2)}, u32[]{:S(2)}) %collective-permute-start.19) | collective-permute-done | bytes 524320 | tf_op jit(solution)/shard_map/ppermute | solution.py:394
  462.6 13.7 %collective-permute-done.22 = bf16[256,1024]{1,0:T(8,128)(2,1)S(1)} collective-permute-done((bf16[256,1024]{1,0:T(8,128)(2,1)S(1)}, bf16[256,1024]{1,0:T(8,128)(2,1)S(1)}, u32[]{:S(2)}, u32[]{:S(2)}) %collective-permute-start.22) | collective-permute-done | bytes 524320 | tf_op jit(solution)/shard_map/ppermute | solution.py:394
  486.6 5.5 convolution_convert_fusion
  502.9 14.5 %mixer_backward.3 = (bf16[512,1408]{1,0:T(8,128)(2,1)S(1)}, f32[8,640]{1,0:T(8,128)S(1)}, f32[8,128]{1,0:T(8,128)S(1)}) custom-call(f32[512,1408]{1,0:T(8,128)S(1)} %fusion.6.proj_ref, f32[512,512]{1,0:T(8,128)S(1)} %fusion.59.dmix_ref, s32[512,1]{1,0:T(8,128)S(1)} %copy.72.segc_ref, s32[1,512]{1,0:T(1,128)S(1)} %bitcast.100, f32[520,8]{1,0:T(8,128)S(1)} %pad.20.link_ref, ...), custom_call_target="tpu_custom_call" | custom-call | flops 3000000000 | bytes 6000000 | tf_op jit(solution)/shard_map/mixer_backward/pallas_call | solution.py:367
  530.4 13.1 %collective-permute-done.25 = bf16[256,1024]{1,0:T(8,128)(2,1)S(1)} collective-permute-done((bf16[256,1024]{1,0:T(8,128)(2,1)S(1)}, bf16[256,1024]{1,0:T(8,128)(2,1)S(1)}, u32[]{:S(2)}, u32[]{:S(2)}) %collective-permute-start.25) | collective-permute-done | bytes 524320 | tf_op jit(solution)/shard_map/ppermute | solution.py:394
  549.6 38.5 %reduce-scatter.9.cloned.1.call-done = bf16[256,1408]{1,0:T(8,128)(2,1)} async-done(((bf16[1024,1408]{1,0:T(8,128)(2,1)}), bf16[256,1408]{1,0:T(8,128)(2,1)}) %reduce-scatter.9.cloned.1.call-update) | async-done | bytes 720912 | tf_op jit(solution)/shard_map/reduce_scatter | solution.py:435
  588.0 62.4 %reduce-scatter.15.cloned.1.call-done = bf16[256,1536]{0,1:T(8,128)(2,1)} async-done(((bf16[1024,1536]{0,1:T(8,128)(2,1)}), bf16[256,1536]{0,1:T(8,128)(2,1)}) %reduce-scatter.15.cloned.1.call-update) | async-done | bytes 786448 | tf_op jit(solution)/shard_map/reduce_scatter | solution.py:435
  650.5 58.4 %reduce-scatter.7.cloned.1.call-done = bf16[256,1408]{1,0:T(8,128)(2,1)} async-done(((bf16[1024,1408]{1,0:T(8,128)(2,1)}), bf16[256,1408]{1,0:T(8,128)(2,1)}) %reduce-scatter.7.cloned.1.call-update) | async-done | bytes 720912 | tf_op jit(solution)/shard_map/reduce_scatter | solution.py:435
  714.8 12.5 %collective-permute-done.11 = bf16[256,1024]{1,0:T(8,128)(2,1)S(1)} collective-permute-done((bf16[256,1024]{1,0:T(8,128)(2,1)S(1)}, bf16[256,1024]{1,0:T(8,128)(2,1)S(1)}, u32[]{:S(2)}, u32[]{:S(2)}) %collective-permute-start.11) | collective-permute-done | bytes 524320 | tf_op jit(solution)/shard_map/ppermute | solution.py:394
  735.2 60.6 %all-reduce.15.cloned.1.call-done = (f32[2,1024]{1,0:T(2,128)}, f32[2,8,640]{2,1,0:T(8,128)}, f32[2,8,128]{2,1,0:T(8,128)}, f32[2,1024]{1,0:T(2,128)}) async-done(((f32[2,1024]{1,0:T(2,128)}, f32[2,8,640]{2,1,0:T(8,128)}, f32[2,8,128]{2,1,0:T(8,128)}, f32[2,1024]{1,0:T(2,128)}), (f32[2,1024]{1,0:T(2,128)}, f32[2,8,640]{2,1,0:T(8,128)}, f32[2,8,128]{2,1,0:T(8,128)}, ...) | async-done | bytes 65552 | tf_op jit(solution)/shard_map/psum | solution.py:622
  797.9 6.6 psum.89
  808.3 85.3 %all-reduce.17.cloned.1.call-done = (bf16[1,256,1408]{2,1,0:T(8,128)(2,1)}, bf16[1,256,1408]{2,1,0:T(8,128)(2,1)}, bf16[1,256,512]{2,1,0:T(8,128)(2,1)}, bf16[1,...) async-done(((bf16[1,256,1408]{2,1,0:T(8,128)(2,1)}, bf16[1,256,1408]{2,1,0:T(8,128)(2,1)}, bf16[1,256,512]{2,1,0:T(8,128)(2,1)}, ...) | async-done | bytes 3538960 | tf_op jit(solution)/shard_map/psum | solution.py:436
  907.4 27.8 %all-reduce.13.cloned.1.call-done = bf16[2,256,536]{2,1,0:T(8,128)(2,1)} async-done(((bf16[2,256,536]{2,1,0:T(8,128)(2,1)}), bf16[2,256,536]{2,1,0:T(8,128)(2,1)}) %all-reduce.13.cloned.1.call-update) | async-done | bytes 548880 | tf_op jit(solution)/shard_map/psum | solution.py:618
  (375 shorter events, 189.6 us)
Async XLA Ops:
  7.2 36.8 %all-gather.19.cloned.1.call-start = ((), (), s32[]{:S(2)}) async-start(), calls=%async_computation.6 | async-start | bytes 1310720 | tf_op jit(solution)/shard_map/all_gather | solution.py:421
  9.6 95.1 %all-gather.23.cloned.1.call-start = ((), (), s32[]{:S(2)}) async-start(), calls=%async_computation.15 | async-start | bytes 3604480 | tf_op jit(solution)/shard_map/all_gather | solution.py:431
  14.7 121.1 %all-gather.25.cloned.1.call-start = ((), (), s32[]{:S(2)}) async-start(), calls=%async_computation.16 | async-start | bytes 1310720 | tf_op jit(solution)/shard_map/all_gather | solution.py:431
  15.6 183.9 %all-gather.27.cloned.1.call-start = ((), (), s32[]{:S(2)}) async-start(), calls=%async_computation.17 | async-start | bytes 3932160 | tf_op jit(solution)/shard_map/all_gather | solution.py:431
  17.7 241.3 %all-gather.29.cloned.1.call-start = ((), (), s32[]{:S(2)}) async-start(), calls=%async_computation.18 | async-start | bytes 3604480 | tf_op jit(solution)/shard_map/all_gather | solution.py:431
  18.2 271.7 %all-gather.31.cloned.1.call-start = ((), (), s32[]{:S(2)}) async-start(), calls=%async_computation.19 | async-start | bytes 1310720 | tf_op jit(solution)/shard_map/all_gather | solution.py:431
  139.7 2.3 collective-permute-start.1
  143.4 14.0 %collective-permute-start.2 = (bf16[256,1024]{1,0:T(8,128)(2,1)S(1)}, bf16[256,1024]{1,0:T(8,128)(2,1)S(1)}, u32[]{:S(2)}, u32[]{:S(2)}) collective-permute-start(bf16[256,1024]{1,0:T(8,128)(2,1)S(1)} %add_convert_fusion.15), channel_id=1, source_target_pairs={{0,8},{4,12},{8,0},{12,4},{1,9},{5,13},{9,1},{13,5},{2,10},{6,14},... | collective-permute-start | bytes 1572872 | tf_op jit(solution)/shard_map/ppermute | solution.py:394
  158.4 10.8 %collective-permute-start.3 = (bf16[256,1024]{1,0:T(8,128)(2,1)}, bf16[256,1024]{1,0:T(8,128)(2,1)}, u32[]{:S(2)}, u32[]{:S(2)}) collective-permute-start(bf16[256,1024]{1,0:T(8,128)(2,1)} %add_convert_fusion.14), channel_id=1, source_target_pairs={{0,4},{4,0},{8,12},{12,8},{1,5},{5,1},{9,13},{13,9},{2,6},{6,2},{1... | collective-permute-start | bytes 1572872 | tf_op jit(solution)/shard_map/ppermute | solution.py:394
  158.4 206.7 %all-gather.33.cloned.1.call-start = ((), (), s32[]{:S(2)}) async-start(), calls=%async_computation.20 | async-start | bytes 3932160 | tf_op jit(solution)/shard_map/all_gather | solution.py:431
  208.0 175.7 %all-gather.21.cloned.1.call-start = ((), (), s32[]{:S(2)}) async-start(), calls=%async_computation.7 | async-start | bytes 1310720 | tf_op jit(solution)/shard_map/all_gather | solution.py:421
  211.6 14.0 %collective-permute-start.5 = (bf16[256,1024]{1,0:T(8,128)(2,1)S(1)}, bf16[256,1024]{1,0:T(8,128)(2,1)S(1)}, u32[]{:S(2)}, u32[]{:S(2)}) collective-permute-start(bf16[256,1024]{1,0:T(8,128)(2,1)S(1)} %add_convert_fusion.13), channel_id=1, source_target_pairs={{0,8},{4,12},{8,0},{12,4},{1,9},{5,13},{9,1},{13,5},{2,10},{6,14},... | collective-permute-start | bytes 1572872 | tf_op jit(solution)/shard_map/ppermute | solution.py:394
  226.7 8.4 collective-permute-start.6
  295.1 14.3 %collective-permute-start.8 = (bf16[256,1024]{1,0:T(8,128)(2,1)}, bf16[256,1024]{1,0:T(8,128)(2,1)}, u32[]{:S(2)}, u32[]{:S(2)}) collective-permute-start(bf16[256,1024]{1,0:T(8,128)(2,1)} %add_convert_fusion.11), channel_id=1, source_target_pairs={{0,8},{4,12},{8,0},{12,4},{1,9},{5,13},{9,1},{13,5},{2,10},{6,14},... | collective-permute-start | bytes 1572872 | tf_op jit(solution)/shard_map/ppermute | solution.py:394
  296.9 252.6 %reduce-scatter.13.cloned.1.call-start = ((), (), s32[]{:S(2)}) async-start(), calls=%async_computation.12 | async-start | bytes 1310720 | tf_op jit(solution)/shard_map/reduce_scatter | solution.py:435
  310.8 35.3 %collective-permute-start.9 = (bf16[256,1024]{1,0:T(8,128)(2,1)S(1)}, bf16[256,1024]{1,0:T(8,128)(2,1)S(1)}, u32[]{:S(2)}, u32[]{:S(2)}) collective-permute-start(bf16[256,1024]{1,0:T(8,128)(2,1)S(1)} %add_convert_fusion.10), channel_id=1, source_target_pairs={{0,4},{4,0},{8,12},{12,8},{1,5},{5,1},{9,13},{13,9},{2,6},{6,2},{1... | collective-permute-start | bytes 1572872 | tf_op jit(solution)/shard_map/ppermute | solution.py:394
  391.4 14.1 %collective-permute-start.16 = (bf16[256,1024]{1,0:T(8,128)(2,1)S(1)}, bf16[256,1024]{1,0:T(8,128)(2,1)S(1)}, u32[]{:S(2)}, u32[]{:S(2)}) collective-permute-start(bf16[256,1024]{1,0:T(8,128)(2,1)S(1)} %add_convert_fusion.7), channel_id=1, source_target_pairs={{0,8},{4,12},{8,0},{12,4},{1,9},{5,13},{9,1},{13,5},{2,10},{6,14},... | collective-permute-start | bytes 1572872 | tf_op jit(solution)/shard_map/ppermute | solution.py:394
  412.3 137.2 %reduce-scatter.17.cloned.1.call-start = ((), (), s32[]{:S(2)}) async-start(), calls=%async_computation.14 | async-start | bytes 3932160 | tf_op jit(solution)/shard_map/reduce_scatter | solution.py:435
  435.0 14.3 %collective-permute-start.19 = (bf16[256,1024]{1,0:T(8,128)(2,1)}, bf16[256,1024]{1,0:T(8,128)(2,1)}, u32[]{:S(2)}, u32[]{:S(2)}) collective-permute-start(bf16[256,1024]{1,0:T(8,128)(2,1)} %add_convert_fusion.5), channel_id=1, source_target_pairs={{0,8},{4,12},{8,0},{12,4},{1,9},{5,13},{9,1},{13,5},{2,10},{6,14},... | collective-permute-start | bytes 1572872 | tf_op jit(solution)/shard_map/ppermute | solution.py:394
  438.1 111.5 %reduce-scatter.11.cloned.1.call-start = ((), (), s32[]{:S(2)}) async-start(), calls=%async_computation.11 | async-start | bytes 1310720 | tf_op jit(solution)/shard_map/reduce_scatter | solution.py:435
  462.2 14.1 %collective-permute-start.22 = (bf16[256,1024]{1,0:T(8,128)(2,1)S(1)}, bf16[256,1024]{1,0:T(8,128)(2,1)S(1)}, u32[]{:S(2)}, u32[]{:S(2)}) collective-permute-start(bf16[256,1024]{1,0:T(8,128)(2,1)S(1)} %add_convert_fusion.3), channel_id=1, source_target_pairs={{0,8},{4,12},{8,0},{12,4},{1,9},{5,13},{9,1},{13,5},{2,10},{6,14},... | collective-permute-start | bytes 1572872 | tf_op jit(solution)/shard_map/ppermute | solution.py:394
  486.6 101.5 %reduce-scatter.9.cloned.1.call-start = ((), (), s32[]{:S(2)}) async-start(), calls=%async_computation.9 | async-start | bytes 3604480 | tf_op jit(solution)/shard_map/reduce_scatter | solution.py:435
  492.2 158.3 %reduce-scatter.15.cloned.1.call-start = ((), (), s32[]{:S(2)}) async-start(), calls=%async_computation.13 | async-start | bytes 3932160 | tf_op jit(solution)/shard_map/reduce_scatter | solution.py:435
  500.0 208.9 %reduce-scatter.7.cloned.1.call-start = ((), (), s32[]{:S(2)}) async-start(), calls=%async_computation.8 | async-start | bytes 3604480 | tf_op jit(solution)/shard_map/reduce_scatter | solution.py:435
  522.2 273.7 %all-reduce.15.cloned.1.call-start = ((), (), s32[]{:S(2)}) async-start(), calls=%async_computation.21 | async-start | bytes 131072 | tf_op jit(solution)/shard_map/psum | solution.py:622
  529.5 14.0 %collective-permute-start.25 = (bf16[256,1024]{1,0:T(8,128)(2,1)S(1)}, bf16[256,1024]{1,0:T(8,128)(2,1)S(1)}, u32[]{:S(2)}, u32[]{:S(2)}) collective-permute-start(bf16[256,1024]{1,0:T(8,128)(2,1)S(1)} %add_convert_fusion.1), channel_id=1, source_target_pairs={{0,8},{4,12},{8,0},{12,4},{1,9},{5,13},{9,1},{13,5},{2,10},{6,14},... | collective-permute-start | bytes 1572872 | tf_op jit(solution)/shard_map/ppermute | solution.py:394
  543.7 4.2 collective-permute-start.26
  549.5 344.1 %all-reduce.17.cloned.1.call-start = ((), (), s32[]{:S(2)}) async-start(), calls=%async_computation.22 | async-start | bytes 7077888 | tf_op jit(solution)/shard_map/psum | solution.py:436
  708.9 226.3 %all-reduce.13.cloned.1.call-start = ((), (), s32[]{:S(2)}) async-start(), calls=%async_computation.10 | async-start | bytes 1310720 | tf_op jit(solution)/shard_map/psum | solution.py:618
  713.3 14.0 %collective-permute-start.11 = (bf16[256,1024]{1,0:T(8,128)(2,1)S(1)}, bf16[256,1024]{1,0:T(8,128)(2,1)S(1)}, u32[]{:S(2)}, u32[]{:S(2)}) collective-permute-start(bf16[256,1024]{1,0:T(8,128)(2,1)S(1)} %add_convert_fusion.9), channel_id=1, source_target_pairs={{0,8},{4,12},{8,0},{12,4},{1,9},{5,13},{9,1},{13,5},{2,10},{6,14},... | collective-permute-start | bytes 1572872 | tf_op jit(solution)/shard_map/ppermute | solution.py:394
  731.9 3.4 collective-permute-start.13
  734.5 73.8 %collective-permute-start.27 = (f32[512,256]{1,0:T(8,128)S(1)}, f32[512,256]{1,0:T(8,128)S(1)}, u32[]{:S(2)}, u32[]{:S(2)}) collective-permute-start(f32[512,256]{1,0:T(8,128)S(1)} %dynamic-slice_add_fusion), channel_id=1, source_target_pairs={{0,0},{1,4},{2,8},{3,12},{4,1},{5,5},{6,9},{7,13},{8,2},{9,6},{10,... | collective-permute-start | bytes 1572872 | tf_op jit(solution)/shard_map/ppermute | solution.py:417
  (85 other events, 634.0 us)
Sparse Core Ops, SparseCore 0:
  10.2 33.1 all-gather.18
  45.5 59.1 all-gather.22
  106.8 28.8 all-gather.24
  137.7 61.7 all-gather.26
  201.6 57.3 all-gather.28
  261.0 28.9 all-gather.30
  292.0 73.0 all-gather.32
  366.7 16.9 all-gather.20
  412.5 27.1 reduce-scatter.12
  441.9 58.9 reduce-scatter.16
  503.8 27.1 reduce-scatter.10
  533.2 54.7 reduce-scatter.8
  590.3 60.1 reduce-scatter.14
  652.6 56.1 reduce-scatter.6
  713.1 82.7 all-reduce.14
  798.4 95.1 all-reduce.16
  899.8 35.3 all-reduce.12

commit v2 on v1

--- a/solution.py
+++ b/solution.py
@@ -349,29 +349,554 @@
     ]
 
 
-def mixer_forward(sizes, proj, side):
-    length, width = proj.shape[0], sizes[3] - sizes[2]
+def fetch(plan, refs, target, semaphores):
+    col = lax.axis_index("col")
+    whole = target.shape[0] // 2
+    copies = []
+    for index, (piece, first, rows, half, distance, source, place, count) in enumerate(plan):
+        if isinstance(half, tuple):
+            at = pl.multiple_of((half[0] ^ (lax.axis_index("dp") & 1)) * whole, rows)
+        else:
+            at = half * whole
+        if isinstance(distance, tuple):
+            at = pl.multiple_of(at + distance[0] * rows, rows)
+        elif distance is not None:
+            at = pl.multiple_of(at + (col ^ distance) * rows, rows)
+        copy = pltpu.make_async_copy(
+            refs[piece].at[pl.ds(first, rows), pl.ds(source, count)],
+            target.at[pl.ds(at, rows), pl.ds(place, count)],
+            semaphores.at[index],
+        )
+        copy.start()
+        copies.append(copy)
+    return copies
+
+
+def arrived(copies):
+    for copy in copies:
+        copy.wait()
+
+
+def own_rows(length):
+    half = length // 2
+    parity = lax.axis_index("row") & 1
+    return (
+        pl.ds(pl.multiple_of(parity * half, half), half),
+        pl.ds(pl.multiple_of((1 - parity) * half, half), half),
+    )
+
+
+def by_rows(length, body):
+    def step(index, carry):
+        body(pl.ds(pl.multiple_of(index * ROWS, ROWS), ROWS))
+        return carry
+
+    lax.fori_loop(0, length // ROWS, step, 0)
+
+
+def add_sum(base_ref, sum_refs, total_ref):
+    for rows, part in zip(own_rows(base_ref.shape[0]), sum_refs):
+        total_ref[rows, :] = base_ref[rows, :] + part[...].astype(f32)
+
+
+def norm_rows(hidden_ref, gain_ref, normed_ref):
+    def body(rows):
+        hidden = hidden_ref[rows, :]
+        inverse = lax.rsqrt(jnp.mean(hidden * hidden, axis=1, keepdims=True) + epsilon)
+        normed_ref[rows, :] = (hidden * inverse * gain_ref[...]).astype(bf16)
+
+    by_rows(hidden_ref.shape[0], body)
+
+
+def norm_back_rows(hidden_ref, gain_ref, grad_ref, base_ref, total_ref, low_ref, dgain_ref):
+    dgain_ref[...] = jnp.zeros_like(dgain_ref)
+
+    def body(rows):
+        hidden, grad = hidden_ref[rows, :], grad_ref[rows, :].astype(f32)
+        inverse = lax.rsqrt(jnp.mean(hidden * hidden, axis=1, keepdims=True) + epsilon)
+        weighted = grad * gain_ref[...]
+        mean = jnp.mean(weighted * hidden, axis=1, keepdims=True)
+        total = base_ref[rows, :] + (
+            inverse * weighted - hidden * (inverse * inverse * inverse * mean)
+        )
+        total_ref[rows, :] = total
+        low_ref[rows, :] = total.astype(bf16)
+        dgain_ref[...] += jnp.sum(grad * hidden * inverse, axis=0, keepdims=True)
+
+    by_rows(hidden_ref.shape[0], body)
+
+
+def set_sum(sum_refs, total_ref):
+    for rows, part in zip(own_rows(total_ref.shape[0]), sum_refs):
+        total_ref[rows, :] = part[...]
+
+
+def times(left_ref, weight_ref, first, last, result_ref, place=0, dims=NN):
+    for column in range(first, last, 256):
+        count = min(256, last - column)
+        result_ref[:, place + column - first : place + column - first + count] = dot(
+            left_ref[...], weight_ref[:, column : column + count]
+        ).astype(result_ref.dtype)
+
+
+def parts(left_ref, weight_ref, first, last, kept_ref, away_ref):
+    for rows, part_ref in zip(own_rows(left_ref.shape[0]), (kept_ref, away_ref)):
+        left = left_ref[rows, :]
+        for feature in range(0, weight_ref.shape[0], 256):
+            part_ref[:, feature : feature + 256] = dot(
+                left, weight_ref[feature : feature + 256, first:last], NT
+            ).astype(bf16)
+
+
+def take(refs, *counts):
+    taken = []
+    for count in counts:
+        taken.append(refs[:count])
+        refs = refs[count:]
+    return taken
+
+
+def first_kernel(sizes, plans, counts, *refs):
+    ins, outs, scratch = take(refs, *counts[:3])
+    summed = len(ins) - counts[3] - 9 == 2
+    base_ref, gain_ref = ins[:2]
+    side = ins[2:9]
+    sums, pieces = ins[9 : len(ins) - counts[3]], ins[len(ins) - counts[3] :]
+    hidden_ref, normed_ref, proj_ref, mixed_ref, kept_ref, away_ref = outs
+    in_ref, out_ref, in_sems, out_sems = scratch[:4]
+    waits = fetch(plans[0], pieces, in_ref, in_sems)
+    out_waits = fetch(plans[1], pieces, out_ref, out_sems)
+    if summed:
+        add_sum(base_ref, sums, hidden_ref)
+    else:
+        hidden_ref[...] = base_ref[...].astype(f32)
+    norm_rows(hidden_ref, gain_ref, normed_ref)
+    arrived(waits)
+    times(normed_ref, in_ref, 0, in_ref.shape[1], proj_ref)
+    mixer_forward_kernel(sizes, proj_ref, *side, mixed_ref, *scratch[4:])
+    arrived(out_waits)
+    parts(mixed_ref, out_ref, 0, out_ref.shape[1], kept_ref, away_ref)
+
+
+def second_kernel(plans, counts, *refs):
+    ins, outs, scratch = take(refs, *counts[:3])
+    hidden_ref, gain_ref, kept_sum, other_sum = ins[:4]
+    middle_ref, post_ref, wide_ref, active_ref, kept_ref, away_ref = outs
+    ffn_ref, sems = scratch
+    waits = fetch(plans[0], ins[4:], ffn_ref, sems)
+    add_sum(hidden_ref, (kept_sum, other_sum), middle_ref)
+    norm_rows(middle_ref, gain_ref, post_ref)
+    arrived(waits)
+    half = ffn_ref.shape[1] // 3
+    times(post_ref, ffn_ref, 0, 2 * half, wide_ref)
+
+    def body(rows):
+        gate, upper = wide_ref[rows, :half], wide_ref[rows, half:]
+        active_ref[rows, :] = (gate * jax.nn.sigmoid(gate) * upper).astype(bf16)
+
+    by_rows(wide_ref.shape[0], body)
+    parts(active_ref, ffn_ref, 2 * half, 3 * half, kept_ref, away_ref)
+
+
+def third_kernel(plans, counts, *refs):
+    ins, outs, scratch = take(refs, *counts[:3])
+    ffn_ref, sems, dactive_ref = scratch[:3]
+    wide_ref = ins[0]
+    pieces = ins[len(ins) - counts[3] :]
+    waits = fetch(plans[0], pieces, ffn_ref, sems)
+    low_ref, dwide_ref, kept_ref, away_ref = outs[:4]
+    if len(outs) == 6:
+        hidden_ref, gain_ref, base_ref, kept_sum, other_sum = ins[1:6]
+        grad_ref, dgain_ref = outs[4:]
+        dnormed_ref = scratch[3]
+        set_sum((kept_sum, other_sum), dnormed_ref)
+        norm_back_rows(hidden_ref, gain_ref, dnormed_ref, base_ref, grad_ref, low_ref, dgain_ref)
+    else:
+        low_ref[...] = ins[1][...].astype(bf16)
+    arrived(waits)
+    half = ffn_ref.shape[1] // 3
+    times(low_ref, ffn_ref, 2 * half, 3 * half, dactive_ref)
+
+    def body(rows):
+        gate, upper = wide_ref[rows, :half], wide_ref[rows, half:]
+        dactive = dactive_ref[rows, :]
+        lifted = jax.nn.sigmoid(gate)
+        dwide_ref[rows, :half] = (
+            dactive * upper * lifted * (1.0 + gate * (1.0 - lifted))
+        ).astype(bf16)
+        dwide_ref[rows, half:] = (dactive * gate * lifted).astype(bf16)
+
+    by_rows(wide_ref.shape[0], body)
+    parts(dwide_ref, ffn_ref, 0, 2 * half, kept_ref, away_ref)
+
+
+def fourth_kernel(sizes, plans, counts, *refs):
+    ins, outs, scratch = take(refs, *counts[:3])
+    base_ref, middle_ref, gain_ref, kept_sum, other_sum, proj_ref = ins[:6]
+    side = ins[6:13]
+    pieces = ins[len(ins) - counts[3] :]
+    dmiddle_ref, low_ref, dgain_ref, dproj_ref, dtaps_ref, dheads_ref, kept_ref, away_ref = outs
+    in_ref, out_ref, in_sems, out_sems, dpost_ref, dmix_ref = scratch[:6]
+    out_waits = fetch(plans[1], pieces, out_ref, out_sems)
+    waits = fetch(plans[0], pieces, in_ref, in_sems)
+    set_sum((kept_sum, other_sum), dpost_ref)
+    norm_back_rows(middle_ref, gain_ref, dpost_ref, base_ref, dmiddle_ref, low_ref, dgain_ref)
+    arrived(out_waits)
+    times(low_ref, out_ref, 0, out_ref.shape[1], dmix_ref)
+    mixer_backward_kernel(
+        sizes, proj_ref, dmix_ref, *side, dproj_ref, dtaps_ref, dheads_ref, *scratch[6:]
+    )
+    arrived(waits)
+    parts(dproj_ref, in_ref, 0, in_ref.shape[1], kept_ref, away_ref)
+
+
+def run_kernel(kernel, name, ins, pieces, out_shapes, scratch, waited=(), flops=10**9):
+    vmem, anywhere = pl.BlockSpec(memory_space=pltpu.VMEM), pl.BlockSpec(memory_space=pl.ANY)
+    arrays = list(ins) + list(waited) + list(pieces)
+    counts = (len(arrays), len(out_shapes), len(scratch), len(pieces) + len(waited))
+
+    def body(*refs):
+        ordered = list(refs)
+        first = len(ins)
+        ordered[first : first + len(waited) + len(pieces)] = (
+            refs[first + len(waited) : len(arrays)] + refs[first : first + len(waited)]
+        )
+        kernel(counts, *ordered)
+
     return pl.pallas_call(
-        partial(mixer_forward_kernel, sizes),
-        out_shape=jax.ShapeDtypeStruct((length, sizes[2]), bf16),
-        scratch_shapes=shared_scratch(length, width),
-        compiler_params=pltpu.CompilerParams(vmem_limit_bytes=40 * 1024 * 1024),
-        cost_estimate=pl.CostEstimate(flops=10**9, bytes_accessed=4 * 10**6, transcendentals=10**6),
-        name="mixer_forward",
-    )(proj, *side)
-
-
-def mixer_backward(sizes, proj, dmix, side):
-    length, width = proj.shape[0], sizes[3] - sizes[2]
-    conv_width = sizes[4] - sizes[2]
-    return pl.pallas_call(
-        partial(mixer_backward_kernel, sizes),
-        out_shape=(
-            jax.ShapeDtypeStruct(proj.shape, bf16),
-            jax.ShapeDtypeStruct((8, conv_width), f32),
-            jax.ShapeDtypeStruct((8, LANES), f32),
+        body,
+        out_shape=out_shapes,
+        in_specs=[vmem] * len(ins) + [anywhere] * (len(waited) + len(pieces)),
+        out_specs=[vmem] * len(out_shapes),
+        scratch_shapes=scratch,
+        compiler_params=pltpu.CompilerParams(vmem_limit_bytes=56 * 1024 * 1024),
+        cost_estimate=pl.CostEstimate(
+            flops=flops, bytes_accessed=10**7, transcendentals=10**6
         ),
-        scratch_shapes=shared_scratch(length, width)
+        name=name,
+    )(*arrays)
+
+
+def shape(kind, *sizes):
+    return jax.ShapeDtypeStruct(sizes, kind)
+
+
+def swap(value, axis, distance):
+    size = lax.axis_size(axis)
+    return lax.ppermute(value, axis, [(i, i ^ distance) for i in range(size)])
+
+
+def after(value, other):
+    last = tuple(size - 1 for size in other.shape)
+    ready = jnp.logical_not(other[last].astype(f32) > 3.3e38)
+    return jnp.where(ready, value, jnp.zeros_like(value))
+
+
+def bound(value, *others):
+    for other in others:
+        value = after(value, other)
+    return value
+
+
+def add(left, right):
+    return (left.astype(f32) + right.astype(f32)).astype(bf16)
+
+
+def row_steps(kept, away):
+    middle = add(kept, swap(away, "row", 1))
+    kept = add(middle, swap(middle, "row", 2))
+    return middle, (kept, swap(kept, "row", 1))
+
+
+def row_sum(kept, away):
+    return row_steps(kept, away)[1]
+
+
+def in_order(own, other, own_is_second, axis):
+    return jnp.where(
+        own_is_second == 0,
+        jnp.concatenate([own, other], axis=axis),
+        jnp.concatenate([other, own], axis=axis),
+    )
+
+
+def half_index():
+    return lax.axis_index("dp") & 1
+
+
+def turn(value, axis):
+    low, high = jnp.split(value, 2, axis=axis)
+    return in_order(low, high, half_index(), axis)
+
+
+def by_half(value):
+    pieces = jnp.split(value, value.shape[1] // LANES, axis=1)
+    return jnp.concatenate(pieces[0::2] + pieces[1::2], axis=1)
+
+
+def by_block(value):
+    count = value.shape[1] // LANES // 2
+    pieces = jnp.split(value, 2 * count, axis=1)
+    return jnp.concatenate(
+        [pieces[half * count + block] for block in range(count) for half in range(2)], axis=1
+    )
+
+
+def transpose_blocks(value):
+    rows, cols = lax.axis_size("row"), lax.axis_size("col")
+    pairs = [(r * cols + c, c * cols + r) for r in range(rows) for c in range(cols)]
+    return lax.ppermute(value, ("row", "col"), pairs)
+
+
+def whole_features(value):
+    block = transpose_blocks(turn(value, 1))
+    row = lax.axis_index("row")
+    pair = in_order(block, swap(block, "row", 1), row & 1, 1)
+    return by_half(in_order(pair, swap(pair, "row", 2), row >> 1, 1))
+
+
+def own_features(value):
+    row = lax.axis_index("row")
+    halves = [
+        lax.dynamic_slice_in_dim(piece, row * LANES, LANES, 1)
+        for piece in jnp.split(value, 2, axis=1)
+    ]
+    return transpose_blocks(turn(jnp.concatenate(halves, axis=1), 1))
+
+
+def gather_first(chunks):
+    halves = [jnp.split(turn(chunk, 0), 2, axis=0) for chunk in chunks]
+    gathered, seconds, earlier = [], [], None
+    for mine, _ in halves:
+        if earlier is not None:
+            mine = after(mine, earlier)
+        seconds.append(swap(mine, "col", 2))
+        earlier = seconds[-1]
+    for (mine, theirs), second in zip(halves, seconds):
+        pair = swap(jnp.concatenate([mine, second], axis=0), "col", 1)
+        others = swap(jnp.concatenate([second, pair], axis=0), "dp", 1)
+        gathered.append((mine, second, pair, theirs, others))
+    return gathered
+
+
+def first_plan(base, rows, columns):
+    places = [(0, 0, 0, 0), (2, 0, 0, 1), (1, 0, 0, 2), (2, rows, 0, 3)]
+    places += [(3, 0, 1, 0), (4, rows, 1, 1), (4, 0, 1, 2), (4, 2 * rows, 1, 3)]
+    return [(base + piece, first, rows, half, distance, *columns) for piece, first, half, distance in places]
+
+
+def gather_later(weight, earlier):
+    half = weight.shape[0] // 2
+    mine, theirs = jnp.split(turn(weight, 0), 2, axis=0)
+    whole = lax.all_gather(after(mine, earlier), "col", axis=0, tiled=True)
+    col = lax.axis_index("col")
+    others = [lax.dynamic_slice_in_dim(whole, (col ^ k) * half, half, 0) for k in range(1, 4)]
+    return (whole, theirs, swap(jnp.concatenate(others, axis=0), "dp", 1))
+
+
+def later_plan(rows, blocks, columns):
+    places = [(0, 0, rows * blocks, 0, None), (1, 0, rows, 1, 0)]
+    places += [(2, (k - 1) * rows, rows, 1, k) for k in range(1, 4)]
+    return [(*place, *columns) for place in places]
+
+
+def gather_whole(weight, earlier):
+    return (lax.all_gather(after(weight, earlier), "col", axis=0, tiled=True),)
+
+
+def whole_plan(rows, blocks, columns):
+    return [
+        (0, (2 * block + half) * rows, rows, (half,), (block,), *columns)
+        for block in range(blocks)
+        for half in range(2)
+    ]
+
+
+def three_parts(value):
+    high = lax.reduce_precision(value, 8, 7)
+    rest = value - high
+    middle = lax.reduce_precision(rest, 8, 7)
+    return [high.astype(bf16), middle.astype(bf16), (rest - middle).astype(bf16)]
+
+
+def other_batches(value):
+    size = lax.axis_size("dp")
+    if size == 2:
+        return value
+    groups = [list(range(0, size, 2)), list(range(1, size, 2))]
+    return lax.psum(value, "dp", axis_index_groups=groups)
+
+
+def col_scatter(value):
+    return other_batches(lax.psum_scatter(value, "col", scatter_dimension=0, tiled=True))
+
+
+def add_kernel(counts, *refs):
+    ins, outs, _ = take(refs, *counts[:3])
+
+    def body(rows):
+        outs[0][rows, :] = (ins[0][rows, :].astype(f32) + ins[1][rows, :].astype(f32)).astype(bf16)
+
+    by_rows(outs[0].shape[0], body)
+
+
+def dp_sum(mine, received, *waited):
+    outs = (jax.ShapeDtypeStruct(mine.shape, bf16),)
+    return run_kernel(add_kernel, "sum_halves", (mine, received), (), outs, [], waited)[0]
+
+
+def sum_batches(value):
+    return add(value, swap(value, "dp", 1))
+
+
+def other_half(value):
+    return in_order(value, swap(value, "dp", 1), half_index(), 0)
+
+
+def sum_small(value):
+    value = value + swap(value, "col", 1)
+    value = value + swap(value, "col", 2)
+    if lax.axis_size("dp") != 2:
+        return lax.psum(value, "dp")
+    return value + swap(value, "dp", 1)
+
+
+def sum_row_small(value):
+    value = value + swap(value, "row", 1)
+    return value + swap(value, "row", 2)
+
+
+def in_blocks(value):
+    value = value.reshape(2, -1, LANES)
+    value = jnp.where(half_index() == 0, value, value[::-1])
+    return jnp.swapaxes(value, 0, 1).reshape(-1)
+
+
+def mixer_scratch(plan, out_plan, features, in_cols, out_cols):
+    return [
+        pltpu.VMEM((features, in_cols), bf16),
+        pltpu.VMEM((features, out_cols), bf16),
+        pltpu.SemaphoreType.DMA((len(plan),)),
+        pltpu.SemaphoreType.DMA((len(out_plan),)),
+    ]
+
+
+def layer_forward(base, sums, params, sizes, waited):
+    input_gain, post_gain, mixer_pieces, plans, ffn_pieces, ffn_plan, side, in_cols, ffn_cols = params
+    length, features = base.shape
+    out_cols, width = sizes[2], sizes[3] - sizes[2]
+    part = shape(bf16, length // 2, features)
+    hidden, normed, proj, mixed, kept, away = run_kernel(
+        partial(first_kernel, sizes, plans),
+        "norm_mixer_out",
+        (base, input_gain, *side, *sums),
+        mixer_pieces,
+        (
+            shape(f32, length, features),
+            shape(bf16, length, features),
+            shape(f32, length, in_cols),
+            shape(bf16, length, out_cols),
+            part,
+            part,
+        ),
+        mixer_scratch(*plans, features, in_cols, out_cols) + shared_scratch(length, width),
+        waited,
+        flops=10**7,
+    )
+    middle, post, wide, active, kept, away = run_kernel(
+        partial(second_kernel, (ffn_plan,)),
+        "norm_feed_forward",
+        (hidden, post_gain, *row_sum(kept, away)),
+        ffn_pieces,
+        (
+            shape(f32, length, features),
+            shape(bf16, length, features),
+            shape(f32, length, 2 * ffn_cols),
+            shape(bf16, length, ffn_cols),
+            part,
+            part,
+        ),
+        [
+            pltpu.VMEM((features, 3 * ffn_cols), bf16),
+            pltpu.SemaphoreType.DMA((len(ffn_plan),)),
+        ],
+        flops=2 * 10**9,
+    )
+    return middle, row_sum(kept, away), (hidden, normed, proj, mixed, middle, post, wide, active)
+
+
+def layer_backward(grad, above, saved, params, sizes, layer, waited):
+    input_gain, post_gain, mixer_pieces, plans, ffn_pieces, ffn_plan, side, in_cols, ffn_cols = params
+    hidden, normed, proj, mixed, middle, post, wide, active = saved
+    length, features = hidden.shape
+    own = features // 2
+    out_cols, width, conv_width = sizes[2], sizes[3] - sizes[2], sizes[4] - sizes[2]
+    part = shape(bf16, length // 2, features)
+    outs = [shape(bf16, length, features), shape(bf16, length, 2 * ffn_cols), part, part]
+    scratch = [
+        pltpu.VMEM((features, 3 * ffn_cols), bf16),
+        pltpu.SemaphoreType.DMA((len(ffn_plan),)),
+        pltpu.VMEM((length, ffn_cols), f32),
+    ]
+    if above is None:
+        ins = (wide, grad)
+    else:
+        ins = (wide, *above)
+        outs += [shape(f32, length, features), shape(f32, 1, features)]
+        scratch.append(pltpu.VMEM((length, features), bf16))
+    low, dwide, kept, away, *rest = run_kernel(
+        partial(third_kernel, (ffn_plan,)),
+        "feed_forward_back",
+        ins,
+        ffn_pieces,
+        tuple(outs),
+        scratch,
+        waited[0],
+        flops=2 * 10**9,
+    )
+    gain_above = None
+    if above is not None:
+        grad, gain_above = rest
+    total = row_sum(kept, away)
+    last = layer == LAYERS - 1
+    theirs = jnp.concatenate(
+        [
+            dot(post[:, own:], dwide, TN).astype(bf16),
+            dot(low[:, own:], active, TN).astype(bf16),
+        ],
+        axis=1,
+    )
+    mine = jnp.concatenate(
+        [
+            dot(post[:, :own], dwide, TN).astype(bf16),
+            dot(low[:, :own], active, TN).astype(bf16),
+        ],
+        axis=1,
+    )
+    wide_mine, wide_received, wide_tie = mine, swap(theirs, "dp", 1), total[1]
+    before = (mine, theirs) + tuple(waited[1])
+    if not last:
+        later = add(waited[2][0], after(waited[2][1], total[1]))
+        later_sum = col_scatter(later)
+        before += (later,)
+    dmiddle, low, post_gain_grad, dproj, dtaps, dheads, kept, away = run_kernel(
+        partial(fourth_kernel, sizes, plans),
+        "norm_mixer_back",
+        (grad, middle, post_gain, *total, proj, *side),
+        mixer_pieces,
+        (
+            shape(f32, length, features),
+            shape(bf16, length, features),
+            shape(f32, 1, features),
+            shape(bf16, length, in_cols),
+            shape(f32, 8, conv_width),
+            shape(f32, 8, LANES),
+            part,
+            part,
+        ),
+        mixer_scratch(*plans, features, in_cols, out_cols)
+        + [pltpu.VMEM((length, features), bf16), pltpu.VMEM((length, out_cols), f32)]
+        + shared_scratch(length, width)
         + [
             pltpu.VMEM((length, conv_width), f32),
             pltpu.VMEM((length, width), f32),
@@ -383,118 +908,52 @@
             pltpu.VMEM((length, LANES), f32),
             pltpu.VMEM((length + 8, conv_width), f32),
         ],
-        compiler_params=pltpu.CompilerParams(vmem_limit_bytes=48 * 1024 * 1024),
-        cost_estimate=pl.CostEstimate(flops=3 * 10**9, bytes_accessed=6 * 10**6, transcendentals=10**6),
-        name="mixer_backward",
-    )(proj, dmix, *side)
-
-
-def swap(value, distance):
-    size = lax.axis_size("row")
-    return lax.ppermute(value, "row", [(i, i ^ distance) for i in range(size)])
-
-
-def row_sum(part):
-    if lax.axis_size("row") != 4:
-        return lax.psum(part, "row")
-    half = part.shape[0] // 2
-    parity = lax.axis_index("row") % 2
-    away = lax.dynamic_slice_in_dim(part, (1 - parity) * half, half, 0)
-    kept = lax.dynamic_slice_in_dim(part, parity * half, half, 0)
-    kept = (kept.astype(f32) + swap(away, 1).astype(f32)).astype(bf16)
-    kept = (kept.astype(f32) + swap(kept, 2).astype(f32)).astype(bf16)
-    other = swap(kept, 1)
-    return jnp.where(
-        parity == 0,
-        jnp.concatenate([kept, other], axis=0),
-        jnp.concatenate([other, kept], axis=0),
-    )
-
-
-def transpose_blocks(value):
-    rows, cols = lax.axis_size("row"), lax.axis_size("col")
-    pairs = [(r * cols + c, c * cols + r) for r in range(rows) for c in range(cols)]
-    return lax.ppermute(value, ("row", "col"), pairs)
-
-
-def whole_features(value):
-    return lax.all_gather(transpose_blocks(value), "row", axis=1, tiled=True)
-
-
-def own_block(value):
-    count = value.shape[1] // lax.axis_size("row")
-    block = lax.dynamic_slice_in_dim(value, lax.axis_index("row") * count, count, 1)
-    return transpose_blocks(block)
-
-
-def gather_weight(weight):
-    return lax.all_gather(weight, "col", axis=0, tiled=True)
-
-
-def scatter_grad(grad):
-    grad = lax.psum_scatter(grad.astype(bf16), "col", scatter_dimension=0, tiled=True)
-    return lax.psum(grad, "dp")
-
-
-def norm(hidden, gain):
+        before,
+        flops=5 * 10**9,
+    )
+    total = row_sum(kept, away)
+    if last:
+        wide = add(wide_mine, after(wide_received, wide_tie))
+        theirs_out = dot(low[:, own:], mixed, TN).astype(bf16)
+        out_received = swap(theirs_out, "dp", 1)
+        mine_out = dot(low[:, :own], mixed, TN).astype(bf16)
+        out = add(mine_out, after(out_received, total[0]))
+        theirs = dot(normed[:, own:], dproj, TN).astype(bf16)
+        mine = dot(normed[:, :own], dproj, TN).astype(bf16)
+        in_received = swap(theirs, "dp", 1)
+        wide_sum, out_sum = col_scatter(wide), col_scatter(out)
+        waited = ((theirs, mine, wide, out), (wide_sum,), (mine, in_received))
+        sums = (wide_sum, out_sum)
+    else:
+        theirs = jnp.concatenate(
+            [
+                dot(normed[:, own:], dproj, TN).astype(bf16),
+                dot(low[:, own:], mixed, TN).astype(bf16),
+            ],
+            axis=1,
+        )
+        received = swap(theirs, "dp", 1)
+        mine = jnp.concatenate(
+            [
+                dot(normed[:, :own], dproj, TN).astype(bf16),
+                dot(low[:, :own], mixed, TN).astype(bf16),
+            ],
+            axis=1,
+        )
+        whole = dp_sum(mine, received, total[0], later_sum)
+        wide = dp_sum(wide_mine, wide_received, whole)
+        sums = (col_scatter(wide), col_scatter(whole), later_sum, wide)
+    above = (hidden, input_gain, dmiddle, *total)
+    return above, waited, gain_above, post_gain_grad, dheads, dtaps, sums
+
+
+def last_norm_back(hidden, gain, base, kept, other):
+    grad = in_order(kept, other, lax.axis_index("row") & 1, 0).astype(f32)
     inverse = lax.rsqrt(jnp.mean(hidden * hidden, axis=1, keepdims=True) + epsilon)
-    return (hidden * inverse * gain[None, :]).astype(bf16), inverse
-
-
-def norm_back(hidden, inverse, gain, grad):
-    weighted = grad * gain[None, :]
+    weighted = grad * gain
     mean = jnp.mean(weighted * hidden, axis=1, keepdims=True)
-    grad_hidden = inverse * weighted - hidden * (inverse * inverse * inverse * mean)
-    return grad_hidden, jnp.sum(grad * hidden * inverse, axis=0)
-
-
-def layer_forward(hidden, params, sizes):
-    input_gain, post_gain, in_weight, out_weight, ffn_weight, side = params
-    half = (ffn_weight.shape[1]) // 3
-    normed, inverse = norm(hidden, input_gain)
-    proj = dot(normed, in_weight)
-    mixed = mixer_forward(sizes, proj, side)
-    middle = hidden + row_sum(dot(mixed, out_weight, NT).astype(bf16)).astype(f32)
-    post, post_inverse = norm(middle, post_gain)
-    wide = dot(post, ffn_weight[:, : 2 * half])
-    gate, upper = wide[:, :half], wide[:, half:]
-    active = (jax.nn.silu(gate) * upper).astype(bf16)
-    output = middle + row_sum(dot(active, ffn_weight[:, 2 * half :], NT).astype(bf16)).astype(f32)
-    return output, (hidden, inverse, normed, proj, mixed, middle, post_inverse, post, wide, active)
-
-
-def layer_backward(grad, saved, params, sizes):
-    input_gain, post_gain, in_weight, out_weight, ffn_weight, side = params
-    hidden, inverse, normed, proj, mixed, middle, post_inverse, post, wide, active = saved
-    half = (ffn_weight.shape[1]) // 3
-    gate, upper = wide[:, :half], wide[:, half:]
-    low = grad.astype(bf16)
-    dactive = dot(low, ffn_weight[:, 2 * half :])
-    lifted = jax.nn.sigmoid(gate)
-    dgate = dactive * upper * lifted * (1.0 + gate * (1.0 - lifted))
-    dwide = jnp.concatenate([dgate, dactive * gate * lifted], axis=1).astype(bf16)
-    dpost = row_sum(dot(dwide, ffn_weight[:, : 2 * half], NT).astype(bf16)).astype(f32)
-    ffn_grad = scatter_grad(
-        jnp.concatenate([dot(post, dwide, TN), dot(low, active, TN)], axis=1)
-    )
-    dmiddle, post_gain_grad = norm_back(middle, post_inverse, post_gain, dpost)
-    dmiddle = dmiddle + grad
-    low = dmiddle.astype(bf16)
-    dmix = dot(low, out_weight)
-    out_grad = scatter_grad(dot(low, mixed, TN))
-    dproj, dtaps, dheads = mixer_backward(sizes, proj, dmix, side)
-    dnormed = row_sum(dot(dproj, in_weight, NT).astype(bf16)).astype(f32)
-    in_grad = scatter_grad(dot(normed, dproj, TN))
-    dhidden, input_gain_grad = norm_back(hidden, inverse, input_gain, dnormed)
-    return dmiddle + dhidden, (
-        ffn_grad,
-        out_grad,
-        in_grad,
-        dtaps,
-        dheads,
-        input_gain_grad,
-        post_gain_grad,
-    )
+    total = base + inverse * weighted - hidden * (inverse * inverse * inverse * mean)
+    return total, jnp.sum(grad * hidden * inverse, axis=0)
 
 
 def shards(
@@ -564,7 +1023,7 @@
         == lax.broadcasted_iota(jnp.int32, (LANES, heads_row * M_HEAD), 1) // M_HEAD
     ).astype(f32)
 
-    params = []
+    sides = []
     for layer in range(LAYERS):
         heads = jnp.stack([step_bias[layer], jnp.exp(decay_log[layer])])
         side = (
@@ -578,80 +1037,187 @@
             jnp.repeat(skip_gain[layer], M_HEAD)[None, :],
             spread,
         )
-        params.append(
+        sides.append(side)
+    local_gains = jnp.concatenate([input_gain, post_gain], axis=0)
+    spare = jnp.stack(three_parts(local_gains), axis=0).reshape(6 * LAYERS, -1).T
+    first_spare = sizes[5] + heads_row
+    in_first = lax.dynamic_update_slice(in_local[0], spare, (0, first_spare))
+    rows, blocks = hidden_in.shape[1] // 2, lax.axis_size("col")
+    in_cols, out_cols, all_ffn = in_local.shape[2], out_local.shape[2], ffn_local.shape[2]
+    cut = sizes[3]
+    chunks = (
+        in_first[:, :cut],
+        jnp.concatenate([in_first[:, cut:], out_local[0]], axis=1),
+        ffn_local[0],
+    )
+    front, rear, ffn_first = gather_first(chunks)
+    rest = in_cols - cut
+    mixer_pieces = [front + rear]
+    plans = [
+        (
+            first_plan(0, rows, (0, 0, cut)) + first_plan(5, rows, (0, cut, rest)),
+            first_plan(5, rows, (rest, 0, out_cols)),
+        )
+    ]
+    ffn_pieces, ffn_plans = [ffn_first], [first_plan(0, rows, (0, 0, all_ffn))]
+    earlier = ffn_first[2]
+    for layer in range(1, LAYERS):
+        later = jnp.concatenate([in_local[layer], out_local[layer]], axis=1)
+        mixer_pieces.append(gather_later(later, earlier))
+        plans.append(
             (
-                lax.all_gather(input_gain[layer], "col", axis=0, tiled=True),
-                lax.all_gather(post_gain[layer], "col", axis=0, tiled=True),
-                gather_weight(in_local[layer]),
-                gather_weight(out_local[layer]),
-                gather_weight(ffn_local[layer]),
-                side,
+                later_plan(rows, blocks, (0, 0, in_cols)),
+                later_plan(rows, blocks, (in_cols, 0, out_cols)),
             )
         )
-
-    hidden = whole_features(hidden_in).astype(f32)
-    grad = whole_features(cotangent).astype(f32)
-    stored = []
+        ffn_pieces.append(gather_whole(ffn_local[layer], mixer_pieces[-1][0]))
+        ffn_plans.append(whole_plan(rows, blocks, (0, 0, all_ffn)))
+    spares = [piece[:, first_spare - cut : first_spare - cut + 6 * LAYERS] for piece in rear]
+    mine, second, pair, theirs, others = spares
+    col = lax.axis_index("col")
+
+    def in_place(own, first, second, third):
+        near, far = in_order(own, first, col & 1, 0), in_order(second, third, col & 1, 0)
+        return in_order(near, far, col >> 1, 0)
+
+    spare = jnp.concatenate(
+        [
+            in_place(mine, pair[:rows], second, pair[rows:]),
+            in_place(theirs, others[rows : 2 * rows], others[:rows], others[2 * rows :]),
+        ],
+        axis=0,
+    )
+    gains = jnp.sum(spare.T.astype(f32).reshape(3, 2 * LAYERS, -1), axis=0)
+    params = [
+        (
+            gains[layer : layer + 1],
+            gains[LAYERS + layer : LAYERS + layer + 1],
+            mixer_pieces[layer],
+            plans[layer],
+            ffn_pieces[layer],
+            ffn_plans[layer],
+            sides[layer],
+            in_cols,
+            all_ffn // 3,
+        )
+        for layer in range(LAYERS)
+    ]
+
+    hidden = whole_features(hidden_in)
+    grad = whole_features(cotangent)
+    stored, summed = [], ()
     for layer in range(LAYERS):
-        hidden, saved = layer_forward(hidden, params[layer], sizes)
+        hidden, summed, saved = layer_forward(
+            hidden, summed, params[layer], sizes, (grad,) if layer == 0 else ()
+        )
         stored.append(saved)
-    hidden_out = own_block(hidden.astype(bf16))
-    collected = [None] * LAYERS
+    hidden_out = hidden + in_order(*summed, row_index & 1, 0).astype(f32)
+    hidden_out = own_features(hidden_out.astype(bf16))
+    sums, above, waited = [None] * LAYERS, None, ((), (), None)
+    heads, taps, input_gains, post_gains = [], [], [], []
     for layer in reversed(range(LAYERS)):
-        grad, collected[layer] = layer_backward(grad, stored[layer], params[layer], sizes)
-    hidden_grad = own_block(grad)
-
-    ffn_grad, out_grad, in_grad, dtaps, dheads, input_gain_grad, post_gain_grad = (
-        jnp.stack([entry[member] for entry in collected]) for member in range(7)
-    )
-    first = sizes[3]
-    states_part = in_grad[:, :, sizes[3] : sizes[4]].astype(f32)
-    key_part = in_grad[:, :, sizes[4] : sizes[4] + HEAD].astype(f32)
-    value_part = in_grad[:, :, sizes[4] + HEAD : sizes[5]].astype(f32)
-    steps_part = in_grad[:, :, sizes[5] : sizes[5] + heads_row].astype(f32)
-    keyval_part = jnp.zeros(keyval_weight.shape, f32)
-    keyval_part = lax.dynamic_update_slice_in_dim(keyval_part, key_part, key_first, 2)
-    keyval_part = lax.dynamic_update_slice_in_dim(keyval_part, value_part, value_first, 2)
-    step_part = lax.dynamic_update_slice_in_dim(
-        jnp.zeros(step_weight.shape, f32), steps_part, step_first, 2
-    )
-    shared_grad = lax.psum(
-        jnp.concatenate([keyval_part, states_part, step_part], axis=2).astype(bf16), "row"
-    ).astype(f32)
-    kv_cols = keyval_weight.shape[2]
-    dtaps, dheads, input_gain_grad, post_gain_grad = lax.psum(
-        (dtaps, dheads, input_gain_grad, post_gain_grad), ("dp", "col")
-    )
-    conv_shared_grad = lax.psum(dtaps[:, :4, input_cols:], "row")
+        above, waited, gain_above, post_gain_grad, dheads, dtaps, sums[layer] = layer_backward(
+            grad, above, stored[layer], params[layer], sizes, layer, waited
+        )
+        if gain_above is not None:
+            input_gains.insert(0, gain_above[0])
+        post_gains.insert(0, post_gain_grad[0])
+        heads.insert(0, dheads[:3].reshape(-1))
+        taps.insert(0, dtaps[:4].reshape(-1))
+    grad, last_gain = last_norm_back(*above)
+    input_gains.insert(0, last_gain)
+    hidden_grad = own_features(grad.astype(bf16)).astype(f32)
+    small = jnp.stack(
+        [
+            jnp.concatenate(
+                [
+                    in_blocks(input_gains[layer]),
+                    in_blocks(post_gains[layer]),
+                    heads[layer],
+                    taps[layer],
+                ]
+            )
+            for layer in range(LAYERS)
+        ]
+    )
+    small = sum_small(after(small, sums[0][1]))
+
+    half, wide = gate_weight.shape[2], 2 * gate_weight.shape[2]
+    collected, shared_parts = [], []
+    for layer in range(LAYERS):
+        if layer == LAYERS - 1:
+            wide_sum, out_sum = sums[layer]
+            whole = jnp.concatenate([wide_sum, sums[0][2], out_sum], axis=1)
+            whole = other_half(after(whole, sums[0][3]))
+            wide_part, down_part, in_part, shared_part, out_part = jnp.split(
+                whole, [wide, wide + half, wide + half + sizes[3], wide + half + in_cols], axis=1
+            )
+        else:
+            wide_sum, mixer_sum = sums[layer][:2]
+            whole, mixer = other_half(wide_sum), other_half(mixer_sum)
+            wide_part, down_part = whole[:, :wide], whole[:, wide:]
+            in_part, shared_part, out_part = jnp.split(mixer, [sizes[3], in_cols], axis=1)
+        shared_parts.append(shared_part)
+        collected.append((wide_part, in_part, down_part, out_part))
+
+    key_cols = keyval_weight.shape[2]
+    placed = []
+    for part in shared_parts:
+        keyval = jnp.zeros((part.shape[0], key_cols), bf16)
+        key_at = state_cols
+        keyval = lax.dynamic_update_slice_in_dim(keyval, part[:, key_at : key_at + HEAD], key_first, 1)
+        keyval = lax.dynamic_update_slice_in_dim(
+            keyval, part[:, key_at + HEAD : key_at + 2 * HEAD], value_first, 1
+        )
+        key_at = key_at + 2 * HEAD
+        steps = lax.dynamic_update_slice_in_dim(
+            jnp.zeros((part.shape[0], step_weight.shape[2]), bf16),
+            part[:, key_at : key_at + heads_row],
+            step_first,
+            1,
+        )
+        total = jnp.concatenate([keyval, part[:, :state_cols], steps], axis=1)
+        total = add(total, swap(total, "row", 1))
+        placed.append(total.astype(f32) + swap(total, "row", 2).astype(f32))
     features = hidden_in.shape[1]
-
-    def own_gain(value):
-        return lax.dynamic_slice_in_dim(value, col_index * features, features, 1)
-
-    half = gate_weight.shape[2]
+    width = features * lax.axis_size("col")
+    taps = small[:, 2 * width + 3 * LANES :].reshape(LAYERS, 4, input_cols + state_cols)
+    heads = small[:, 2 * width : 2 * width + 3 * LANES].reshape(LAYERS, 3, LANES)
+
+    def own_gain(first):
+        return lax.dynamic_slice_in_dim(small, first + col_index * features, features, 1)
+
+    def outputs(member, first=None, last=None, turned=False):
+        entries = [entry[member].astype(f32) for entry in collected]
+        if turned:
+            entries = [entry.T[first:last] for entry in entries]
+        else:
+            entries = [entry[:, first:last] for entry in entries]
+        return jnp.stack(entries)
+
     attn_rows = attention_out.shape[1]
-    out_grad = jnp.swapaxes(out_grad.astype(f32), 1, 2)
+    shared = jnp.stack(placed)
     return (
         hidden_out,
         hidden_grad,
-        own_gain(input_gain_grad),
-        in_grad[:, :, :query_cols].astype(f32),
-        shared_grad[:, :, :kv_cols],
-        in_grad[:, :, sizes[1] : sizes[2]].astype(f32),
-        in_grad[:, :, sizes[2] : sizes[3]].astype(f32),
-        shared_grad[:, :, kv_cols : kv_cols + state_cols],
-        shared_grad[:, :, kv_cols + state_cols :],
-        dtaps[:, :4, :input_cols],
-        conv_shared_grad,
-        dheads[:, 0, :heads_row],
-        dheads[:, 1, :heads_row],
-        dheads[:, 2, :heads_row],
-        out_grad[:, :attn_rows, :],
-        out_grad[:, attn_rows:, :],
-        own_gain(post_gain_grad),
-        ffn_grad[:, :, :half].astype(f32),
-        ffn_grad[:, :, half : 2 * half].astype(f32),
-        jnp.swapaxes(ffn_grad[:, :, 2 * half :].astype(f32), 1, 2),
+        own_gain(0),
+        outputs(1, 0, sizes[1]),
+        shared[:, :, :key_cols],
+        outputs(1, sizes[1], sizes[2]),
+        outputs(1, sizes[2], sizes[3]),
+        shared[:, :, key_cols : key_cols + state_cols],
+        shared[:, :, key_cols + state_cols :],
+        taps[:, :, :input_cols],
+        sum_row_small(taps[:, :, input_cols:]),
+        heads[:, 0, :heads_row],
+        heads[:, 1, :heads_row],
+        heads[:, 2, :heads_row],
+        outputs(3, 0, attn_rows, True),
+        outputs(3, attn_rows, None, True),
+        own_gain(width),
+        outputs(0, 0, half),
+        outputs(0, half, wide),
+        outputs(2, 0, None, True),
     )
 
 

time: 957 us -> 648 us (0.68)
  waiting for transfers between devices: 633 us -> 278 us
  blocking collectives: 81.6 us -> 0 us
  Pallas kernels: 39.8 us -> 115 us
  starting transfers between devices: 16 us -> 69.7 us
  matrix products: 64.4 us -> 27.7 us
  other arithmetic: 52.1 us -> 70.1 us
  local copies, waits for them, and re-layouts: 45.4 us -> 57 us
    psum x3 -> x0, waiting for transfers between devices: 174 us -> none  [the longest x1 85.3 us: scatter_grad(): return lax.psum(grad, 'dp')]
    all_gather x8 -> x2, waiting for transfers between devices: 176 us -> 6.74 us  [the longest x1 6.74 us: gather_later(): whole = lax.all_gather(after(mine, earlier), 'col', axis=0, tiled=True)]
    reduce_scatter x6 -> x5, waiting for transfers between devices: 159 us -> 20.7 us  [col_scatter(): lax.psum_scatter(value, 'col', scatter_dimension=0, tiled=True)]
    ppermute x24 -> x55, waiting for transfers between devices: 124 us -> 251 us  [swap(): return lax.ppermute(value, axis, [(i, i ^ distance) for i in range(size)])]
    pallas_call x4 -> x10, Pallas kernels: 39.8 us -> 115 us  [run_kernel(): pl.pallas_call(body, out_shape=out_shapes, in_specs=[vmem] * len(ins) + [...]
    all_gather x4 -> x0, blocking collectives: 75 us -> none  [the longest x2 42.7 us: shards(): lax.all_gather(post_gain[layer], 'col', axis=0, tiled=True)]
    ppermute x24 -> x55, starting transfers between devices: 10.1 us -> 59.6 us  [swap(): return lax.ppermute(value, axis, [(i, i ^ distance) for i in range(size)])]
    dot_general x24 -> x16, matrix products: 64.4 us -> 27.7 us  [dot(): lax.dot_general(left, right, dims, precision=precision, preferred_element...]
  transfers between devices with their start and end apart: 45 -> 66, of which waited for: 33 -> 41; matrix products, arithmetic and copies ran while one was open for 13% -> 21% of each run, Pallas kernels for 4% -> 17%
where the time goes in v2:
time: 648 us; the launch traced here: 640 us
  waiting for transfers between devices  278 us (43%)
  Pallas kernels  115 us (18%)
  other arithmetic  70.1 us (11%)
  starting transfers between devices  69.7 us (11%)
  local copies, waits for them, and re-layouts  57 us (9%)
  matrix products  27.7 us (4%)
  between operations  22.9 us (4%)
    ppermute x55, waiting for transfers between devices, swap(): return lax.ppermute(value, axis, [(i, i ^ distance) for i in range(size)])  251 us
    pallas_call x10, Pallas kernels, run_kernel(): pl.pallas_call(body, out_shape=out_shapes, in_specs=[vmem] * len(ins) + [...  115 us
    ppermute x55, starting transfers between devices, swap(): return lax.ppermute(value, axis, [(i, i ^ distance) for i in range(size)])  59.6 us
    dot_general x16, matrix products, dot(): lax.dot_general(left, right, dims, precision=precision, preferred_element...  27.7 us
    unnamed x239, local copies, waits for them, and re-layouts  23.3 us
    reduce_scatter x5, waiting for transfers between devices, col_scatter(): lax.psum_scatter(value, 'col', scatter_dimension=0, tiled=True)  20.7 us
    select_n x21, other arithmetic, in_order(): jnp.where(own_is_second == 0, jnp.concatenate([own, other], axis=axis), j...  15.9 us
  transfers between devices with their start and end apart: 66, of which 41 were waited for; matrix products, arithmetic and copies ran while one was open for 21% of the time, Pallas kernels for 17%

profile of v2, /device:TPU:0, one launch (start us, length us, event | category | flops | bytes accessed | tf_op | source)
XLA Modules:
  0.0 640.3 jit_solution(15090601228565911426)
XLA Ops:
  34.5 16.9 %collective-permute-done.3.refs_11_.refs_18_ = bf16[128,896]{1,0:T(8,128)(2,1)} collective-permute-done((bf16[128,896]{1,0:T(8,128)(2,1)S(1)}, bf16[128,896]{1,0:T(8,128)(2,1)}, u32[]{:S(2)}, u32[]{:S(2)}) %collective-permute-start.3) | collective-permute-done | bytes 229408 | tf_op jit(solution)/shard_map/ppermute | solution.py:586
  86.9 6.2 collective-permute-done.5.refs_17_.refs_24_
  104.3 4.7 collective-permute-done.16.refs_6_.refs_12_
  115.7 14.1 %norm_mixer_out.2 = (f32[512,1024]{1,0:T(8,128)}, bf16[512,1024]{1,0:T(8,128)(2,1)}, f32[512,1408]{1,0:T(8,128)}, bf16[512,512]{1,0:T(8,128)(2,1)}, bf16[256,102...) custom-call(bf16[512,1024]{1,0:T(8,128)(2,1)} %copy-done.27, f32[1,1024]{1,0:T(1,128)} %get-tuple-element.265.refs_1_, ...), custom_call_target="tpu_custom_call" | custom-call | flops 10000000 | bytes 10000000 | tf_op jit(solution)/shard_map/norm_mixer_out/pallas_call | solution.py:566
  137.1 10.2 %collective-permute-done.13 = bf16[256,1024]{1,0:T(8,128)(2,1)S(1)} collective-permute-done((bf16[256,1024]{1,0:T(8,128)(2,1)S(1)}, bf16[256,1024]{1,0:T(8,128)(2,1)S(1)}, u32[]{:S(2)}, u32[]{:S(2)}) %collective-permute-start.13) | collective-permute-done | bytes 524320 | tf_op jit(solution)/shard_map/ppermute | solution.py:586
  147.6 6.7 %all-gather.4.cloned.1.call-done.refs_11_.refs_15_ = bf16[512,1920]{1,0:T(8,128)(2,1)} async-done(((bf16[128,1920]{1,0:T(8,128)(2,1)}), bf16[512,1920]{1,0:T(8,128)(2,1)}) %all-gather.4.cloned.1.call-update) | async-done | bytes 1966096 | tf_op jit(solution)/shard_map/all_gather | solution.py:691
  157.8 6.8 %collective-permute-done.17.refs_8_.refs_14_ = bf16[384,1536]{1,0:T(8,128)(2,1)S(1)} collective-permute-done((bf16[384,1536]{1,0:T(8,128)(2,1)}, bf16[384,1536]{1,0:T(8,128)(2,1)S(1)}, u32[]{:S(2)}, u32[]{:S(2)}) %collective-permute-start.17) | collective-permute-done | bytes 1179680 | tf_op jit(solution)/shard_map/ppermute | solution.py:586
  165.6 8.1 %norm_feed_forward.2 = (f32[512,1024]{1,0:T(8,128)}, bf16[512,1024]{1,0:T(8,128)(2,1)}, f32[512,1024]{1,0:T(8,128)}, bf16[512,512]{1,0:T(8,128)(2,1)}, bf16[256,...) custom-call(f32[512,1024]{1,0:T(8,128)} %get-tuple-element.70.refs_0_, f32[1,1024]{1,0:T(1,128)} %get-tuple-element.264.refs_1_.refs_2_, ...), custom_call_target="tpu_custom_call" | custom-call | flops 2000000000 | bytes 10000000 | tf_op jit(solution)/shard_map/norm_feed_forward/pallas_call | solution.py:566
  177.4 12.8 %collective-permute-done.19 = bf16[256,1024]{1,0:T(8,128)(2,1)S(1)} collective-permute-done((bf16[256,1024]{1,0:T(8,128)(2,1)S(1)}, bf16[256,1024]{1,0:T(8,128)(2,1)S(1)}, u32[]{:S(2)}, u32[]{:S(2)}) %collective-permute-start.19) | collective-permute-done | bytes 524320 | tf_op jit(solution)/shard_map/ppermute | solution.py:586
  192.5 16.4 %collective-permute-done.21.refs_13_.refs_17_ = bf16[384,1920]{1,0:T(8,128)(2,1)S(1)} collective-permute-done((bf16[384,1920]{1,0:T(8,128)(2,1)S(1)}, bf16[384,1920]{1,0:T(8,128)(2,1)S(1)}, u32[]{:S(2)}, u32[]{:S(2)}) %collective-permute-start.21) | collective-permute-done | bytes 1474592 | tf_op jit(solution)/shard_map/ppermute | solution.py:586
  210.0 14.2 %norm_mixer_out.3 = (f32[512,1024]{1,0:T(8,128)}, bf16[512,1024]{1,0:T(8,128)(2,1)}, f32[512,1408]{1,0:T(8,128)}, bf16[512,512]{1,0:T(8,128)(2,1)}, bf16[256,102...) custom-call(f32[512,1024]{1,0:T(8,128)} %get-tuple-element.73.refs_0_.refs_1_, f32[1,1024]{1,0:T(1,128)} %get-tuple-element.263.refs_1_.refs_2_, ...), custom_call_target="tpu_custom_call" | custom-call | flops 10000000 | bytes 10000000 | tf_op jit(solution)/shard_map/norm_mixer_out/pallas_call | solution.py:566
  228.9 12.8 %collective-permute-done.23 = bf16[256,1024]{1,0:T(8,128)(2,1)S(1)} collective-permute-done((bf16[256,1024]{1,0:T(8,128)(2,1)S(1)}, bf16[256,1024]{1,0:T(8,128)(2,1)S(1)}, u32[]{:S(2)}, u32[]{:S(2)}) %collective-permute-start.23) | collective-permute-done | bytes 524320 | tf_op jit(solution)/shard_map/ppermute | solution.py:586
  244.7 8.0 %norm_feed_forward.3 = (f32[512,1024]{1,0:T(8,128)}, bf16[512,1024]{1,0:T(8,128)(2,1)}, f32[512,1024]{1,0:T(8,128)}, bf16[512,512]{1,0:T(8,128)(2,1)}, bf16[256,...) custom-call(f32[512,1024]{1,0:T(8,128)} %get-tuple-element.76.refs_0_.refs_1_, f32[1,1024]{1,0:T(1,128)} %get-tuple-element.262.refs_1_.refs_2_, ...), custom_call_target="tpu_custom_call" | custom-call | flops 2000000000 | bytes 10000000 | tf_op jit(solution)/shard_map/norm_feed_forward/pallas_call | solution.py:566
  252.9 7.1 %feed_forward_back.2 = (bf16[512,1024]{1,0:T(8,128)(2,1)}, bf16[512,1024]{1,0:T(8,128)(2,1)}, bf16[256,1024]{1,0:T(8,128)(2,1)}, bf16[256,1024]{1,0:T(8,128)(2,1)}) custom-call(f32[512,1024]{1,0:T(8,128)} %get-tuple-element.83.refs_0_, bf16[512,1024]{1,0:T(8,128)(2,1)} %slice_dynamic-update-slice_fusion.refs_9_.refs_1_.refs_0_, bf16[1024,1536]{1,0:T(8,128)(2,1)} %bitcast.165), custom_call_target="tpu_custom_call" | custom-call | flops 2000000000 | bytes 10000000 | tf_op jit(solution)/shard_map/feed_forward_back/pallas_call | solution.py:566
  266.9 11.5 %collective-permute-done.30 = bf16[256,1024]{1,0:T(8,128)(2,1)S(1)} collective-permute-done((bf16[256,1024]{1,0:T(8,128)(2,1)S(1)}, bf16[256,1024]{1,0:T(8,128)(2,1)S(1)}, u32[]{:S(2)}, u32[]{:S(2)}) %collective-permute-start.30) | collective-permute-done | bytes 524320 | tf_op jit(solution)/shard_map/ppermute | solution.py:586
  281.4 23.1 %norm_mixer_back.2 = (f32[512,1024]{1,0:T(8,128)}, bf16[512,1024]{1,0:T(8,128)(2,1)}, f32[1,1024]{1,0:T(1,128)}, bf16[512,1408]{1,0:T(8,128)(2,1)}, f32[8,640]{1...) custom-call(bf16[512,1024]{1,0:T(8,128)(2,1)} %slice_dynamic-update-slice_fusion.refs_9_.refs_1_, ...), custom_call_target="tpu_custom_call" | custom-call | flops 5000000000 | bytes 10000000 | tf_op jit(solution)/shard_map/norm_mixer_back/pallas_call | solution.py:566
  316.3 11.1 %collective-permute-done.33 = bf16[256,1024]{1,0:T(8,128)(2,1)S(1)} collective-permute-done((bf16[256,1024]{1,0:T(8,128)(2,1)S(1)}, bf16[256,1024]{1,0:T(8,128)(2,1)S(1)}, u32[]{:S(2)}, u32[]{:S(2)}) %collective-permute-start.33) | collective-permute-done | bytes 524320 | tf_op jit(solution)/shard_map/ppermute | solution.py:586
  336.2 9.2 %feed_forward_back.3 = (bf16[512,1024]{1,0:T(8,128)(2,1)}, bf16[512,1024]{1,0:T(8,128)(2,1)}, bf16[256,1024]{1,0:T(8,128)(2,1)}, bf16[256,1024]{1,0:T(8,128)(2,1...) custom-call(f32[512,1024]{1,0:T(8,128)} %get-tuple-element.82.refs_0_, f32[512,1024]{1,0:T(8,128)} %get-tuple-element.76.refs_0_.refs_1_, ...), custom_call_target="tpu_custom_call" | custom-call | flops 2000000000 | bytes 10000000 | tf_op jit(solution)/shard_map/feed_forward_back/pallas_call | solution.py:566
  354.0 8.6 %collective-permute-done.26 = bf16[256,1024]{1,0:T(8,128)(2,1)} collective-permute-done((bf16[256,1024]{1,0:T(8,128)(2,1)S(1)}, bf16[256,1024]{1,0:T(8,128)(2,1)}, u32[]{:S(2)}, u32[]{:S(2)}) %collective-permute-start.26) | collective-permute-done | bytes 524320 | tf_op jit(solution)/shard_map/ppermute | solution.py:586
  364.8 8.3 %collective-permute-done.38 = bf16[256,1024]{1,0:T(8,128)(2,1)S(1)} collective-permute-done((bf16[256,1024]{1,0:T(8,128)(2,1)S(1)}, bf16[256,1024]{1,0:T(8,128)(2,1)S(1)}, u32[]{:S(2)}, u32[]{:S(2)}) %collective-permute-start.38) | collective-permute-done | bytes 524320 | tf_op jit(solution)/shard_map/ppermute | solution.py:586
  376.6 7.2 %collective-permute-done.40 = bf16[512,1408]{1,0:T(8,128)(2,1)S(1)} collective-permute-done((bf16[512,1408]{1,0:T(8,128)(2,1)S(1)}, bf16[512,1408]{1,0:T(8,128)(2,1)S(1)}, u32[]{:S(2)}, u32[]{:S(2)}) %collective-permute-start.40) | collective-permute-done | bytes 1441824 | tf_op jit(solution)/shard_map/ppermute | solution.py:586
  390.3 23.7 %norm_mixer_back.3 = (f32[512,1024]{1,0:T(8,128)}, bf16[512,1024]{1,0:T(8,128)(2,1)}, f32[1,1024]{1,0:T(1,128)}, bf16[512,1408]{1,0:T(8,128)(2,1)}, f32[8,640]{1...) custom-call(f32[512,1024]{1,0:T(8,128)} %get-tuple-element.98.refs_0_, ...), custom_call_target="tpu_custom_call" | custom-call | flops 5000000000 | bytes 10000000 | tf_op jit(solution)/shard_map/norm_mixer_back/pallas_call | solution.py:566
  426.3 4.0 collective-permute-start.42
  432.3 12.8 %collective-permute-done.42 = bf16[256,1024]{1,0:T(8,128)(2,1)S(1)} collective-permute-done((bf16[256,1024]{1,0:T(8,128)(2,1)S(1)}, bf16[256,1024]{1,0:T(8,128)(2,1)S(1)}, u32[]{:S(2)}, u32[]{:S(2)}) %collective-permute-start.42) | collective-permute-done | bytes 524320 | tf_op jit(solution)/shard_map/ppermute | solution.py:586
  446.1 18.5 %collective-permute-done.45.refs_1_ = bf16[512,1920]{1,0:T(8,128)(2,1)} collective-permute-done((bf16[512,1920]{1,0:T(8,128)(2,1)}, bf16[512,1920]{1,0:T(8,128)(2,1)}, u32[]{:S(2)}, u32[]{:S(2)}) %collective-permute-start.45) | collective-permute-done | bytes 1966112 | tf_op jit(solution)/shard_map/ppermute | solution.py:586
  464.7 3.9 sum_halves.2.refs_2_
  468.6 28.0 %collective-permute-done.50.refs_1_ = bf16[512,1536]{1,0:T(8,128)(2,1)} collective-permute-done((bf16[512,1536]{1,0:T(8,128)(2,1)}, bf16[512,1536]{1,0:T(8,128)(2,1)}, u32[]{:S(2)}, u32[]{:S(2)}) %collective-permute-start.50) | collective-permute-done | bytes 1572896 | tf_op jit(solution)/shard_map/ppermute | solution.py:586
  512.2 16.1 %collective-permute-done.51 = bf16[128,3456]{1,0:T(8,128)(2,1)} collective-permute-done((bf16[128,3456]{1,0:T(8,128)(2,1)S(1)}, bf16[128,3456]{1,0:T(8,128)(2,1)}, u32[]{:S(2)}, u32[]{:S(2)}) %collective-permute-start.51) | collective-permute-done | bytes 884768 | tf_op jit(solution)/shard_map/ppermute | solution.py:586
  532.3 8.6 %collective-permute-start.54 = (bf16[256,536]{1,0:T(8,128)(2,1)S(1)}, bf16[256,536]{1,0:T(8,128)(2,1)S(1)}, u32[]{:S(2)}, u32[]{:S(2)}) collective-permute-start(bf16[256,536]{1,0:T(8,128)(2,1)S(1)} %pad_maximum_fusion.23), channel_id=1, source_target_pairs={{0,4},{4,0},{8,12},{12,8},{1,5},{5,1},{9,13},{13,9},{2,6},{6,2},{1... | collective-permute-start | bytes 823304 | tf_op jit(solution)/shard_map/ppermute | solution.py:586
  543.8 8.8 %collective-permute-start.55 = (bf16[256,536]{1,0:T(8,128)(2,1)S(1)}, bf16[256,536]{1,0:T(8,128)(2,1)S(1)}, u32[]{:S(2)}, u32[]{:S(2)}) collective-permute-start(bf16[256,536]{1,0:T(8,128)(2,1)S(1)} %add_convert_fusion.19), channel_id=1, source_target_pairs={{0,8},{4,12},{8,0},{12,4},{1,9},{5,13},{9,1},{13,5},{2,10},{6,14},... | collective-permute-start | bytes 823304 | tf_op jit(solution)/shard_map/ppermute | solution.py:586
  554.7 6.2 collective-permute-done.55
  567.0 20.7 %reduce-scatter.10.cloned.1.call-done = bf16[128,1920]{1,0:T(8,128)(2,1)} async-done(((bf16[512,1920]{1,0:T(8,128)(2,1)}), bf16[128,1920]{1,0:T(8,128)(2,1)}) %reduce-scatter.10.cloned.1.call-update) | async-done | bytes 491536 | tf_op jit(solution)/shard_map/reduce_scatter | solution.py:731
  (589 shorter events, 241.9 us)
Async XLA Ops:
  7.2 147.1 %all-gather.4.cloned.1.call-start = ((), (), s32[]{:S(2)}) async-start(), calls=%async_computation.5 | async-start | bytes 2457600 | tf_op jit(solution)/shard_map/all_gather | solution.py:691
  10.1 49.6 %collective-permute-start = (bf16[512,256]{1,0:T(8,128)(2,1)}, bf16[512,256]{1,0:T(8,128)(2,1)}, u32[]{:S(2)}, u32[]{:S(2)}) collective-permute-start(bf16[512,256]{1,0:T(8,128)(2,1)} %maximum_select_fusion.11), channel_id=1, source_target_pairs={{0,0},{1,4},{2,8},{3,12},{4,1},{5,5},{6,9},{7,13},{8,2},{9,6},{10,... | collective-permute-start | bytes 786440 | tf_op jit(solution)/shard_map/ppermute | solution.py:648
  18.1 33.3 %collective-permute-start.3 = (bf16[128,896]{1,0:T(8,128)(2,1)S(1)}, bf16[128,896]{1,0:T(8,128)(2,1)}, u32[]{:S(2)}, u32[]{:S(2)}) collective-permute-start(bf16[128,896]{1,0:T(8,128)(2,1)S(1)} %get-tuple-element.253.refs_10_.refs_17_), channel_id=1, source_target_pairs={{0,2},{1,3},{2,0},{3,1},{4,6},{5,7},{6,4},{7,5},{8,10},{9,11},{10,... | collective-permute-start | bytes 688136 | tf_op jit(solution)/shard_map/ppermute | solution.py:586
  22.6 37.2 %collective-permute-start.7 = (bf16[512,256]{1,0:T(8,128)(2,1)}, bf16[512,256]{1,0:T(8,128)(2,1)}, u32[]{:S(2)}, u32[]{:S(2)}) collective-permute-start(bf16[512,256]{1,0:T(8,128)(2,1)} %maximum_select_fusion.12), channel_id=1, source_target_pairs={{0,0},{1,4},{2,8},{3,12},{4,1},{5,5},{6,9},{7,13},{8,2},{9,6},{10,... | collective-permute-start | bytes 786440 | tf_op jit(solution)/shard_map/ppermute | solution.py:648
  59.7 19.6 %collective-permute-start.10 = (bf16[256,896]{1,0:T(8,128)(2,1)}, bf16[256,896]{1,0:T(8,128)(2,1)}, u32[]{:S(2)}, u32[]{:S(2)}) collective-permute-start(bf16[256,896]{1,0:T(8,128)(2,1)} %pad_maximum_fusion.21), channel_id=1, source_target_pairs={{0,1},{1,0},{2,3},{3,2},{4,5},{5,4},{6,7},{7,6},{8,9},{9,8},{10,11... | collective-permute-start | bytes 1376264 | tf_op jit(solution)/shard_map/ppermute | solution.py:586
  65.9 19.1 %collective-permute-start.15 = (bf16[128,1536]{1,0:T(8,128)(2,1)}, bf16[128,1536]{1,0:T(8,128)(2,1)S(1)}, u32[]{:S(2)}, u32[]{:S(2)}) collective-permute-start(bf16[128,1536]{1,0:T(8,128)(2,1)} %get-tuple-element.234), channel_id=1, source_target_pairs={{0,2},{1,3},{2,0},{3,1},{4,6},{5,7},{6,4},{7,5},{8,10},{9,11},{10,... | collective-permute-start | bytes 1179656 | tf_op jit(solution)/shard_map/ppermute | solution.py:586
  67.3 25.8 %collective-permute-start.5 = (bf16[256,1024]{1,0:T(8,128)(2,1)}, bf16[256,1024]{1,0:T(8,128)(2,1)S(1)}, u32[]{:S(2)}, u32[]{:S(2)}) collective-permute-start(bf16[256,1024]{1,0:T(8,128)(2,1)} %pad_maximum_fusion.20), channel_id=1, source_target_pairs={{0,1},{1,0},{2,3},{3,2},{4,5},{5,4},{6,7},{7,6},{8,9},{9,8},{10,11... | collective-permute-start | bytes 1572872 | tf_op jit(solution)/shard_map/ppermute | solution.py:586
  71.6 23.4 %collective-permute-start.2 = (bf16[512,512]{1,0:T(8,128)(2,1)}, bf16[512,512]{1,0:T(8,128)(2,1)}, u32[]{:S(2)}, u32[]{:S(2)}) collective-permute-start(bf16[512,512]{1,0:T(8,128)(2,1)} %maximum_select_fusion.9), channel_id=1, source_target_pairs={{0,8},{4,12},{8,0},{12,4},{1,9},{5,13},{9,1},{13,5},{2,10},{6,14},... | collective-permute-start | bytes 1572872 | tf_op jit(solution)/shard_map/ppermute | solution.py:586
  75.2 23.1 %collective-permute-start.9 = (bf16[512,512]{1,0:T(8,128)(2,1)}, bf16[512,512]{1,0:T(8,128)(2,1)}, u32[]{:S(2)}, u32[]{:S(2)}) collective-permute-start(bf16[512,512]{1,0:T(8,128)(2,1)} %maximum_select_fusion.10), channel_id=1, source_target_pairs={{0,8},{4,12},{8,0},{12,4},{1,9},{5,13},{9,1},{13,5},{2,10},{6,14},... | collective-permute-start | bytes 1572872 | tf_op jit(solution)/shard_map/ppermute | solution.py:586
  81.3 34.5 %collective-permute-start.11 = (bf16[384,896]{1,0:T(8,128)(2,1)}, bf16[384,896]{1,0:T(8,128)(2,1)}, u32[]{:S(2)}, u32[]{:S(2)}) collective-permute-start(bf16[384,896]{1,0:T(8,128)(2,1)} %pad_maximum_fusion.18), channel_id=1, source_target_pairs={{0,16},{16,0},{1,17},{17,1},{2,18},{18,2},{3,19},{19,3},{4,20},{20... | collective-permute-start | bytes 2064392 | tf_op jit(solution)/shard_map/ppermute | solution.py:586
  86.1 22.9 %collective-permute-start.16 = (bf16[256,1536]{1,0:T(8,128)(2,1)}, bf16[256,1536]{1,0:T(8,128)(2,1)}, u32[]{:S(2)}, u32[]{:S(2)}) collective-permute-start(bf16[256,1536]{1,0:T(8,128)(2,1)} %pad_maximum_fusion.14), channel_id=1, source_target_pairs={{0,1},{1,0},{2,3},{3,2},{4,5},{5,4},{6,7},{7,6},{8,9},{9,8},{10,11... | collective-permute-start | bytes 2359304 | tf_op jit(solution)/shard_map/ppermute | solution.py:586
  94.0 19.8 %collective-permute-start.6 = (bf16[384,1024]{1,0:T(8,128)(2,1)}, bf16[384,1024]{1,0:T(8,128)(2,1)}, u32[]{:S(2)}, u32[]{:S(2)}) collective-permute-start(bf16[384,1024]{1,0:T(8,128)(2,1)} %pad_maximum_fusion.13), channel_id=1, source_target_pairs={{0,16},{16,0},{1,17},{17,1},{2,18},{18,2},{3,19},{19,3},{4,20},{20... | collective-permute-start | bytes 2359304 | tf_op jit(solution)/shard_map/ppermute | solution.py:586
  111.9 132.0 %all-gather.6.cloned.1.call-start = ((), (), s32[]{:S(2)}) async-start(), calls=%async_computation.11 | async-start | bytes 3932160 | tf_op jit(solution)/shard_map/all_gather | solution.py:704
  136.7 27.9 %collective-permute-start.17 = (bf16[384,1536]{1,0:T(8,128)(2,1)}, bf16[384,1536]{1,0:T(8,128)(2,1)S(1)}, u32[]{:S(2)}, u32[]{:S(2)}) collective-permute-start(bf16[384,1536]{1,0:T(8,128)(2,1)} %pad_maximum_fusion.8), channel_id=1, source_target_pairs={{0,16},{16,0},{1,17},{17,1},{2,18},{18,2},{3,19},{19,3},{4,20},{20... | collective-permute-start | bytes 3538952 | tf_op jit(solution)/shard_map/ppermute | solution.py:586
  157.3 233.1 %reduce-scatter.6.cloned.1.call-start = ((), (), s32[]{:S(2)}) async-start(), calls=%async_computation.6 | async-start | bytes 1966080 | tf_op jit(solution)/shard_map/reduce_scatter | solution.py:731
  174.1 34.7 %collective-permute-start.21 = (bf16[384,1920]{1,0:T(8,128)(2,1)S(1)}, bf16[384,1920]{1,0:T(8,128)(2,1)S(1)}, u32[]{:S(2)}, u32[]{:S(2)}) collective-permute-start(bf16[384,1920]{1,0:T(8,128)(2,1)S(1)} %pad_maximum_fusion.6), channel_id=1, source_target_pairs={{0,16},{16,0},{1,17},{17,1},{2,18},{18,2},{3,19},{19,3},{4,20},{20... | collective-permute-start | bytes 4423688 | tf_op jit(solution)/shard_map/ppermute | solution.py:586
  252.7 93.0 %collective-permute-start.25 = (bf16[256,1024]{1,0:T(8,128)(2,1)}, bf16[256,1024]{1,0:T(8,128)(2,1)S(1)}, u32[]{:S(2)}, u32[]{:S(2)}) collective-permute-start(bf16[256,1024]{1,0:T(8,128)(2,1)} %get-tuple-element.81), channel_id=1, source_target_pairs={{0,4},{4,0},{8,12},{12,8},{1,5},{5,1},{9,13},{13,9},{2,6},{6,2},{1... | collective-permute-start | bytes 1572872 | tf_op jit(solution)/shard_map/ppermute | solution.py:586
  265.6 49.0 %collective-permute-start.35 = (bf16[512,1536]{1,0:T(8,128)(2,1)S(1)}, bf16[512,1536]{1,0:T(8,128)(2,1)S(1)}, u32[]{:S(2)}, u32[]{:S(2)}) collective-permute-start(bf16[512,1536]{1,0:T(8,128)(2,1)S(1)} %pad_maximum_fusion.3.refs_14_), channel_id=1, source_target_pairs={{0,16},{16,0},{1,17},{17,1},{2,18},{18,2},{3,19},{19,3},{4,20},{20... | collective-permute-start | bytes 4718600 | tf_op jit(solution)/shard_map/ppermute | solution.py:586
  309.2 23.7 %collective-permute-start.36 = (bf16[512,512]{1,0:T(8,128)(2,1)}, bf16[512,512]{1,0:T(8,128)(2,1)}, u32[]{:S(2)}, u32[]{:S(2)}) collective-permute-start(bf16[512,512]{1,0:T(8,128)(2,1)} %convolution_convert_fusion.12), channel_id=1, source_target_pairs={{0,16},{16,0},{1,17},{17,1},{2,18},{18,2},{3,19},{19,3},{4,20},{20... | collective-permute-start | bytes 1572872 | tf_op jit(solution)/shard_map/ppermute | solution.py:586
  331.6 133.1 %reduce-scatter.8.cloned.1.call-start = ((), (), s32[]{:S(2)}) async-start(), calls=%async_computation.7 | async-start | bytes 1802240 | tf_op jit(solution)/shard_map/reduce_scatter | solution.py:731
  350.4 33.5 %collective-permute-start.40 = (bf16[512,1408]{1,0:T(8,128)(2,1)S(1)}, bf16[512,1408]{1,0:T(8,128)(2,1)S(1)}, u32[]{:S(2)}, u32[]{:S(2)}) collective-permute-start(bf16[512,1408]{1,0:T(8,128)(2,1)S(1)} %copy-done.26), channel_id=1, source_target_pairs={{0,16},{16,0},{1,17},{17,1},{2,18},{18,2},{3,19},{19,3},{4,20},{20... | collective-permute-start | bytes 4325384 | tf_op jit(solution)/shard_map/ppermute | solution.py:586
  353.1 20.0 %collective-permute-start.38 = (bf16[256,1024]{1,0:T(8,128)(2,1)S(1)}, bf16[256,1024]{1,0:T(8,128)(2,1)S(1)}, u32[]{:S(2)}, u32[]{:S(2)}) collective-permute-start(bf16[256,1024]{1,0:T(8,128)(2,1)S(1)} %add_convert_fusion.6), channel_id=1, source_target_pairs={{0,8},{4,12},{8,0},{12,4},{1,9},{5,13},{9,1},{13,5},{2,10},{6,14},... | collective-permute-start | bytes 1572872 | tf_op jit(solution)/shard_map/ppermute | solution.py:586
  363.9 56.3 %collective-permute-start.27 = (bf16[256,1024]{1,0:T(8,128)(2,1)S(1)}, bf16[256,1024]{1,0:T(8,128)(2,1)S(1)}, u32[]{:S(2)}, u32[]{:S(2)}) collective-permute-start(bf16[256,1024]{1,0:T(8,128)(2,1)S(1)} %add_convert_fusion.11), channel_id=1, source_target_pairs={{0,4},{4,0},{8,12},{12,8},{1,5},{5,1},{9,13},{13,9},{2,6},{6,2},{1... | collective-permute-start | bytes 1572872 | tf_op jit(solution)/shard_map/ppermute | solution.py:586
  385.5 119.5 %reduce-scatter.12.cloned.1.call-start = ((), (), s32[]{:S(2)}) async-start(), calls=%async_computation.9 | async-start | bytes 655360 | tf_op jit(solution)/shard_map/reduce_scatter | solution.py:731
  418.6 46.1 %collective-permute-start.45 = (bf16[512,1920]{1,0:T(8,128)(2,1)}, bf16[512,1920]{1,0:T(8,128)(2,1)}, u32[]{:S(2)}, u32[]{:S(2)}) collective-permute-start(bf16[512,1920]{1,0:T(8,128)(2,1)} %pad_maximum_fusion.1), channel_id=1, source_target_pairs={{0,16},{16,0},{1,17},{17,1},{2,18},{18,2},{3,19},{19,3},{4,20},{20... | collective-permute-start | bytes 5898248 | tf_op jit(solution)/shard_map/ppermute | solution.py:586
  421.0 75.7 %collective-permute-start.50 = (bf16[512,1536]{1,0:T(8,128)(2,1)}, bf16[512,1536]{1,0:T(8,128)(2,1)}, u32[]{:S(2)}, u32[]{:S(2)}) collective-permute-start(bf16[512,1536]{1,0:T(8,128)(2,1)} %pad_maximum_fusion.5.refs_14_), channel_id=1, source_target_pairs={{0,16},{16,0},{1,17},{17,1},{2,18},{18,2},{3,19},{19,3},{4,20},{20... | collective-permute-start | bytes 4718600 | tf_op jit(solution)/shard_map/ppermute | solution.py:586
  422.0 78.3 %collective-permute-start.28 = (bf16[512,256]{1,0:T(8,128)(2,1)S(1)}, bf16[512,256]{1,0:T(8,128)(2,1)}, u32[]{:S(2)}, u32[]{:S(2)}) collective-permute-start(bf16[512,256]{1,0:T(8,128)(2,1)S(1)} %maximum_select_fusion.13), channel_id=1, source_target_pairs={{0,0},{1,4},{2,8},{3,12},{4,1},{5,5},{6,9},{7,13},{8,2},{9,6},{10,... | collective-permute-start | bytes 786440 | tf_op jit(solution)/shard_map/ppermute | solution.py:648
  423.4 129.8 %reduce-scatter.14.cloned.1.call-start = ((), (), s32[]{:S(2)}) async-start(), calls=%async_computation.10 | async-start | bytes 1966080 | tf_op jit(solution)/shard_map/reduce_scatter | solution.py:731
  426.3 18.8 %collective-permute-start.42 = (bf16[256,1024]{1,0:T(8,128)(2,1)S(1)}, bf16[256,1024]{1,0:T(8,128)(2,1)S(1)}, u32[]{:S(2)}, u32[]{:S(2)}) collective-permute-start(bf16[256,1024]{1,0:T(8,128)(2,1)S(1)} %add_convert_fusion.4), channel_id=1, source_target_pairs={{0,8},{4,12},{8,0},{12,4},{1,9},{5,13},{9,1},{13,5},{2,10},{6,14},... | collective-permute-start | bytes 1572872 | tf_op jit(solution)/shard_map/ppermute | solution.py:586
  500.1 87.5 %reduce-scatter.10.cloned.1.call-start = ((), (), s32[]{:S(2)}) async-start(), calls=%async_computation.8 | async-start | bytes 2457600 | tf_op jit(solution)/shard_map/reduce_scatter | solution.py:731
  506.4 21.9 %collective-permute-start.51 = (bf16[128,3456]{1,0:T(8,128)(2,1)S(1)}, bf16[128,3456]{1,0:T(8,128)(2,1)}, u32[]{:S(2)}, u32[]{:S(2)}) collective-permute-start(bf16[128,3456]{1,0:T(8,128)(2,1)S(1)} %maximum_select_fusion.6), channel_id=1, source_target_pairs={{0,16},{16,0},{1,17},{17,1},{2,18},{18,2},{3,19},{19,3},{4,20},{20... | collective-permute-start | bytes 2654216 | tf_op jit(solution)/shard_map/ppermute | solution.py:586
  543.8 17.2 %collective-permute-start.55 = (bf16[256,536]{1,0:T(8,128)(2,1)S(1)}, bf16[256,536]{1,0:T(8,128)(2,1)S(1)}, u32[]{:S(2)}, u32[]{:S(2)}) collective-permute-start(bf16[256,536]{1,0:T(8,128)(2,1)S(1)} %add_convert_fusion.19), channel_id=1, source_target_pairs={{0,8},{4,12},{8,0},{12,4},{1,9},{5,13},{9,1},{13,5},{2,10},{6,14},... | collective-permute-start | bytes 823304 | tf_op jit(solution)/shard_map/ppermute | solution.py:586
  (142 other events, 1319.6 us)
Sparse Core Ops, SparseCore 0:
  112.1 42.2 all-gather.3
  157.4 62.3 all-gather.5
  331.7 34.1 reduce-scatter.5
  385.6 32.4 reduce-scatter.7
  423.5 24.0 reduce-scatter.11
  500.3 41.8 reduce-scatter.13
  544.4 43.1 reduce-scatter.9

commit v3 on v2

--- a/solution.py
+++ b/solution.py
@@ -941,8 +941,9 @@
             axis=1,
         )
         whole = dp_sum(mine, received, total[0], later_sum)
-        wide = dp_sum(wide_mine, wide_received, whole)
-        sums = (col_scatter(wide), col_scatter(whole), later_sum, wide)
+        whole_sum = col_scatter(whole)
+        wide = dp_sum(wide_mine, wide_received, whole_sum)
+        sums = (col_scatter(wide), whole_sum, later_sum, wide)
     above = (hidden, input_gain, dmiddle, *total)
     return above, waited, gain_above, post_gain_grad, dheads, dtaps, sums
 

time: 648 us -> 614 us (0.948)
  waiting for transfers between devices: 278 us -> 260 us
    ppermute x55, waiting for transfers between devices: 251 us -> 195 us  [swap(): return lax.ppermute(value, axis, [(i, i ^ distance) for i in range(size)])]
    reduce_scatter x5, waiting for transfers between devices: 20.7 us -> 57.8 us  [col_scatter(): lax.psum_scatter(value, 'col', scatter_dimension=0, tiled=True)]
    ppermute x55, starting transfers between devices: 59.6 us -> 47.8 us  [swap(): return lax.ppermute(value, axis, [(i, i ^ distance) for i in range(size)])]
    reduce_scatter x5, starting transfers between devices: 0.61 us -> 11.5 us  [col_scatter(): lax.psum_scatter(value, 'col', scatter_dimension=0, tiled=True)]
    unnamed x239 -> x223, local copies, waits for them, and re-layouts: 23.3 us -> 20.9 us
  transfers between devices with their start and end apart: 66 -> 66, of which waited for: 41 -> 34; matrix products, arithmetic and copies ran while one was open for 21% -> 20% of each run, Pallas kernels for 17% -> 16%
where the time goes in v3:
time: 614 us; the launch traced here: 609 us
  waiting for transfers between devices  260 us (42%)
  Pallas kernels  115 us (19%)
  starting transfers between devices  69 us (11%)
  other arithmetic  65.7 us (11%)
  local copies, waits for them, and re-layouts  52.5 us (9%)
  matrix products  24.2 us (4%)
  between operations  22.6 us (4%)
    ppermute x55, waiting for transfers between devices, swap(): return lax.ppermute(value, axis, [(i, i ^ distance) for i in range(size)])  195 us
    pallas_call x10, Pallas kernels, run_kernel(): pl.pallas_call(body, out_shape=out_shapes, in_specs=[vmem] * len(ins) + [...  115 us
    reduce_scatter x5, waiting for transfers between devices, col_scatter(): lax.psum_scatter(value, 'col', scatter_dimension=0, tiled=True)  57.8 us
    ppermute x55, starting transfers between devices, swap(): return lax.ppermute(value, axis, [(i, i ^ distance) for i in range(size)])  47.8 us
    dot_general x16, matrix products, dot(): lax.dot_general(left, right, dims, precision=precision, preferred_element...  24.2 us
    unnamed x223, local copies, waits for them, and re-layouts  20.9 us
    select_n x21, other arithmetic, in_order(): jnp.where(own_is_second == 0, jnp.concatenate([own, other], axis=axis), j...  14.7 us
    convert_element_type x20, other arithmetic, add(): return (left.astype(f32) + right.astype(f32)).astype(bf16)  12.3 us
  transfers between devices with their start and end apart: 66, of which 34 were waited for; matrix products, arithmetic and copies ran while one was open for 20% of the time, Pallas kernels for 16%

profile of v3, /device:TPU:0, one launch (start us, length us, event | category | flops | bytes accessed | tf_op | source)
XLA Modules:
  0.0 608.6 jit_solution(8476806171045081828)
XLA Ops:
  10.1 3.6 collective-permute-start
  18.1 3.7 collective-permute-start.3
  22.6 3.6 collective-permute-start.7
  34.4 16.9 %collective-permute-done.3.refs_11_.refs_18_ = bf16[128,896]{1,0:T(8,128)(2,1)} collective-permute-done((bf16[128,896]{1,0:T(8,128)(2,1)S(1)}, bf16[128,896]{1,0:T(8,128)(2,1)}, u32[]{:S(2)}, u32[]{:S(2)}) %collective-permute-start.3) | collective-permute-done | bytes 229408 | tf_op jit(solution)/shard_map/ppermute | solution.py:586
  86.9 6.2 %collective-permute-done.5.refs_17_.refs_24_ = bf16[256,1024]{1,0:T(8,128)(2,1)S(1)} collective-permute-done((bf16[256,1024]{1,0:T(8,128)(2,1)}, bf16[256,1024]{1,0:T(8,128)(2,1)S(1)}, u32[]{:S(2)}, u32[]{:S(2)}) %collective-permute-start.5) | collective-permute-done | bytes 524320 | tf_op jit(solution)/shard_map/ppermute | solution.py:586
  104.3 4.7 collective-permute-done.16.refs_6_.refs_12_
  115.7 14.1 %norm_mixer_out.2 = (f32[512,1024]{1,0:T(8,128)}, bf16[512,1024]{1,0:T(8,128)(2,1)}, f32[512,1408]{1,0:T(8,128)}, bf16[512,512]{1,0:T(8,128)(2,1)}, bf16[256,102...) custom-call(bf16[512,1024]{1,0:T(8,128)(2,1)} %copy-done.26, f32[1,1024]{1,0:T(1,128)} %get-tuple-element.265.refs_1_, ...), custom_call_target="tpu_custom_call" | custom-call | flops 10000000 | bytes 10000000 | tf_op jit(solution)/shard_map/norm_mixer_out/pallas_call | solution.py:566
  137.3 10.0 %collective-permute-done.13 = bf16[256,1024]{1,0:T(8,128)(2,1)S(1)} collective-permute-done((bf16[256,1024]{1,0:T(8,128)(2,1)S(1)}, bf16[256,1024]{1,0:T(8,128)(2,1)S(1)}, u32[]{:S(2)}, u32[]{:S(2)}) %collective-permute-start.13) | collective-permute-done | bytes 524320 | tf_op jit(solution)/shard_map/ppermute | solution.py:586
  147.6 6.7 %all-gather.4.cloned.1.call-done.refs_11_.refs_15_ = bf16[512,1920]{1,0:T(8,128)(2,1)} async-done(((bf16[128,1920]{1,0:T(8,128)(2,1)}), bf16[512,1920]{1,0:T(8,128)(2,1)}) %all-gather.4.cloned.1.call-update) | async-done | bytes 1966096 | tf_op jit(solution)/shard_map/all_gather | solution.py:691
  157.3 11.4 %reduce-scatter.6.cloned.1.call-start = ((), (), s32[]{:S(2)}) async-start(), calls=%async_computation.6 | async-start | bytes 1966080 | tf_op jit(solution)/shard_map/reduce_scatter | solution.py:731
  169.7 8.2 %norm_feed_forward.2 = (f32[512,1024]{1,0:T(8,128)}, bf16[512,1024]{1,0:T(8,128)(2,1)}, f32[512,1024]{1,0:T(8,128)}, bf16[512,512]{1,0:T(8,128)(2,1)}, bf16[256,...) custom-call(f32[512,1024]{1,0:T(8,128)} %get-tuple-element.70.refs_0_, f32[1,1024]{1,0:T(1,128)} %get-tuple-element.264.refs_1_.refs_2_, ...), custom_call_target="tpu_custom_call" | custom-call | flops 2000000000 | bytes 10000000 | tf_op jit(solution)/shard_map/norm_feed_forward/pallas_call | solution.py:566
  181.8 12.5 %collective-permute-done.19 = bf16[256,1024]{1,0:T(8,128)(2,1)S(1)} collective-permute-done((bf16[256,1024]{1,0:T(8,128)(2,1)S(1)}, bf16[256,1024]{1,0:T(8,128)(2,1)S(1)}, u32[]{:S(2)}, u32[]{:S(2)}) %collective-permute-start.19) | collective-permute-done | bytes 524320 | tf_op jit(solution)/shard_map/ppermute | solution.py:586
  196.6 16.4 %collective-permute-done.21.refs_13_.refs_17_ = bf16[384,1920]{1,0:T(8,128)(2,1)S(1)} collective-permute-done((bf16[384,1920]{1,0:T(8,128)(2,1)S(1)}, bf16[384,1920]{1,0:T(8,128)(2,1)S(1)}, u32[]{:S(2)}, u32[]{:S(2)}) %collective-permute-start.21) | collective-permute-done | bytes 1474592 | tf_op jit(solution)/shard_map/ppermute | solution.py:586
  214.2 14.2 %norm_mixer_out.3 = (f32[512,1024]{1,0:T(8,128)}, bf16[512,1024]{1,0:T(8,128)(2,1)}, f32[512,1408]{1,0:T(8,128)}, bf16[512,512]{1,0:T(8,128)(2,1)}, bf16[256,102...) custom-call(f32[512,1024]{1,0:T(8,128)} %get-tuple-element.73.refs_0_.refs_1_, f32[1,1024]{1,0:T(1,128)} %get-tuple-element.263.refs_1_.refs_2_, ...), custom_call_target="tpu_custom_call" | custom-call | flops 10000000 | bytes 10000000 | tf_op jit(solution)/shard_map/norm_mixer_out/pallas_call | solution.py:566
  233.3 12.5 %collective-permute-done.23 = bf16[256,1024]{1,0:T(8,128)(2,1)S(1)} collective-permute-done((bf16[256,1024]{1,0:T(8,128)(2,1)S(1)}, bf16[256,1024]{1,0:T(8,128)(2,1)S(1)}, u32[]{:S(2)}, u32[]{:S(2)}) %collective-permute-start.23) | collective-permute-done | bytes 524320 | tf_op jit(solution)/shard_map/ppermute | solution.py:586
  248.8 8.0 %norm_feed_forward.3 = (f32[512,1024]{1,0:T(8,128)}, bf16[512,1024]{1,0:T(8,128)(2,1)}, f32[512,1024]{1,0:T(8,128)}, bf16[512,512]{1,0:T(8,128)(2,1)}, bf16[256,...) custom-call(f32[512,1024]{1,0:T(8,128)} %get-tuple-element.76.refs_0_.refs_1_, f32[1,1024]{1,0:T(1,128)} %get-tuple-element.262.refs_1_.refs_2_, ...), custom_call_target="tpu_custom_call" | custom-call | flops 2000000000 | bytes 10000000 | tf_op jit(solution)/shard_map/norm_feed_forward/pallas_call | solution.py:566
  256.8 7.1 %feed_forward_back.2 = (bf16[512,1024]{1,0:T(8,128)(2,1)}, bf16[512,1024]{1,0:T(8,128)(2,1)}, bf16[256,1024]{1,0:T(8,128)(2,1)}, bf16[256,1024]{1,0:T(8,128)(2,1)}) custom-call(f32[512,1024]{1,0:T(8,128)} %get-tuple-element.83.refs_0_, bf16[512,1024]{1,0:T(8,128)(2,1)} %slice_dynamic-update-slice_fusion.refs_9_.refs_1_.refs_0_, bf16[1024,1536]{1,0:T(8,128)(2,1)} %bitcast.165), custom_call_target="tpu_custom_call" | custom-call | flops 2000000000 | bytes 10000000 | tf_op jit(solution)/shard_map/feed_forward_back/pallas_call | solution.py:566
  272.0 10.2 %collective-permute-done.30 = bf16[256,1024]{1,0:T(8,128)(2,1)S(1)} collective-permute-done((bf16[256,1024]{1,0:T(8,128)(2,1)S(1)}, bf16[256,1024]{1,0:T(8,128)(2,1)S(1)}, u32[]{:S(2)}, u32[]{:S(2)}) %collective-permute-start.30) | collective-permute-done | bytes 524320 | tf_op jit(solution)/shard_map/ppermute | solution.py:586
  285.2 22.9 %norm_mixer_back.2 = (f32[512,1024]{1,0:T(8,128)}, bf16[512,1024]{1,0:T(8,128)(2,1)}, f32[1,1024]{1,0:T(1,128)}, bf16[512,1408]{1,0:T(8,128)(2,1)}, f32[8,640]{1...) custom-call(bf16[512,1024]{1,0:T(8,128)(2,1)} %slice_dynamic-update-slice_fusion.refs_9_.refs_1_, ...), custom_call_target="tpu_custom_call" | custom-call | flops 5000000000 | bytes 10000000 | tf_op jit(solution)/shard_map/norm_mixer_back/pallas_call | solution.py:566
  318.0 3.7 convolution_convert_fusion.3.refs_6_
  322.2 6.5 %collective-permute-done.33 = bf16[256,1024]{1,0:T(8,128)(2,1)} collective-permute-done((bf16[256,1024]{1,0:T(8,128)(2,1)S(1)}, bf16[256,1024]{1,0:T(8,128)(2,1)}, u32[]{:S(2)}, u32[]{:S(2)}) %collective-permute-start.33) | collective-permute-done | bytes 524320 | tf_op jit(solution)/shard_map/ppermute | solution.py:586
  336.6 9.2 %feed_forward_back.3 = (bf16[512,1024]{1,0:T(8,128)(2,1)}, bf16[512,1024]{1,0:T(8,128)(2,1)}, bf16[256,1024]{1,0:T(8,128)(2,1)}, bf16[256,1024]{1,0:T(8,128)(2,1...) custom-call(f32[512,1024]{1,0:T(8,128)} %get-tuple-element.82.refs_0_, f32[512,1024]{1,0:T(8,128)} %get-tuple-element.76.refs_0_.refs_1_, ...), custom_call_target="tpu_custom_call" | custom-call | flops 2000000000 | bytes 10000000 | tf_op jit(solution)/shard_map/feed_forward_back/pallas_call | solution.py:566
  352.6 10.5 %collective-permute-done.38 = bf16[256,1024]{1,0:T(8,128)(2,1)S(1)} collective-permute-done((bf16[256,1024]{1,0:T(8,128)(2,1)S(1)}, bf16[256,1024]{1,0:T(8,128)(2,1)S(1)}, u32[]{:S(2)}, u32[]{:S(2)}) %collective-permute-start.38) | collective-permute-done | bytes 524320 | tf_op jit(solution)/shard_map/ppermute | solution.py:586
  368.3 23.9 %norm_mixer_back.3 = (f32[512,1024]{1,0:T(8,128)}, bf16[512,1024]{1,0:T(8,128)(2,1)}, f32[1,1024]{1,0:T(1,128)}, bf16[512,1408]{1,0:T(8,128)(2,1)}, f32[8,640]{1...) custom-call(f32[512,1024]{1,0:T(8,128)} %get-tuple-element.98.refs_0_, ...), custom_call_target="tpu_custom_call" | custom-call | flops 5000000000 | bytes 10000000 | tf_op jit(solution)/shard_map/norm_mixer_back/pallas_call | solution.py:566
  403.2 20.0 %collective-permute-done.42 = bf16[256,1024]{1,0:T(8,128)(2,1)S(1)} collective-permute-done((bf16[256,1024]{1,0:T(8,128)(2,1)S(1)}, bf16[256,1024]{1,0:T(8,128)(2,1)S(1)}, u32[]{:S(2)}, u32[]{:S(2)}) %collective-permute-start.42) | collective-permute-done | bytes 524320 | tf_op jit(solution)/shard_map/ppermute | solution.py:586
  424.1 17.4 %collective-permute-done.45.refs_1_ = bf16[512,1920]{1,0:T(8,128)(2,1)S(1)} collective-permute-done((bf16[512,1920]{1,0:T(8,128)(2,1)S(1)}, bf16[512,1920]{1,0:T(8,128)(2,1)S(1)}, u32[]{:S(2)}, u32[]{:S(2)}) %collective-permute-start.45) | collective-permute-done | bytes 1966112 | tf_op jit(solution)/shard_map/ppermute | solution.py:586
  442.9 3.9 sum_halves.2
  457.9 47.3 %reduce-scatter.10.cloned.1.call-done.refs_2_ = bf16[128,1920]{1,0:T(8,128)(2,1)} async-done(((bf16[512,1920]{1,0:T(8,128)(2,1)}), bf16[128,1920]{1,0:T(8,128)(2,1)}) %reduce-scatter.10.cloned.1.call-update) | async-done | bytes 491536 | tf_op jit(solution)/shard_map/reduce_scatter | solution.py:731
  507.2 4.6 collective-permute-start.46
  522.1 10.4 %reduce-scatter.12.cloned.1.call-done = bf16[128,512]{1,0:T(8,128)(2,1)} async-done(((bf16[512,512]{1,0:T(8,128)(2,1)}), bf16[128,512]{1,0:T(8,128)(2,1)}) %reduce-scatter.12.cloned.1.call-update) | async-done | bytes 131088 | tf_op jit(solution)/shard_map/reduce_scatter | solution.py:731
  541.3 22.6 %collective-permute-done.49 = bf16[128,1920]{1,0:T(8,128)(2,1)S(1)} collective-permute-done((bf16[128,1920]{1,0:T(8,128)(2,1)S(1)}, bf16[128,1920]{1,0:T(8,128)(2,1)S(1)}, u32[]{:S(2)}, u32[]{:S(2)}) %collective-permute-start.49) | collective-permute-done | bytes 491552 | tf_op jit(solution)/shard_map/ppermute | solution.py:586
  585.1 4.2 collective-permute-done.55
  (573 shorter events, 208.9 us)
Async XLA Ops:
  7.2 147.1 %all-gather.4.cloned.1.call-start = ((), (), s32[]{:S(2)}) async-start(), calls=%async_computation.5 | async-start | bytes 2457600 | tf_op jit(solution)/shard_map/all_gather | solution.py:691
  10.1 49.6 %collective-permute-start = (bf16[512,256]{1,0:T(8,128)(2,1)}, bf16[512,256]{1,0:T(8,128)(2,1)}, u32[]{:S(2)}, u32[]{:S(2)}) collective-permute-start(bf16[512,256]{1,0:T(8,128)(2,1)} %maximum_select_fusion.11), channel_id=1, source_target_pairs={{0,0},{1,4},{2,8},{3,12},{4,1},{5,5},{6,9},{7,13},{8,2},{9,6},{10,... | collective-permute-start | bytes 786440 | tf_op jit(solution)/shard_map/ppermute | solution.py:648
  18.1 33.2 %collective-permute-start.3 = (bf16[128,896]{1,0:T(8,128)(2,1)S(1)}, bf16[128,896]{1,0:T(8,128)(2,1)}, u32[]{:S(2)}, u32[]{:S(2)}) collective-permute-start(bf16[128,896]{1,0:T(8,128)(2,1)S(1)} %get-tuple-element.253.refs_10_.refs_17_), channel_id=1, source_target_pairs={{0,2},{1,3},{2,0},{3,1},{4,6},{5,7},{6,4},{7,5},{8,10},{9,11},{10,... | collective-permute-start | bytes 688136 | tf_op jit(solution)/shard_map/ppermute | solution.py:586
  22.6 37.2 %collective-permute-start.7 = (bf16[512,256]{1,0:T(8,128)(2,1)}, bf16[512,256]{1,0:T(8,128)(2,1)}, u32[]{:S(2)}, u32[]{:S(2)}) collective-permute-start(bf16[512,256]{1,0:T(8,128)(2,1)} %maximum_select_fusion.12), channel_id=1, source_target_pairs={{0,0},{1,4},{2,8},{3,12},{4,1},{5,5},{6,9},{7,13},{8,2},{9,6},{10,... | collective-permute-start | bytes 786440 | tf_op jit(solution)/shard_map/ppermute | solution.py:648
  59.7 19.6 %collective-permute-start.10 = (bf16[256,896]{1,0:T(8,128)(2,1)}, bf16[256,896]{1,0:T(8,128)(2,1)}, u32[]{:S(2)}, u32[]{:S(2)}) collective-permute-start(bf16[256,896]{1,0:T(8,128)(2,1)} %pad_maximum_fusion.21), channel_id=1, source_target_pairs={{0,1},{1,0},{2,3},{3,2},{4,5},{5,4},{6,7},{7,6},{8,9},{9,8},{10,11... | collective-permute-start | bytes 1376264 | tf_op jit(solution)/shard_map/ppermute | solution.py:586
  67.3 25.8 %collective-permute-start.5 = (bf16[256,1024]{1,0:T(8,128)(2,1)}, bf16[256,1024]{1,0:T(8,128)(2,1)S(1)}, u32[]{:S(2)}, u32[]{:S(2)}) collective-permute-start(bf16[256,1024]{1,0:T(8,128)(2,1)} %pad_maximum_fusion.20), channel_id=1, source_target_pairs={{0,1},{1,0},{2,3},{3,2},{4,5},{5,4},{6,7},{7,6},{8,9},{9,8},{10,11... | collective-permute-start | bytes 1572872 | tf_op jit(solution)/shard_map/ppermute | solution.py:586
  71.6 23.3 %collective-permute-start.2 = (bf16[512,512]{1,0:T(8,128)(2,1)}, bf16[512,512]{1,0:T(8,128)(2,1)}, u32[]{:S(2)}, u32[]{:S(2)}) collective-permute-start(bf16[512,512]{1,0:T(8,128)(2,1)} %maximum_select_fusion.9), channel_id=1, source_target_pairs={{0,8},{4,12},{8,0},{12,4},{1,9},{5,13},{9,1},{13,5},{2,10},{6,14},... | collective-permute-start | bytes 1572872 | tf_op jit(solution)/shard_map/ppermute | solution.py:586
  75.2 23.1 %collective-permute-start.9 = (bf16[512,512]{1,0:T(8,128)(2,1)}, bf16[512,512]{1,0:T(8,128)(2,1)}, u32[]{:S(2)}, u32[]{:S(2)}) collective-permute-start(bf16[512,512]{1,0:T(8,128)(2,1)} %maximum_select_fusion.10), channel_id=1, source_target_pairs={{0,8},{4,12},{8,0},{12,4},{1,9},{5,13},{9,1},{13,5},{2,10},{6,14},... | collective-permute-start | bytes 1572872 | tf_op jit(solution)/shard_map/ppermute | solution.py:586
  81.3 34.5 %collective-permute-start.11 = (bf16[384,896]{1,0:T(8,128)(2,1)}, bf16[384,896]{1,0:T(8,128)(2,1)}, u32[]{:S(2)}, u32[]{:S(2)}) collective-permute-start(bf16[384,896]{1,0:T(8,128)(2,1)} %pad_maximum_fusion.18), channel_id=1, source_target_pairs={{0,16},{16,0},{1,17},{17,1},{2,18},{18,2},{3,19},{19,3},{4,20},{20... | collective-permute-start | bytes 2064392 | tf_op jit(solution)/shard_map/ppermute | solution.py:586
  86.0 22.9 %collective-permute-start.16 = (bf16[256,1536]{1,0:T(8,128)(2,1)}, bf16[256,1536]{1,0:T(8,128)(2,1)}, u32[]{:S(2)}, u32[]{:S(2)}) collective-permute-start(bf16[256,1536]{1,0:T(8,128)(2,1)} %pad_maximum_fusion.14), channel_id=1, source_target_pairs={{0,1},{1,0},{2,3},{3,2},{4,5},{5,4},{6,7},{7,6},{8,9},{9,8},{10,11... | collective-permute-start | bytes 2359304 | tf_op jit(solution)/shard_map/ppermute | solution.py:586
  94.1 19.8 %collective-permute-start.6 = (bf16[384,1024]{1,0:T(8,128)(2,1)}, bf16[384,1024]{1,0:T(8,128)(2,1)}, u32[]{:S(2)}, u32[]{:S(2)}) collective-permute-start(bf16[384,1024]{1,0:T(8,128)(2,1)} %pad_maximum_fusion.13), channel_id=1, source_target_pairs={{0,16},{16,0},{1,17},{17,1},{2,18},{18,2},{3,19},{19,3},{4,20},{20... | collective-permute-start | bytes 2359304 | tf_op jit(solution)/shard_map/ppermute | solution.py:586
  111.9 136.1 %all-gather.6.cloned.1.call-start = ((), (), s32[]{:S(2)}) async-start(), calls=%async_computation.11 | async-start | bytes 3932160 | tf_op jit(solution)/shard_map/all_gather | solution.py:704
  136.8 31.9 %collective-permute-start.17 = (bf16[384,1536]{1,0:T(8,128)(2,1)}, bf16[384,1536]{1,0:T(8,128)(2,1)S(1)}, u32[]{:S(2)}, u32[]{:S(2)}) collective-permute-start(bf16[384,1536]{1,0:T(8,128)(2,1)} %pad_maximum_fusion.8), channel_id=1, source_target_pairs={{0,16},{16,0},{1,17},{17,1},{2,18},{18,2},{3,19},{19,3},{4,20},{20... | collective-permute-start | bytes 3538952 | tf_op jit(solution)/shard_map/ppermute | solution.py:586
  147.5 21.2 %collective-permute-start.14 = (bf16[256,1024]{1,0:T(8,128)(2,1)S(1)}, bf16[256,1024]{1,0:T(8,128)(2,1)}, u32[]{:S(2)}, u32[]{:S(2)}) collective-permute-start(bf16[256,1024]{1,0:T(8,128)(2,1)S(1)} %add_convert_fusion.17.refs_2_), channel_id=1, source_target_pairs={{0,4},{4,0},{8,12},{12,8},{1,5},{5,1},{9,13},{13,9},{2,6},{6,2},{1... | collective-permute-start | bytes 1572872 | tf_op jit(solution)/shard_map/ppermute | solution.py:586
  157.3 211.0 %reduce-scatter.6.cloned.1.call-start = ((), (), s32[]{:S(2)}) async-start(), calls=%async_computation.6 | async-start | bytes 1966080 | tf_op jit(solution)/shard_map/reduce_scatter | solution.py:731
  178.3 34.7 %collective-permute-start.21 = (bf16[384,1920]{1,0:T(8,128)(2,1)S(1)}, bf16[384,1920]{1,0:T(8,128)(2,1)S(1)}, u32[]{:S(2)}, u32[]{:S(2)}) collective-permute-start(bf16[384,1920]{1,0:T(8,128)(2,1)S(1)} %pad_maximum_fusion.6), channel_id=1, source_target_pairs={{0,16},{16,0},{1,17},{17,1},{2,18},{18,2},{3,19},{19,3},{4,20},{20... | collective-permute-start | bytes 4423688 | tf_op jit(solution)/shard_map/ppermute | solution.py:586
  269.7 46.5 %collective-permute-start.35 = (bf16[512,1536]{1,0:T(8,128)(2,1)S(1)}, bf16[512,1536]{1,0:T(8,128)(2,1)S(1)}, u32[]{:S(2)}, u32[]{:S(2)}) collective-permute-start(bf16[512,1536]{1,0:T(8,128)(2,1)S(1)} %pad_maximum_fusion.3.refs_14_), channel_id=1, source_target_pairs={{0,16},{16,0},{1,17},{17,1},{2,18},{18,2},{3,19},{19,3},{4,20},{20... | collective-permute-start | bytes 4718600 | tf_op jit(solution)/shard_map/ppermute | solution.py:586
  308.5 89.1 %collective-permute-start.25 = (bf16[256,1024]{1,0:T(8,128)(2,1)}, bf16[256,1024]{1,0:T(8,128)(2,1)S(1)}, u32[]{:S(2)}, u32[]{:S(2)}) collective-permute-start(bf16[256,1024]{1,0:T(8,128)(2,1)} %get-tuple-element.81), channel_id=1, source_target_pairs={{0,4},{4,0},{8,12},{12,8},{1,5},{5,1},{9,13},{13,9},{2,6},{6,2},{1... | collective-permute-start | bytes 1572872 | tf_op jit(solution)/shard_map/ppermute | solution.py:586
  312.9 20.5 %collective-permute-start.36 = (bf16[512,512]{1,0:T(8,128)(2,1)}, bf16[512,512]{1,0:T(8,128)(2,1)}, u32[]{:S(2)}, u32[]{:S(2)}) collective-permute-start(bf16[512,512]{1,0:T(8,128)(2,1)} %convolution_convert_fusion.12), channel_id=1, source_target_pairs={{0,16},{16,0},{1,17},{17,1},{2,18},{18,2},{3,19},{19,3},{4,20},{20... | collective-permute-start | bytes 1572872 | tf_op jit(solution)/shard_map/ppermute | solution.py:586
  317.9 123.7 %reduce-scatter.8.cloned.1.call-start = ((), (), s32[]{:S(2)}) async-start(), calls=%async_computation.7 | async-start | bytes 1802240 | tf_op jit(solution)/shard_map/reduce_scatter | solution.py:731
  321.6 45.0 %collective-permute-start.40 = (bf16[512,1408]{1,0:T(8,128)(2,1)}, bf16[512,1408]{1,0:T(8,128)(2,1)S(1)}, u32[]{:S(2)}, u32[]{:S(2)}) collective-permute-start(bf16[512,1408]{1,0:T(8,128)(2,1)} %convolution_convert_fusion.3.refs_6_), channel_id=1, source_target_pairs={{0,16},{16,0},{1,17},{17,1},{2,18},{18,2},{3,19},{19,3},{4,20},{20... | collective-permute-start | bytes 4325384 | tf_op jit(solution)/shard_map/ppermute | solution.py:586
  368.2 137.0 %reduce-scatter.10.cloned.1.call-start = ((), (), s32[]{:S(2)}) async-start(), calls=%async_computation.8 | async-start | bytes 2457600 | tf_op jit(solution)/shard_map/reduce_scatter | solution.py:731
  396.4 45.1 %collective-permute-start.45 = (bf16[512,1920]{1,0:T(8,128)(2,1)S(1)}, bf16[512,1920]{1,0:T(8,128)(2,1)S(1)}, u32[]{:S(2)}, u32[]{:S(2)}) collective-permute-start(bf16[512,1920]{1,0:T(8,128)(2,1)S(1)} %pad_maximum_fusion.1), channel_id=1, source_target_pairs={{0,16},{16,0},{1,17},{17,1},{2,18},{18,2},{3,19},{19,3},{4,20},{20... | collective-permute-start | bytes 5898248 | tf_op jit(solution)/shard_map/ppermute | solution.py:586
  397.9 49.1 %collective-permute-start.26 = (bf16[256,1024]{1,0:T(8,128)(2,1)S(1)}, bf16[256,1024]{1,0:T(8,128)(2,1)}, u32[]{:S(2)}, u32[]{:S(2)}) collective-permute-start(bf16[256,1024]{1,0:T(8,128)(2,1)S(1)} %add_convert_fusion.12), channel_id=1, source_target_pairs={{0,8},{4,12},{8,0},{12,4},{1,9},{5,13},{9,1},{13,5},{2,10},{6,14},... | collective-permute-start | bytes 1572872 | tf_op jit(solution)/shard_map/ppermute | solution.py:586
  400.7 22.4 %collective-permute-start.42 = (bf16[256,1024]{1,0:T(8,128)(2,1)S(1)}, bf16[256,1024]{1,0:T(8,128)(2,1)S(1)}, u32[]{:S(2)}, u32[]{:S(2)}) collective-permute-start(bf16[256,1024]{1,0:T(8,128)(2,1)S(1)} %add_convert_fusion.4), channel_id=1, source_target_pairs={{0,8},{4,12},{8,0},{12,4},{1,9},{5,13},{9,1},{13,5},{2,10},{6,14},... | collective-permute-start | bytes 1572872 | tf_op jit(solution)/shard_map/ppermute | solution.py:586
  446.9 85.7 %reduce-scatter.12.cloned.1.call-start = ((), (), s32[]{:S(2)}) async-start(), calls=%async_computation.9 | async-start | bytes 655360 | tf_op jit(solution)/shard_map/reduce_scatter | solution.py:731
  451.2 60.6 %collective-permute-start.28 = (bf16[512,256]{1,0:T(8,128)(2,1)S(1)}, bf16[512,256]{1,0:T(8,128)(2,1)}, u32[]{:S(2)}, u32[]{:S(2)}) collective-permute-start(bf16[512,256]{1,0:T(8,128)(2,1)S(1)} %maximum_select_fusion.13), channel_id=1, source_target_pairs={{0,0},{1,4},{2,8},{3,12},{4,1},{5,5},{6,9},{7,13},{8,2},{9,6},{10,... | collective-permute-start | bytes 786440 | tf_op jit(solution)/shard_map/ppermute | solution.py:648
  452.6 62.4 %collective-permute-start.50 = (bf16[512,1536]{1,0:T(8,128)(2,1)}, bf16[512,1536]{1,0:T(8,128)(2,1)}, u32[]{:S(2)}, u32[]{:S(2)}) collective-permute-start(bf16[512,1536]{1,0:T(8,128)(2,1)} %pad_maximum_fusion.5.refs_14_), channel_id=1, source_target_pairs={{0,16},{16,0},{1,17},{17,1},{2,18},{18,2},{3,19},{19,3},{4,20},{20... | collective-permute-start | bytes 4718600 | tf_op jit(solution)/shard_map/ppermute | solution.py:586
  457.1 54.7 %collective-permute-start.44 = (bf16[512,256]{1,0:T(8,128)(2,1)S(1)}, bf16[512,256]{1,0:T(8,128)(2,1)S(1)}, u32[]{:S(2)}, u32[]{:S(2)}) collective-permute-start(bf16[512,256]{1,0:T(8,128)(2,1)S(1)} %maximum_select_fusion.14), channel_id=1, source_target_pairs={{0,0},{1,4},{2,8},{3,12},{4,1},{5,5},{6,9},{7,13},{8,2},{9,6},{10,... | collective-permute-start | bytes 786440 | tf_op jit(solution)/shard_map/ppermute | solution.py:648
  511.8 71.8 %reduce-scatter.14.cloned.1.call-start = ((), (), s32[]{:S(2)}) async-start(), calls=%async_computation.10 | async-start | bytes 1966080 | tf_op jit(solution)/shard_map/reduce_scatter | solution.py:731
  533.6 37.1 %collective-permute-start.51 = (bf16[128,3456]{1,0:T(8,128)(2,1)S(1)}, bf16[128,3456]{1,0:T(8,128)(2,1)}, u32[]{:S(2)}, u32[]{:S(2)}) collective-permute-start(bf16[128,3456]{1,0:T(8,128)(2,1)S(1)} %maximum_select_fusion.6), channel_id=1, source_target_pairs={{0,16},{16,0},{1,17},{17,1},{2,18},{18,2},{3,19},{19,3},{4,20},{20... | collective-permute-start | bytes 2654216 | tf_op jit(solution)/shard_map/ppermute | solution.py:586
  535.1 28.8 %collective-permute-start.49 = (bf16[128,1920]{1,0:T(8,128)(2,1)S(1)}, bf16[128,1920]{1,0:T(8,128)(2,1)S(1)}, u32[]{:S(2)}, u32[]{:S(2)}) collective-permute-start(bf16[128,1920]{1,0:T(8,128)(2,1)S(1)} %copy-done.22), channel_id=1, source_target_pairs={{0,16},{16,0},{1,17},{17,1},{2,18},{18,2},{3,19},{19,3},{4,20},{20... | collective-permute-start | bytes 1474568 | tf_op jit(solution)/shard_map/ppermute | solution.py:586
  (134 other events, 1042.1 us)
Sparse Core Ops, SparseCore 0:
  112.1 42.2 all-gather.3
  157.4 62.3 all-gather.5
  318.0 32.4 reduce-scatter.5
  368.3 31.2 reduce-scatter.7
  447.0 58.1 reduce-scatter.9
  511.9 20.6 reduce-scatter.11
  534.9 33.4 reduce-scatter.13
